TPU v7x, 128 devices: a whole 4x4x4 slice. The times are simulated.
128 devices in a mesh: inst: 4 (over z_hi, core), cuts: 32 (over y, x, z_lo).
Axes of the slice: x: 4, y: 4, z: 4 (z_hi: 2, z_lo: 2; z = z_hi * 2 + z_lo), core: 2. Of those that a mesh axis runs over, the one named last changes fastest.
Arguments:
- hidden: bfloat16 [4096, 4096], P(('inst', 'cuts')), may hold values from -6 to 6
- cache_kv: bfloat16 [4096, 128, 1024], P(('inst', 'cuts')), may hold values from -96 to 96
- cache_len: int32 [4096], P(('inst', 'cuts')), may hold values from 1 to 127, as said below
- mig_source: int32 [4096], P(('inst', 'cuts')), may hold values from 0 to 4095, as said below
- expert_ids: int32 [4096, 8], P(('inst', 'cuts')), may hold values from 0 to 127, all different within a row; in each aligned block of 32 rows (0 to 31, 32 to 63, ...) at most 4 rows name the same one
- gate_w: bfloat16 [4096, 8], P(('inst', 'cuts')), may hold values from 0.5 to 2
- attn_gain: bfloat16 [4096], replicated, may hold values from 0.5 to 1.5
- w_query: bfloat16 [4096, 8192], P(None, 'cuts'), may hold values from -0.09375 to 0.09375
- w_keyval: bfloat16 [4096, 1024], P(None, 'cuts'), may hold values from -0.09375 to 0.09375
- q_gain: float32 [128], replicated, may hold values from 0.5 to 8
- k_gain: float32 [128], replicated, may hold values from 0.25 to 1.75
- w_out: bfloat16 [8192, 4096], P('cuts'), may hold values from -0.25 to 0.25
- moe_gain: bfloat16 [4096], replicated, may hold values from 0.099609375 to 1.8984375
- w_gate: bfloat16 [4096, 12288], P(None, 'cuts'), may hold values from -0.09375 to 0.09375
- w_up: bfloat16 [4096, 12288], P(None, 'cuts'), may hold values from -0.09375 to 0.09375
- w_down: bfloat16 [12288, 4096], P('cuts'), may hold values from -0.21875 to 0.21875
Outputs:
- hidden_next: bfloat16 [4096, 4096], P(('inst', 'cuts'))
- cache_next: bfloat16 [4096, 128, 1024], P(('inst', 'cuts'))
Inputs may be any that keep to these rules, and one draw needn't show every extreme that they name: `mig_source`: each row is named once. Entry r names either r itself or the row in the same local slot of the device with the same cuts index in another group; each device hands exactly 2 rows to each other group. `cache_len`: rows that come from another group have at least 64 positions.
All inputs are finite; a program needn't handle non-finite values.
Results may differ from a plain program's by a relative error of at most 0.03.
Values may be sent and summed in bfloat16 or wider, within the bound.
No kernel may reach another device: no remote copies, remote signals or barrier semaphores. Data moves between devices by JAX's collectives and lax.ppermute only.
A program may use at most 192 MiB of HBM per device.

v0:
```python
import jax
import jax.numpy as jnp
from jax import lax
from jax.sharding import PartitionSpec as P

HD = 128
MIG = 2
MOST = 4


EPSILON = 1e-06
ROPE_BASE = 1000000.0


def norm_rows(values, gain_vec):
    mean_square = jnp.mean(values * values, axis=-1, keepdims=True)
    return values * lax.rsqrt(mean_square + EPSILON) * gain_vec


def rotate(values, position):
    half_width = values.shape[-1] // 2
    frequency = ROPE_BASE ** (-2.0 * jnp.arange(half_width, dtype=jnp.float32) / values.shape[-1])
    angles = position.astype(jnp.float32)[:, None] * frequency[None, :]
    cosine = jnp.concatenate([jnp.cos(angles), jnp.cos(angles)], axis=-1)[:, None, :]
    sine_part = jnp.concatenate([jnp.sin(angles), jnp.sin(angles)], axis=-1)[:, None, :]
    turned = jnp.concatenate([-values[..., half_width:], values[..., :half_width]], axis=-1)
    return values * cosine + turned * sine_part


def attend(q_raw, kv_raw, cache_rows, lengths, q_gain, k_gain):
    row_count = q_raw.shape[0]
    head_count = q_raw.shape[1] // HD
    kv_count = kv_raw.shape[1] // (2 * HD)
    group_size = head_count // kv_count
    length_cap = cache_rows.shape[1]
    queries = norm_rows(q_raw.astype(jnp.float32).reshape(row_count, head_count, HD), q_gain)
    queries = (
        rotate(queries, lengths).astype(jnp.bfloat16).reshape(row_count, kv_count, group_size, HD)
    )
    key_raw = kv_raw[:, : kv_count * HD].astype(jnp.float32).reshape(row_count, kv_count, HD)
    key_new = rotate(norm_rows(key_raw, k_gain), lengths).astype(jnp.bfloat16)
    value_new = kv_raw[:, kv_count * HD :].reshape(row_count, kv_count, HD)
    key_cache = cache_rows[:, :, : kv_count * HD].reshape(row_count, length_cap, kv_count, HD)
    value_cache = cache_rows[:, :, kv_count * HD :].reshape(row_count, length_cap, kv_count, HD)
    score_scale = HD ** (-0.5)
    scores = (
        jnp.einsum("rkgd,rpkd->rkgp", queries, key_cache, preferred_element_type=jnp.float32)
        * score_scale
    )
    positions = jnp.arange(length_cap, dtype=jnp.int32)
    usable = positions[None, :] < lengths[:, None]
    scores = jnp.where(usable[:, None, None, :], scores, -jnp.inf)
    self_score = (
        jnp.einsum("rkgd,rkd->rkg", queries, key_new, preferred_element_type=jnp.float32)
        * score_scale
    )
    peak = jnp.maximum(jnp.max(scores, axis=-1), self_score)
    weights = jnp.exp(scores - peak[..., None])
    self_weight = jnp.exp(self_score - peak)
    denominator = jnp.sum(weights, axis=-1) + self_weight
    probs = (weights / denominator[..., None]).astype(jnp.bfloat16)
    self_prob = (self_weight / denominator).astype(jnp.bfloat16)
    summed = jnp.einsum("rkgp,rpkd->rkgd", probs, value_cache, preferred_element_type=jnp.float32)
    summed = (
        summed
        + self_prob.astype(jnp.float32)[..., None] * value_new.astype(jnp.float32)[:, :, None, :]
    )
    attention = summed.reshape(row_count, head_count * HD).astype(jnp.bfloat16)
    new_entry = jnp.concatenate(
        [key_new.reshape(row_count, -1), value_new.reshape(row_count, -1)], axis=-1
    )
    at_length = (positions[None, :] == lengths[:, None])[:, :, None]
    cache_next = jnp.where(at_length, new_entry[:, None, :], cache_rows)
    return (attention, cache_next)


def pick_slots(flags, slot_ids):
    rank = jnp.cumsum(flags.astype(jnp.int32), axis=1) - 1
    slot_range = jnp.arange(MOST, dtype=jnp.int32)
    match = flags[:, None, :] & (rank[:, None, :] == slot_range[None, :, None])
    pick = jnp.sum(jnp.where(match, slot_ids[None, None, :], 0), axis=2)
    live = jnp.any(match, axis=2)
    return (pick, live)


def body(
    hidden,
    cache_kv,
    cache_len,
    mig_source,
    expert_ids,
    gate_w,
    attn_gain,
    w_query,
    w_keyval,
    q_gain,
    k_gain,
    w_out,
    moe_gain,
    w_gate,
    w_up,
    w_down,
):
    group_count = lax.axis_size("inst")
    cut_count = lax.axis_size("cuts")
    local_rows = hidden.shape[0]
    group_total = local_rows * cut_count
    group_id = lax.axis_index("inst")
    cut_id = lax.axis_index("cuts")
    slot_ids = jnp.arange(local_rows, dtype=jnp.int32)
    own_rows = (group_id * cut_count + cut_id) * local_rows + slot_ids
    all_plans = lax.all_gather(mig_source, "inst", axis=0, tiled=True).reshape(
        group_count, local_rows
    )
    targets = jnp.arange(group_count, dtype=jnp.int32)
    leaving = (all_plans == own_rows[None, :]) & (targets[:, None] != group_id)
    leave_rank = jnp.cumsum(leaving.astype(jnp.int32), axis=1) - 1
    chosen = leaving[:, None, :] & (
        leave_rank[:, None, :] == jnp.arange(MIG, dtype=jnp.int32)[None, :, None]
    )
    send_slot = jnp.sum(jnp.where(chosen, slot_ids[None, None, :], 0), axis=2)
    source_group = mig_source // group_total
    arriving = source_group != group_id
    from_group = (source_group[None, :] == targets[:, None]) & arriving[None, :]
    arrival_rank = jnp.sum(
        jnp.where(from_group, jnp.cumsum(from_group.astype(jnp.int32), axis=1) - 1, 0), axis=0
    )
    source_pick = jnp.where(arriving, source_group, 0)

    def settle(received, current):
        landed = received[source_pick, arrival_rank]
        row_mask = arriving.reshape((local_rows,) + (1,) * (current.ndim - 1))
        return jnp.where(row_mask, landed, current)

    got_states, got_cache = (
        lax.all_to_all(hidden[send_slot], "inst", split_axis=0, concat_axis=0, tiled=True),
        lax.all_to_all(cache_kv[send_slot], "inst", split_axis=0, concat_axis=0, tiled=True),
    )
    migrated = settle(got_states, hidden)
    cache_rows = settle(got_cache, cache_kv)
    expert_range = jnp.arange(cut_count // 2, dtype=jnp.int32)
    combine = jnp.sum(
        jnp.where(
            expert_ids[:, :, None] == expert_range[None, None, :],
            gate_w.astype(jnp.float32)[:, :, None],
            jnp.zeros((), jnp.float32),
        ),
        axis=1,
    )
    whole_rows, whole_combine = (
        lax.all_gather(migrated, "cuts", axis=0, tiled=True),
        lax.all_gather(combine.astype(jnp.bfloat16), "cuts", axis=0, tiled=True),
    )
    normed = norm_rows(whole_rows.astype(jnp.float32), attn_gain.astype(jnp.float32)).astype(
        jnp.bfloat16
    )
    q_raw = jnp.dot(normed, w_query, preferred_element_type=jnp.float32).astype(jnp.bfloat16)
    kv_raw = jnp.dot(normed, w_keyval, preferred_element_type=jnp.float32).astype(jnp.bfloat16)
    q_rows, kv_rows = (
        lax.all_to_all(q_raw, "cuts", split_axis=0, concat_axis=1, tiled=True),
        lax.all_to_all(kv_raw, "cuts", split_axis=0, concat_axis=1, tiled=True),
    )
    attention, cache_next = attend(q_rows, kv_rows, cache_rows, cache_len, q_gain, k_gain)
    attn_heads = lax.all_to_all(attention, "cuts", split_axis=1, concat_axis=0, tiled=True)
    slab_rows = attn_heads
    partial_value = jnp.dot(slab_rows, w_out, preferred_element_type=jnp.float32).astype(
        jnp.bfloat16
    )
    partial_value = lax.optimization_barrier(partial_value)
    attn_out = lax.psum_scatter(
        partial_value.astype(jnp.float32).astype(jnp.bfloat16),
        "cuts",
        scatter_dimension=0,
        tiled=True,
    ).astype(jnp.float32)
    mixed_rows = migrated.astype(jnp.float32) + attn_out
    moe_local = norm_rows(mixed_rows, moe_gain.astype(jnp.float32)).astype(jnp.bfloat16)
    moe_rows = lax.all_gather(moe_local, "cuts", axis=0, tiled=True)
    scale_column = lax.dynamic_slice_in_dim(whole_combine, cut_id // 2, 1, 1).astype(jnp.float32)
    column = scale_column[:, 0].reshape(cut_count, local_rows)
    pick, live = pick_slots(column > 0.0, slot_ids)
    rows_grid = moe_rows.reshape(cut_count, local_rows, -1)
    slab_rows = jnp.take_along_axis(rows_grid, pick[:, :, None], axis=1).reshape(
        cut_count * MOST, -1
    )
    slot_scale = jnp.where(live, jnp.take_along_axis(column, pick, axis=1), 0.0).reshape(-1, 1)
    gate_part = jnp.dot(slab_rows, w_gate, preferred_element_type=jnp.float32)
    upward = jnp.dot(slab_rows, w_up, preferred_element_type=jnp.float32)
    activation = (jax.nn.silu(gate_part) * upward * slot_scale).astype(jnp.bfloat16)
    partial_value = jnp.dot(activation, w_down, preferred_element_type=jnp.float32).astype(
        jnp.bfloat16
    )
    partial_value = lax.optimization_barrier(partial_value).reshape(cut_count, MOST, -1)
    returned = lax.all_to_all(partial_value, "cuts", split_axis=0, concat_axis=0, tiled=True)
    own_pick, own_live = pick_slots(jnp.transpose(combine > 0.0), slot_ids)
    sender_expert = jnp.arange(cut_count, dtype=jnp.int32) // 2
    sender_pick = own_pick[sender_expert]
    sender_live = own_live[sender_expert]
    placing = (
        (sender_pick[:, :, None] == slot_ids[None, None, :]) & sender_live[:, :, None]
    ).astype(jnp.bfloat16)
    moe_out = jnp.einsum("cks,ckd->sd", placing, returned, preferred_element_type=jnp.float32)
    hidden_next = (mixed_rows + moe_out).astype(jnp.bfloat16)
    return (hidden_next, cache_next)


def solution(mesh):
    in_specs = (
        P(("inst", "cuts"), None),
        P(("inst", "cuts"), None, None),
        P(("inst", "cuts")),
        P(("inst", "cuts")),
        P(("inst", "cuts"), None),
        P(("inst", "cuts"), None),
        P(),
        P(None, "cuts"),
        P(None, "cuts"),
        P(),
        P(),
        P("cuts", None),
        P(),
        P(None, "cuts"),
        P(None, "cuts"),
        P("cuts", None),
    )
    out_specs = (P(("inst", "cuts"), None), P(("inst", "cuts"), None, None))
    return jax.shard_map(body, mesh=mesh, in_specs=in_specs, out_specs=out_specs, check_vma=False)
```

profile of v0, /device:TPU:0, one launch (start us, length us, event | category | flops | bytes accessed | tf_op | source)
XLA Modules:
  0.0 784.7 jit_solution(12275309061389933406)
XLA Ops:
  10.1 7.4 all-reduce
  20.6 3.6 all-to-all-start
  25.1 4.7 all-to-all-done
  32.7 5.4 gather_fusion.2
  38.1 4.5 all-to-all-start.2
  43.0 70.4 %all-to-all-done.2 = bf16[4,2,128,1024]{3,2,1,0:T(8,128)(2,1)} async-done(((bf16[4,2,128,1024]{3,2,1,0:T(8,128)(2,1)}), bf16[4,2,128,1024]{3,2,1,0:T(8,128)(2,1)}, u32[]{:S(2)}, u32[]{:S(2)}) %all-to-all-start.2) | async-done | bytes 2097184 | tf_op jit(solution)/shard_map/all_to_all | solution.py:137
  113.4 6.7 gather_fusion.3
  120.1 122.8 %all-gather.4.cloned.1.call-done = bf16[1024,4096]{1,0:T(8,128)(2,1)} async-done(((bf16[32,4096]{1,0:T(8,128)(2,1)}), bf16[1024,4096]{1,0:T(8,128)(2,1)}) %all-gather.4.cloned.1.call-update) | async-done | bytes 8388624 | tf_op jit(solution)/shard_map/all_gather | solution.py:151
  243.0 5.2 fusion
  248.7 3.7 fusion.16
  253.5 7.2 all-to-all-start.3
  260.7 7.2 fusion.10
  269.1 7.2 all-to-all-start.1
  280.8 9.2 %broadcast_select_fusion.1 = (bf16[32,128,1024]{2,1,0:T(8,128)(2,1)}, bf16[32,128,1024]{2,1,0:T(8,128)(2,1)S(1)}) fusion(pred[32,128]{1,0:T(8,128)(4,1)S(1)} %get-tuple-element.30, bf16[32,1024]{1,0:T(8,128)(2,1)S(1)} %pad_maximum_fusion, bf16[32,128,1024]{2,1,0:T(8,128)(2,1)} %gather_fusion.3, bf16[32,128,1024]{2,1,0:T(8,128)(2,1)} %param.17, ...), kind=kLoop, calls=%fused_computation.14 | loop fusion | flops 8388608 | bytes 33624096 | tf_op jit(solution)/shard_map/jit(_where)/select_n | solution.py:73
  290.0 3.8 fusion.69
  293.8 6.4 copy.106
  300.2 6.4 copy.110
  311.7 2.4 reshape.390
  315.7 2.5 multiply_multiply_fusion
  324.9 3.2 fusion.13
  331.5 18.8 %all_to_all.63 = bf16[32,32,256]{2,0,1:T(8,128)(2,1)S(1)} all-to-all(bf16[32,32,256]{2,0,1:T(8,128)(2,1)S(1)} %copy.112), channel_id=1, replica_groups=mesh['inst'=4,'cuts'=32] {'cuts'}, dimensions={1} | all-to-all | bytes 1048576 | tf_op jit(solution)/shard_map/all_to_all | solution.py:164
  350.3 7.2 convolution_convert_fusion
  358.2 186.9 %reduce-scatter.2.cloned.1.call-done = bf16[32,4096]{1,0:T(8,128)(2,1)} async-done(((bf16[1024,4096]{1,0:T(8,128)(2,1)}), bf16[32,4096]{1,0:T(8,128)(2,1)}) %reduce-scatter.2.cloned.1.call-update) | async-done | bytes 262160 | tf_op jit(solution)/shard_map/reduce_scatter | solution.py:170
  548.1 80.6 %all-gather = bf16[32,32,16]{1,2,0:T(8,128)(2,1)S(1)} all-gather(bf16[1,32,16]{1,2,0:T(8,128)(2,1)S(1)} %convert_bitcast_fusion.1), channel_id=1, replica_groups=mesh['inst'=4,'cuts'=32] {'cuts'}, dimensions={0}, use_global_device_ids=true | all-gather | bytes 33792 | tf_op jit(solution)/shard_map/all_gather | solution.py:152
  633.1 104.8 %all-gather.6.cloned.1.call-done = bf16[1024,4096]{1,0:T(8,128)(2,1)} async-done(((bf16[32,4096]{1,0:T(8,128)(2,1)}), bf16[1024,4096]{1,0:T(8,128)(2,1)}) %all-gather.6.cloned.1.call-update) | async-done | bytes 8388624 | tf_op jit(solution)/shard_map/all_gather | solution.py:178
  737.9 4.9 gather_fusion.6
  742.8 3.7 fusion.25
  746.5 4.6 convolution_convert_fusion.1
  751.1 2.3 reshape.389
  753.4 6.0 all-to-all-start.5
  761.5 14.0 %all-to-all-done.5 = bf16[32,4,4096]{2,1,0:T(4,128)(2,1)} async-done(((bf16[32,4,4096]{2,1,0:T(4,128)(2,1)}), bf16[32,4,4096]{2,1,0:T(4,128)(2,1)}, u32[]{:S(2)}, u32[]{:S(2)}) %all-to-all-start.5) | async-done | bytes 1048608 | tf_op jit(solution)/shard_map/all_to_all | solution.py:194
  775.5 2.7 fusion.4
  (136 shorter events, 43.1 us)
Async XLA Ops:
  7.2 739.3 %copy-start = (bf16[384,4096]{1,0:T(8,128)(2,1)S(1)}, bf16[384,4096]{1,0:T(8,128)(2,1)}, u32[]{:S(2)}) copy-start(bf16[384,4096]{1,0:T(8,128)(2,1)} %param.31) | copy-start | bytes 9437188
  20.6 9.3 %all-to-all-start = ((bf16[4,2,4096]{2,1,0:T(2,128)(2,1)}), bf16[4,2,4096]{2,1,0:T(2,128)(2,1)S(1)}, u32[]{:S(2)}, u32[]{:S(2)}) async-start(bf16[4,2,4096]{2,1,0:T(2,128)(2,1)} %reshape.395), calls=%async_computation | async-start | bytes 131072 | tf_op jit(solution)/shard_map/all_to_all | solution.py:136
  24.2 218.8 %all-gather.4.cloned.1.call-start = ((), (), s32[]{:S(2)}) async-start(), calls=%async_computation.7 | async-start | bytes 8650752 | tf_op jit(solution)/shard_map/all_gather | solution.py:151
  32.6 10.0 %copy-start.12 = (s32[32]{0:T(128)S(1)}, s32[32]{0:T(128)}, u32[]{:S(2)}) copy-start(s32[32]{0:T(128)} %param.18) | copy-start | bytes 388
  32.6 10.0 %copy-start.6 = (bf16[4096]{0:T(1024)(128)(2,1)S(1)}, bf16[4096]{0:T(1024)(128)(2,1)}, u32[]{:S(2)}) copy-start(bf16[4096]{0:T(1024)(128)(2,1)} %param.22) | copy-start | bytes 24580
  32.7 10.2 %copy-start.8 = (f32[128]{0:T(128)S(1)}, f32[128]{0:T(128)}, u32[]{:S(2)}) copy-start(f32[128]{0:T(128)} %param.26) | copy-start | bytes 1540
  38.1 75.3 %all-to-all-start.2 = ((bf16[4,2,128,1024]{3,2,1,0:T(8,128)(2,1)}), bf16[4,2,128,1024]{3,2,1,0:T(8,128)(2,1)}, u32[]{:S(2)}, u32[]{:S(2)}) async-start(bf16[4,2,128,1024]{3,2,1,0:T(8,128)(2,1)} %bitcast.89), calls=%async_computation.2 | async-start | bytes 4194304 | tf_op jit(solution)/shard_map/all_to_all | solution.py:137
  243.0 5.8 copy-start.2
  253.5 15.6 %all-to-all-start.3 = ((bf16[32,2,512]{2,1,0:T(2,128)(2,1)}), bf16[32,2,512]{2,1,0:T(2,128)(2,1)S(1)}, u32[]{:S(2)}, u32[]{:S(2)}) async-start(bf16[32,2,512]{2,1,0:T(2,128)(2,1)} %reshape.476), calls=%async_computation.3 | async-start | bytes 131072 | tf_op jit(solution)/shard_map/all_to_all | solution.py:161
  269.1 37.5 %all-to-all-start.1 = ((bf16[32,32,256]{2,1,0:T(8,128)(2,1)}), bf16[32,32,256]{2,1,0:T(8,128)(2,1)}, u32[]{:S(2)}, u32[]{:S(2)}) async-start(bf16[32,32,256]{2,1,0:T(8,128)(2,1)} %bitcast.96), calls=%async_computation.1 | async-start | bytes 1048576 | tf_op jit(solution)/shard_map/all_to_all | solution.py:160
  276.3 268.7 %reduce-scatter.2.cloned.1.call-start = ((), (), s32[]{:S(2)}) async-start(), calls=%async_computation.8 | async-start | bytes 8650752 | tf_op jit(solution)/shard_map/reduce_scatter | solution.py:170
  306.6 9.1 %copy-start.11 = (f32[128]{0:T(128)S(1)}, f32[128]{0:T(128)}, u32[]{:S(2)}) copy-start(f32[128]{0:T(128)} %param.25) | copy-start | bytes 1540
  318.3 4.4 copy-start.1
  322.3 2.5 copy-start.3
  322.3 2.5 copy-start.5
  357.5 0.7 copy-start.7
  357.5 187.6 %copy-start.4 = (bf16[32,4096]{1,0:T(8,128)(2,1)S(1)}, bf16[32,4096]{1,0:T(8,128)(2,1)}, u32[]{:S(2)}) copy-start(bf16[32,4096]{1,0:T(8,128)(2,1)} %broadcast_select_fusion.6) | copy-start | bytes 786436
  357.5 190.6 %copy-start.10 = (bf16[32,8]{0,1:T(8,128)(2,1)S(1)}, bf16[32,8]{0,1:T(8,128)(2,1)}, u32[]{:S(2)}) copy-start(bf16[32,8]{0,1:T(8,128)(2,1)} %param.21) | copy-start | bytes 1540
  357.5 190.6 %copy-start.9 = (s32[32,8]{0,1:T(8,128)S(1)}, s32[32,8]{0,1:T(8,128)}, u32[]{:S(2)}) copy-start(s32[32,8]{0,1:T(8,128)} %param.20) | copy-start | bytes 3076
  357.6 380.4 %all-gather.6.cloned.1.call-start = ((), (), s32[]{:S(2)}) async-start(), calls=%async_computation.9 | async-start | bytes 8650752 | tf_op jit(solution)/shard_map/all_gather | solution.py:178
  753.4 22.1 %all-to-all-start.5 = ((bf16[32,4,4096]{2,1,0:T(4,128)(2,1)}), bf16[32,4,4096]{2,1,0:T(4,128)(2,1)}, u32[]{:S(2)}, u32[]{:S(2)}) async-start(bf16[32,4,4096]{2,1,0:T(4,128)(2,1)} %reshape.389), calls=%async_computation.6 | async-start | bytes 2097152 | tf_op jit(solution)/shard_map/all_to_all | solution.py:194
Sparse Core Ops, SparseCore 0:
  32.8 210.1 all-gather.3
  357.7 187.3 reduce-scatter.1
  548.2 189.7 all-gather.5
where the time goes:
time: 786 us; the launch traced here: 785 us
  waiting for transfers between devices  505 us (64%)
  blocking collectives  107 us (14%)
  local copies, waits for them, and re-layouts  62 us (8%)
  matrix products  34 us (4%)
  other arithmetic  33.1 us (4%)
  starting transfers between devices  28.9 us (4%)
  between operations  14.9 us (2%)
    reduce_scatter x1, waiting for transfers between devices, body(): lax.psum_scatter(partial_value.astype(jnp.float32).astype(jnp.bfloat16),...  187 us
    all_gather x1, waiting for transfers between devices, body(): lax.all_gather(migrated, 'cuts', axis=0, tiled=True)  123 us
    all_gather x1, waiting for transfers between devices, body(): moe_rows = lax.all_gather(moe_local, 'cuts', axis=0, tiled=True)  105 us
    all_gather x1, blocking collectives, body(): lax.all_gather(combine.astype(jnp.bfloat16), 'cuts', axis=0, tiled=True)  80.6 us
    all_to_all x1, waiting for transfers between devices, body(): lax.all_to_all(cache_kv[send_slot], 'inst', split_axis=0, concat_axis=0,...  70.4 us
    all_to_all x1, blocking collectives, body(): lax.all_to_all(attention, 'cuts', split_axis=1, concat_axis=0, tiled=True)  18.8 us
  transfers between devices with their start and end apart: 8, of which 7 were waited for; matrix products, arithmetic and copies ran while one was open for 7% of the time, Pallas kernels for 0%

commit v1 on v0

v1 whole, which is shorter than its diff:
```python
import functools
import jax
import jax.numpy as jnp
from jax import lax
from jax.experimental import pallas as pl
from jax.experimental.pallas import tpu as pltpu
from jax.sharding import PartitionSpec as P

HD = 128
MIG = 2
MOST = 4
EPSILON = 1e-06
ROPE_BASE = 1000000.0
SIDE = 4
PLANE = SIDE * SIDE
BF16 = jnp.bfloat16
F32 = jnp.float32


def cut_index(y, x, z):
    return (y * SIDE + x) * 2 + z


PLANES = [[cut_index(y, x, z) for y in range(SIDE) for x in range(SIDE)] for z in range(2)]


def pair_perm(side):
    out = []
    for z in range(4):
        other = z ^ 1 if side == 0 else (z + 1 if z % 2 else z - 1) % 4
        for core in range(2):
            for y in range(SIDE):
                for x in range(SIDE):
                    out.append(
                        (
                            ((z // 2) * 2 + core) * 32 + cut_index(y, x, z % 2),
                            ((other // 2) * 2 + core) * 32 + cut_index(y, x, other % 2),
                        )
                    )
    return out


def from_pair(array, side):
    return lax.ppermute(array, ("inst", "cuts"), pair_perm(side))


def norm_rows(values, gain_vec):
    mean_square = jnp.mean(values * values, axis=-1, keepdims=True)
    return values * lax.rsqrt(mean_square + EPSILON) * gain_vec


def attend_kernel(
    lens_ref, q_ref, kv_ref, cos_ref, sin_ref, qg_ref, kg_ref, cache_ref,
    att_ref, entry_ref, qs_ref, ks_ref, vs_ref, os_ref, *, rows_step, kv_count, group_size,
):
    step = pl.program_id(0)
    peers = q_ref.shape[0]
    per_peer = att_ref.shape[2] // HD
    length_cap = cache_ref.shape[1]
    width = kv_count * HD

    @pl.when(step == 0)
    def _():
        cosine = cos_ref[...]
        sine = sin_ref[...]

        def prepare(values, gain):
            values = norm_rows(values, gain)
            return values * cosine + pltpu.roll(values, HD // 2, 1) * sine

        for p in range(peers):
            for j in range(per_peer):
                values = q_ref[p, :, j * HD : (j + 1) * HD].astype(F32)
                qs_ref[:, p * per_peer + j, :] = prepare(values, qg_ref[...])
        for k in range(kv_count):
            key = prepare(kv_ref[:, k * HD : (k + 1) * HD].astype(F32), kg_ref[...]).astype(BF16)
            entry_ref[:, k * HD : (k + 1) * HD] = key
            ks_ref[:, k, :] = key.astype(F32)
            value = kv_ref[:, width + k * HD : width + (k + 1) * HD]
            entry_ref[:, width + k * HD : width + (k + 1) * HD] = value
            vs_ref[:, k, :] = value.astype(F32)

    scale = HD ** (-0.5)
    heads = kv_count * group_size
    positions = lax.broadcasted_iota(jnp.int32, (heads, length_cap), 1)
    spans = [slice(k * group_size, (k + 1) * group_size) for k in range(kv_count)]
    first = step * rows_step
    queries = [qs_ref[first + i].astype(BF16) for i in range(rows_step)]
    keys_new = [ks_ref[first + i] for i in range(rows_step)]
    values_new = [vs_ref[first + i] for i in range(rows_step)]
    scores = [
        jnp.concatenate(
            [
                lax.dot_general(
                    queries[i][spans[k]], cache_ref[i, :, k * HD : (k + 1) * HD],
                    (((1,), (1,)), ((), ())), preferred_element_type=F32,
                )
                for k in range(kv_count)
            ],
            axis=0,
        )
        for i in range(rows_step)
    ]
    outs = []
    for i in range(rows_step):
        spread = jnp.concatenate(
            [
                jnp.broadcast_to(keys_new[i][k : k + 1], (group_size, HD))
                for k in range(kv_count)
            ],
            axis=0,
        )
        self_score = jnp.sum(queries[i].astype(F32) * spread, axis=1, keepdims=True) * scale
        score = jnp.where(positions < lens_ref[first + i], scores[i] * scale, -1e30)
        peak = jnp.maximum(jnp.max(score, axis=1, keepdims=True), self_score)
        weights = jnp.exp(score - peak)
        self_weight = jnp.exp(self_score - peak)
        inverse = 1.0 / (jnp.sum(weights, axis=1, keepdims=True) + self_weight)
        outs.append(
            ((weights * inverse).astype(BF16), (self_weight * inverse).astype(BF16).astype(F32))
        )
    results = [
        jnp.concatenate(
            [
                jnp.dot(
                    outs[i][0][spans[k]],
                    cache_ref[i, :, width + k * HD : width + (k + 1) * HD],
                    preferred_element_type=F32,
                )
                + outs[i][1][spans[k]] * values_new[i][k : k + 1]
                for k in range(kv_count)
            ],
            axis=0,
        )
        for i in range(rows_step)
    ]
    for i in range(rows_step):
        os_ref[first + i] = results[i]

    @pl.when(step == pl.num_programs(0) - 1)
    def _():
        for p in range(peers):
            for j in range(per_peer):
                att_ref[p, :, j * HD : (j + 1) * HD] = os_ref[:, p * per_peer + j, :].astype(BF16)


def attend(q_peers, q_width, kv_rows, cache_kv, lengths, q_gain, k_gain):
    peers, rows, sent_width = q_peers.shape
    length_cap, entry_width = cache_kv.shape[1:]
    kv_count = entry_width // (2 * HD)
    heads = peers * q_width // HD
    rows_step = 4
    frequency = ROPE_BASE ** (-2.0 * jnp.arange(HD // 2, dtype=F32) / HD)
    angles = lengths.astype(F32)[:, None] * frequency[None, :]
    cosine = jnp.concatenate([jnp.cos(angles), jnp.cos(angles)], axis=-1)
    sine = jnp.concatenate([-jnp.sin(angles), jnp.sin(angles)], axis=-1)
    whole = lambda shape: pl.BlockSpec(shape, lambda i, lens: (0,) * len(shape))
    return pl.pallas_call(
        functools.partial(
            attend_kernel, rows_step=rows_step, kv_count=kv_count, group_size=heads // kv_count
        ),
        grid_spec=pltpu.PrefetchScalarGridSpec(
            num_scalar_prefetch=1,
            grid=(rows // rows_step,),
            in_specs=[
                whole((peers, rows, sent_width)),
                whole((rows, entry_width)),
                whole((rows, HD)),
                whole((rows, HD)),
                whole((1, HD)),
                whole((1, HD)),
                pl.BlockSpec((rows_step, length_cap, entry_width), lambda i, lens: (i, 0, 0)),
            ],
            out_specs=[whole((peers, rows, q_width)), whole((rows, entry_width))],
            scratch_shapes=[
                pltpu.VMEM((rows, heads, HD), F32),
                pltpu.VMEM((rows, kv_count, HD), F32),
                pltpu.VMEM((rows, kv_count, HD), F32),
                pltpu.VMEM((rows, heads, HD), F32),
            ],
        ),
        out_shape=[
            jax.ShapeDtypeStruct((peers, rows, q_width), BF16),
            jax.ShapeDtypeStruct((rows, entry_width), BF16),
        ],
        compiler_params=pltpu.CompilerParams(vmem_limit_bytes=32 * 1024 * 1024),
        cost_estimate=pl.CostEstimate(
            flops=4 * rows * heads * HD * length_cap,
            bytes_accessed=cache_kv.size * 2 + q_peers.size * 4,
            transcendentals=rows * heads * length_cap,
        ),
        name="attend",
    )(lengths, q_peers, kv_rows, cosine, sine, q_gain[None, :], k_gain[None, :], cache_kv)


def place_kernel(lens_ref, arrive_ref, slot_ref, entry_ref, cache_ref, landed_ref, out_ref):
    row = pl.program_id(0)
    position = lax.broadcasted_iota(jnp.int32, out_ref.shape[1:], 0)
    at_length = position == lens_ref[row]

    @pl.when(arrive_ref[row] == 0)
    def _():
        out_ref[0] = jnp.where(at_length, entry_ref[0], cache_ref[0])

    @pl.when(arrive_ref[row] != 0)
    def _():
        out_ref[0] = jnp.where(at_length, entry_ref[0], landed_ref[0])


def place_cache(lengths, arriving, landed_slot, entries, cache_kv, landed):
    rows, length_cap, entry_width = cache_kv.shape
    return pl.pallas_call(
        place_kernel,
        grid_spec=pltpu.PrefetchScalarGridSpec(
            num_scalar_prefetch=3,
            grid=(rows,),
            in_specs=[
                pl.BlockSpec((1, 1, entry_width), lambda i, a, b, c: (i, 0, 0)),
                pl.BlockSpec((1, length_cap, entry_width), lambda i, a, b, c: (i, 0, 0)),
                pl.BlockSpec((1, length_cap, entry_width), lambda i, a, b, c: (c[i], 0, 0)),
            ],
            out_specs=pl.BlockSpec((1, length_cap, entry_width), lambda i, a, b, c: (i, 0, 0)),
        ),
        out_shape=jax.ShapeDtypeStruct(cache_kv.shape, BF16),
        compiler_params=pltpu.CompilerParams(vmem_limit_bytes=16 * 1024 * 1024),
        cost_estimate=pl.CostEstimate(
            flops=0, bytes_accessed=cache_kv.size * 4, transcendentals=0
        ),
        name="place_cache",
    )(lengths, arriving.astype(jnp.int32), landed_slot, entries[:, None, :], cache_kv, landed)


def pick_kernel(slot_ref, *refs):
    count = len(refs) // 2
    for source, target in zip(refs[:count], refs[count:]):
        target[...] = source[...]


def pick_caches(slots, cache_kv):
    shifts, count = slots.shape
    block = (1,) + cache_kv.shape[1:]
    return pl.pallas_call(
        pick_kernel,
        grid_spec=pltpu.PrefetchScalarGridSpec(
            num_scalar_prefetch=1,
            grid=(count,),
            in_specs=[
                pl.BlockSpec(block, lambda i, slots, k=k: (slots[k, i], 0, 0))
                for k in range(shifts)
            ],
            out_specs=[pl.BlockSpec(block, lambda i, slots: (i, 0, 0)) for k in range(shifts)],
        ),
        out_shape=[
            jax.ShapeDtypeStruct((count,) + cache_kv.shape[1:], BF16) for k in range(shifts)
        ],
        compiler_params=pltpu.CompilerParams(vmem_limit_bytes=16 * 1024 * 1024),
        cost_estimate=pl.CostEstimate(
            flops=0,
            bytes_accessed=4 * shifts * count * cache_kv.shape[1] * cache_kv.shape[2],
            transcendentals=0,
        ),
        name="pick_caches",
    )(slots, *([cache_kv] * shifts))


def exchange(array):
    return lax.all_to_all(array, "cuts", 0, 0, tiled=True, axis_index_groups=PLANES)


def body(
    hidden,
    cache_kv,
    cache_len,
    mig_source,
    expert_ids,
    gate_w,
    attn_gain,
    w_query,
    w_keyval,
    q_gain,
    k_gain,
    w_out,
    moe_gain,
    w_gate,
    w_up,
    w_down,
):
    group_count = lax.axis_size("inst")
    cut_count = lax.axis_size("cuts")
    local_rows, width = hidden.shape
    group_total = local_rows * cut_count
    group_id = lax.axis_index("inst")
    cut_id = lax.axis_index("cuts")
    low = cut_id % 2 == 0
    slot_ids = jnp.arange(local_rows, dtype=jnp.int32)
    own_rows = (group_id * cut_count + cut_id) * local_rows + slot_ids

    w_query_pair = from_pair(w_query, 0)
    w_keyval_pair = from_pair(w_keyval, 0)
    w_out_pair = from_pair(w_out, 1)

    normed = norm_rows(hidden.astype(F32), attn_gain.astype(F32)).astype(BF16)
    plane_rows = exchange(jnp.broadcast_to(normed[None], (PLANE,) + normed.shape)).reshape(
        PLANE * local_rows, width
    )

    facts = jnp.stack([mig_source, cache_len]).astype(F32)
    all_facts = lax.all_to_all(
        jnp.broadcast_to(facts[None], (group_count,) + facts.shape), "inst", 0, 0, tiled=True
    )
    goes_to = all_facts[:, 0].astype(jnp.int32) == own_rows[None, :]
    lengths = jnp.sum(jnp.where(goes_to, all_facts[:, 1], 0.0), axis=0).astype(jnp.int32)
    targets = jnp.arange(group_count, dtype=jnp.int32)
    leaving = goes_to & (targets[:, None] != group_id)
    leave_rank = jnp.cumsum(leaving.astype(jnp.int32), axis=1) - 1
    chosen = leaving[:, None, :] & (
        leave_rank[:, None, :] == jnp.arange(MIG, dtype=jnp.int32)[None, :, None]
    )
    send_slot = jnp.sum(jnp.where(chosen, slot_ids[None, None, :], 0), axis=2)
    source_group = mig_source // group_total
    arriving = source_group != group_id
    from_group = (source_group[None, :] == targets[:, None]) & arriving[None, :]
    arrival_rank = jnp.sum(
        jnp.where(from_group, jnp.cumsum(from_group.astype(jnp.int32), axis=1) - 1, 0), axis=0
    )
    source_pick = jnp.where(arriving, source_group, 0)

    shifts = jnp.arange(1, group_count, dtype=jnp.int32)
    picked = pick_caches(send_slot[(group_id + shifts) % group_count], cache_kv)
    landed = jnp.concatenate(
        [
            lax.ppermute(
                array, "inst", [(g, (g + shift) % group_count) for g in range(group_count)]
            )
            for shift, array in zip(range(1, group_count), picked)
        ]
    )
    distance = (group_id - source_group) % group_count
    landed_slot = jnp.where(arriving, (distance - 1) * MIG + arrival_rank, 0)

    w_project = jnp.concatenate([w_query, w_query_pair, w_keyval, w_keyval_pair], axis=1)
    projected = jnp.dot(plane_rows, w_project, preferred_element_type=F32).astype(BF16)
    arrived = exchange(projected.reshape(PLANE, local_rows, -1))
    q_width = 2 * w_query.shape[1]
    kv_width = w_keyval.shape[1]
    own_kv = arrived[:, :, q_width : q_width + kv_width]
    pair_kv = arrived[:, :, q_width + kv_width :]
    kv_rows = jnp.where(
        low,
        jnp.concatenate([own_kv, pair_kv], axis=2),
        jnp.concatenate([pair_kv, own_kv], axis=2),
    )
    kv_rows = jnp.transpose(kv_rows, (1, 0, 2)).reshape(local_rows, -1)
    attention, entries = attend(arrived, q_width, kv_rows, cache_kv, lengths, q_gain, k_gain)

    w_gate, w_up, w_down, arrived_mark = lax.optimization_barrier(
        (w_gate, w_up, w_down, w_project)
    )
    w_gate_pair = from_pair(w_gate, 0)
    w_up_pair = from_pair(w_up, 1)

    w_out_both = jnp.concatenate([w_out, w_out_pair])
    attn_heads = exchange(attention).reshape(PLANE * local_rows, q_width)
    attn_heads, w_gate_pair, w_up_pair, landed, w_down = lax.optimization_barrier(
        (attn_heads, w_gate_pair, w_up_pair, landed, w_down)
    )
    w_down_pair = from_pair(w_down, 0)
    partial_value = jnp.dot(attn_heads, w_out_both, preferred_element_type=F32).astype(BF16)
    sums = exchange(partial_value.reshape(PLANE, local_rows, width))

    got_entries = lax.all_to_all(entries[send_slot], "inst", 0, 0, tiled=True)
    new_entries = jnp.where(arriving[:, None], got_entries[source_pick, arrival_rank], entries)
    cache_next = place_cache(cache_len, arriving, landed_slot, new_entries, cache_kv, landed)
    sums, cache_next, w_down_pair = lax.optimization_barrier((sums, cache_next, w_down_pair))

    mixed_rows = hidden.astype(F32) + jnp.sum(sums.astype(F32), axis=0)
    got_rows = lax.all_to_all(mixed_rows[send_slot], "inst", 0, 0, tiled=True)
    mixed_rows = jnp.where(arriving[:, None], got_rows[source_pick, arrival_rank], mixed_rows)
    moe_local = norm_rows(mixed_rows, moe_gain.astype(F32)).astype(BF16)

    expert_range = jnp.arange(PLANE, dtype=jnp.int32)
    combine = jnp.sum(
        jnp.where(
            expert_ids[:, :, None] == expert_range[None, None, :],
            gate_w.astype(F32)[:, :, None],
            0.0,
        ),
        axis=1,
    )
    flags = jnp.transpose(combine) > 0.0
    rank = jnp.cumsum(flags.astype(jnp.int32), axis=1) - 1
    slot_range = jnp.arange(MOST, dtype=jnp.int32)
    match = flags[:, None, :] & (rank[:, None, :] == slot_range[None, :, None])
    match = match.reshape(PLANE * MOST, local_rows)
    slab = jnp.dot(match.astype(BF16), moe_local, preferred_element_type=F32).astype(BF16)
    slab_rows = exchange(slab.reshape(PLANE, MOST, width)).reshape(PLANE * MOST, width)

    def expert_half(gate, up, down):
        gate_part = jnp.dot(slab_rows, gate, preferred_element_type=F32)
        upward = jnp.dot(slab_rows, up, preferred_element_type=F32)
        activation = (jax.nn.silu(gate_part) * upward).astype(BF16)
        return jnp.dot(activation, down, preferred_element_type=F32)

    expert_out = (
        expert_half(w_gate, w_up, w_down) + expert_half(w_gate_pair, w_up_pair, w_down_pair)
    ).astype(BF16)
    returned = exchange(expert_out.reshape(PLANE, MOST, width)).reshape(PLANE * MOST, width)
    slot_gate = jnp.where(
        match, jnp.repeat(jnp.transpose(combine), MOST, axis=0), 0.0
    ).astype(BF16)
    moe_out = lax.dot_general(
        slot_gate, returned, (((0,), (0,)), ((), ())), preferred_element_type=F32
    )
    hidden_next = (mixed_rows + moe_out).astype(BF16)
    return (hidden_next, cache_next)


def solution(mesh):
    in_specs = (
        P(("inst", "cuts"), None),
        P(("inst", "cuts"), None, None),
        P(("inst", "cuts")),
        P(("inst", "cuts")),
        P(("inst", "cuts"), None),
        P(("inst", "cuts"), None),
        P(),
        P(None, "cuts"),
        P(None, "cuts"),
        P(),
        P(),
        P("cuts", None),
        P(),
        P(None, "cuts"),
        P(None, "cuts"),
        P("cuts", None),
    )
    out_specs = (P(("inst", "cuts"), None), P(("inst", "cuts"), None, None))
    return jax.shard_map(body, mesh=mesh, in_specs=in_specs, out_specs=out_specs, check_vma=False)
```

time: 786 us -> 352 us (0.45)
  waiting for transfers between devices: 505 us -> 184 us
  blocking collectives: 107 us -> 17.7 us
  local copies, waits for them, and re-layouts: 62 us -> 22.6 us
  Pallas kernels: 0 us -> 28.1 us
  starting transfers between devices: 28.9 us -> 52.4 us
  other arithmetic: 33.1 us -> 16.3 us
  between operations: 14.9 us -> 1.1 us
    all_gather x2 -> x0, waiting for transfers between devices: 228 us -> none  [the longest x1 123 us: body(): lax.all_gather(migrated, 'cuts', axis=0, tiled=True)]
    reduce_scatter x1 -> x0, waiting for transfers between devices: 187 us -> none  [body(): lax.psum_scatter(partial_value.astype(jnp.float32).astype(jnp.bfloat16),...]
    ppermute x0 -> x9, waiting for transfers between devices: none -> 144 us  [the longest x6 102 us: from_pair(): return lax.ppermute(array, ('inst', 'cuts'), pair_perm(side))]
    all_gather x1 -> x0, blocking collectives: 80.6 us -> none  [body(): lax.all_gather(combine.astype(jnp.bfloat16), 'cuts', axis=0, tiled=True)]
    all_to_all x5 -> x8, waiting for transfers between devices: 90.4 us -> 40.5 us  [the longest x5 32.1 us: exchange(): lax.all_to_all(array, 'cuts', 0, 0, tiled=True, axis_index_groups=PLANES)]
    pallas_call x0 -> x3, Pallas kernels: none -> 28.1 us  [the longest x1 14.6 us: attend(): pl.pallas_call(functools.partial(attend_kernel, rows_step=rows_step, kv_c...]
    gather x13 -> x7, local copies, waits for them, and re-layouts: 23.2 us -> 5.18 us  [the longest x1 1.35 us: body(): got_rows[source_pick, arrival_rank]]
    slice x3 -> x1, local copies, waits for them, and re-layouts: 16.6 us -> 0.11 us  [body(): pair_kv = arrived[:, :, q_width + kv_width:]]
  transfers between devices with their start and end apart: 8 -> 17, of which waited for: 7 -> 8; matrix products, arithmetic and copies ran while one was open for 7% -> 9% of each run, Pallas kernels for 0% -> 8%
where the time goes in v1:
time: 352 us; the launch traced here: 350 us
  waiting for transfers between devices  184 us (52%)
  starting transfers between devices  52.4 us (15%)
  Pallas kernels  28.1 us (8%)
  matrix products  28.1 us (8%)
  local copies, waits for them, and re-layouts  22.6 us (6%)
  blocking collectives  17.7 us (5%)
  other arithmetic  16.3 us (5%)
    ppermute x6, waiting for transfers between devices, from_pair(): return lax.ppermute(array, ('inst', 'cuts'), pair_perm(side))  102 us
    ppermute x3, waiting for transfers between devices, body(): lax.ppermute(array, 'inst', [(g, (g + shift) % group_count) for g in rang...  41.6 us
    all_to_all x5, waiting for transfers between devices, exchange(): lax.all_to_all(array, 'cuts', 0, 0, tiled=True, axis_index_groups=PLANES)  32.1 us
    all_to_all x5, starting transfers between devices, exchange(): lax.all_to_all(array, 'cuts', 0, 0, tiled=True, axis_index_groups=PLANES)  28.8 us
    all_to_all x1, blocking collectives, exchange(): lax.all_to_all(array, 'cuts', 0, 0, tiled=True, axis_index_groups=PLANES)  17.7 us
    pallas_call x1, Pallas kernels, attend(): pl.pallas_call(functools.partial(attend_kernel, rows_step=rows_step, kv_c...  14.6 us
    pallas_call x1, Pallas kernels, place_cache(): pl.pallas_call(place_kernel, grid_spec=pltpu.PrefetchScalarGridSpec(num_s...  12.7 us
    unnamed x27, local copies, waits for them, and re-layouts  10.7 us
  transfers between devices with their start and end apart: 17, of which 8 were waited for; matrix products, arithmetic and copies ran while one was open for 9% of the time, Pallas kernels for 8%

profile of v1, /device:TPU:0, one launch (start us, length us, event | category | flops | bytes accessed | tf_op | source)
XLA Modules:
  0.0 350.3 jit_solution(10654190050667086298)
XLA Ops:
  1.9 5.2 %all-to-all-start = ((f32[4,2,32]{2,1,0:T(2,128)}), f32[4,2,32]{2,1,0:T(2,128)S(1)}, u32[]{:S(2)}, u32[]{:S(2)}) async-start(f32[4,2,32]{2,1,0:T(2,128)} %broadcast_in_dim.65), calls=%async_computation | async-start | bytes 8192 | tf_op jit(solution)/shard_map/all_to_all | solution.py:308
  10.0 2.4 all-to-all-done
  12.4 2.5 broadcast_in_dim.67
  14.9 7.2 %all-to-all-start.1 = ((bf16[16,32,4096]{2,1,0:T(8,128)(2,1)}), bf16[16,32,4096]{2,1,0:T(8,128)(2,1)}, u32[]{:S(2)}, u32[]{:S(2)}) async-start(bf16[16,32,4096]{2,1,0:T(8,128)(2,1)} %broadcast_in_dim.67), calls=%async_computation.1 | async-start | bytes 8388608 | tf_op jit(solution)/shard_map/all_to_all | solution.py:267
  26.2 48.9 %collective-permute-done.1 = bf16[4096,32]{0,1:T(8,128)(2,1)S(1)} collective-permute-done((bf16[4096,32]{0,1:T(8,128)(2,1)S(1)}, bf16[4096,32]{0,1:T(8,128)(2,1)S(1)}, u32[]{:S(2)}, u32[]{:S(2)}) %collective-permute-start.1) | collective-permute-done | bytes 262176 | tf_op jit(solution)/shard_map/ppermute | solution.py:44
  75.6 6.4 %pad_maximum_fusion = bf16[4096,576]{1,0:T(8,128)(2,1)} fusion(bf16[4096,32]{1,0:T(8,128)(2,1)S(1)} %copy.61, bf16[4096,32]{1,0:T(8,128)(2,1)S(1)} %copy.60, bf16[4096,256]{1,0:T(8,128)(2,1)} %collective-permute-done, bf16[4096,256]{1,0:T(8,128)(2,1)} %param.23), kind=kLoop, calls=%fused_computation.7 | loop fusion | flops 18874368 | bytes 9437184 | tf_op jit(solution)/shard_map/concatenate | solution.py:341
  85.1 3.4 copy-done
  91.5 6.4 %convolution_convert_fusion.2 = bf16[512,576]{0,1:T(8,128)(2,1)S(1)} fusion(bf16[512,4096]{1,0:T(8,128)(2,1)} %bitcast.4, bf16[4096,576]{1,0:T(8,128)(2,1)} %pad_maximum_fusion), kind=kOutput, calls=%fused_computation.18 | convolution fusion | flops 2416214016 | bytes 9502720 | tf_op jit(solution)/shard_map/dot_general | solution.py:342
  99.0 6.8 %all-to-all-start.2 = ((bf16[16,32,576]{2,1,0:T(8,128)(2,1)}), bf16[16,32,576]{2,1,0:T(8,128)(2,1)S(1)}, u32[]{:S(2)}, u32[]{:S(2)}) async-start(bf16[16,32,576]{2,1,0:T(8,128)(2,1)} %bitcast.5), calls=%async_computation.2 | async-start | bytes 1310720 | tf_op jit(solution)/shard_map/all_to_all | solution.py:267
  106.1 13.0 %all-to-all-done.2.q_ref = bf16[16,32,576]{2,1,0:T(8,128)(2,1)S(1)} async-done(((bf16[16,32,576]{2,1,0:T(8,128)(2,1)}), bf16[16,32,576]{2,1,0:T(8,128)(2,1)S(1)}, u32[]{:S(2)}, u32[]{:S(2)}) %all-to-all-start.2) | async-done | bytes 589856 | tf_op jit(solution)/shard_map/all_to_all | solution.py:267
  119.2 41.6 %collective-permute-done.6 = bf16[2,128,1024]{2,1,0:T(8,128)(2,1)S(1)} collective-permute-done((bf16[2,128,1024]{2,1,0:T(8,128)(2,1)S(1)}, bf16[2,128,1024]{2,1,0:T(8,128)(2,1)S(1)}, u32[]{:S(2)}, u32[]{:S(2)}) %collective-permute-start.6) | collective-permute-done | bytes 524320 | tf_op jit(solution)/shard_map/ppermute | solution.py:332
  160.8 2.8 collective-permute-start.4
  164.0 3.4 copy-done.1
  167.3 14.6 %attend.1 = (bf16[16,32,512]{2,1,0:T(8,128)(2,1)}, bf16[32,1024]{1,0:T(8,128)(2,1)S(1)}) custom-call(s32[32]{0:T(128)S(1)} %get-tuple-element.50.lens_ref, bf16[16,32,576]{2,1,0:T(8,128)(2,1)S(1)} %all-to-all-done.2.q_ref, bf16[32,1024]{1,0:T(8,128)(2,1)S(1)} %reshape.215.kv_ref, f32[32,128]{1,0:T(8,128)S(1)} %get-tuple-element.51.cos_ref, ...), custom_call_target="tpu_custom_call" | custom-call | flops 134217728 | bytes 9568256 | tf_op jit(solution)/shard_map/attend/pallas_call | solution.py:158
  182.0 6.5 %all-to-all-start.3 = ((bf16[16,32,512]{2,1,0:T(8,128)(2,1)}), bf16[16,32,512]{2,1,0:T(8,128)(2,1)S(1)}, u32[]{:S(2)}, u32[]{:S(2)}) async-start(bf16[16,32,512]{2,1,0:T(8,128)(2,1)} %get-tuple-element.18), calls=%async_computation.3 | async-start | bytes 1048576 | tf_op jit(solution)/shard_map/all_to_all | solution.py:267
  191.4 8.8 %all-to-all-done.3 = bf16[16,32,512]{2,1,0:T(8,128)(2,1)S(1)} async-done(((bf16[16,32,512]{2,1,0:T(8,128)(2,1)}), bf16[16,32,512]{2,1,0:T(8,128)(2,1)S(1)}, u32[]{:S(2)}, u32[]{:S(2)}) %all-to-all-start.3) | async-done | bytes 524320 | tf_op jit(solution)/shard_map/all_to_all | solution.py:267
  200.2 3.3 all-to-all-start.5
  203.5 6.5 %convolution_convert_fusion = bf16[512,4096]{1,0:T(8,128)(2,1)} fusion(bf16[512,512]{1,0:T(8,128)(2,1)S(1)} %bitcast.63, bf16[256,4096]{1,0:T(8,128)(2,1)} %collective-permute-done.7, bf16[256,4096]{1,0:T(8,128)(2,1)} %param.27), kind=kOutput, calls=%fused_computation.6 | convolution fusion | flops 2157969408 | bytes 8912896 | tf_op jit(solution)/shard_map/dot_general | solution.py:368
  210.0 4.7 %all-to-all-start.4 = ((bf16[16,32,4096]{2,1,0:T(8,128)(2,1)}), bf16[16,32,4096]{2,1,0:T(8,128)(2,1)}, u32[]{:S(2)}, u32[]{:S(2)}) async-start(bf16[16,32,4096]{2,1,0:T(8,128)(2,1)} %bitcast.62), calls=%async_computation.4 | async-start | bytes 8388608 | tf_op jit(solution)/shard_map/all_to_all | solution.py:267
  216.4 3.4 copy-done.2
  219.8 12.7 %place_cache.1 = bf16[32,128,1024]{2,1,0:T(8,128)(2,1)} custom-call(s32[32]{0:T(128)S(1)} %copy-done.3, s32[32]{0:T(128)S(1)} %fusion.48.arrive_ref, s32[32]{0:T(128)S(1)} %fusion.34.slot_ref, bf16[32,1,1024]{2,1,0:T(2,128)(2,1)S(1)} %copy.66.entry_ref, bf16[32,128,1024]{2,1,0:T(8,128)(2,1)S(1)} %copy-done.2, ...), custom_call_target="tpu_custom_call" | custom-call | bytes 16777216 | tf_op jit(solution)/shard_map/place_cache/pallas_call | solution.py:212
  232.5 53.1 %collective-permute-done.8 = bf16[384,4096]{1,0:T(8,128)(2,1)} collective-permute-done((bf16[384,4096]{1,0:T(8,128)(2,1)}, bf16[384,4096]{1,0:T(8,128)(2,1)}, u32[]{:S(2)}, u32[]{:S(2)}) %collective-permute-start.8) | collective-permute-done | bytes 3145760 | tf_op jit(solution)/shard_map/ppermute | solution.py:44
  285.6 3.0 convert_reduce_fusion
  290.0 4.4 %all-to-all-start.6 = ((f32[4,2,4096]{2,1,0:T(2,128)}), f32[4,2,4096]{2,1,0:T(2,128)S(1)}, u32[]{:S(2)}, u32[]{:S(2)}) async-start(f32[4,2,4096]{2,1,0:T(2,128)} %reshape.244), calls=%async_computation.6 | async-start | bytes 262144 | tf_op jit(solution)/shard_map/all_to_all | solution.py:377
  294.6 6.0 %all-to-all-done.6 = f32[4,2,4096]{2,1,0:T(2,128)S(1)} async-done(((f32[4,2,4096]{2,1,0:T(2,128)}), f32[4,2,4096]{2,1,0:T(2,128)S(1)}, u32[]{:S(2)}, u32[]{:S(2)}) %all-to-all-start.6) | async-done | bytes 131104 | tf_op jit(solution)/shard_map/all_to_all | solution.py:377
  302.8 17.7 %all_to_all.45 = bf16[16,4,4096]{2,1,0:T(4,128)(2,1)S(1)} all-to-all(bf16[16,4,4096]{2,1,0:T(4,128)(2,1)S(1)} %reshape.218), channel_id=1, replica_groups={{0,2,4,6,8,10,12,14,16,18,20,22,24,26,28,30},{1,3,5,7,9,11,13,15,17,19,..., dimensions={0} | all-to-all | bytes 1048576 | tf_op jit(solution)/shard_map/all_to_all | solution.py:267
  320.6 2.5 fusion.54
  323.1 2.5 fusion.55
  325.6 4.4 %fusion.19 = f32[64,4096]{1,0:T(8,128)S(1)} fusion(bf16[384,4096]{1,0:T(8,128)(2,1)} %collective-permute-done.8, f32[64,384]{1,0:T(8,128)S(1)} %fusion.55, bf16[64,4096]{1,0:T(8,128)(2,1)S(1)} %reshape.219, bf16[4096,384]{1,0:T(8,128)(2,1)} %collective-permute-done.3), kind=kOutput, calls=%fused_computation.44 | convolution fusion | flops 402800640 | bytes 7962624 | tf_op jit(solution)/shard_map/dot_general | solution.py:402
  329.9 4.4 %fusion = bf16[64,4096]{1,0:T(8,128)(2,1)S(1)} fusion(f32[64,4096]{1,0:T(8,128)S(1)} %fusion.19, bf16[384,4096]{1,0:T(8,128)(2,1)} %param.31, bf16[64,4096]{1,0:T(8,128)(2,1)S(1)} %reshape.219, bf16[4096,384]{1,0:T(8,128)(2,1)} %param.30, f32[64,384]{1,0:T(8,128)S(1)} %fusion.54), kind=kOutput, calls=%fused_computation.9 | convolution fusion | flops 403324928 | bytes 8486912 | tf_op jit(solution)/shard_map/dot_general | solution.py:402
  335.3 3.6 %all-to-all-start.8 = ((bf16[16,4,4096]{2,1,0:T(4,128)(2,1)}), bf16[16,4,4096]{2,1,0:T(4,128)(2,1)S(1)}, u32[]{:S(2)}, u32[]{:S(2)}) async-start(bf16[16,4,4096]{2,1,0:T(4,128)(2,1)} %reshape.220), calls=%async_computation.8 | async-start | bytes 1048576 | tf_op jit(solution)/shard_map/all_to_all | solution.py:267
  338.9 10.3 %all-to-all-done.8 = bf16[16,4,4096]{2,1,0:T(4,128)(2,1)S(1)} async-done(((bf16[16,4,4096]{2,1,0:T(4,128)(2,1)}), bf16[16,4,4096]{2,1,0:T(4,128)(2,1)S(1)}, u32[]{:S(2)}, u32[]{:S(2)}) %all-to-all-start.8) | async-done | bytes 524320 | tf_op jit(solution)/shard_map/all_to_all | solution.py:267
  (110 shorter events, 26.9 us)
Async XLA Ops:
  1.9 10.5 %all-to-all-start = ((f32[4,2,32]{2,1,0:T(2,128)}), f32[4,2,32]{2,1,0:T(2,128)S(1)}, u32[]{:S(2)}, u32[]{:S(2)}) async-start(f32[4,2,32]{2,1,0:T(2,128)} %broadcast_in_dim.65), calls=%async_computation | async-start | bytes 8192 | tf_op jit(solution)/shard_map/all_to_all | solution.py:308
  14.9 8.3 %copy-start.8 = (bf16[4096,32]{0,1:T(8,128)(2,1)S(1)}, bf16[4096,32]{0,1:T(8,128)(2,1)}, u32[]{:S(2)}) copy-start(bf16[4096,32]{0,1:T(8,128)(2,1)} %param.24) | copy-start | bytes 786436
  14.9 76.5 %all-to-all-start.1 = ((bf16[16,32,4096]{2,1,0:T(8,128)(2,1)}), bf16[16,32,4096]{2,1,0:T(8,128)(2,1)}, u32[]{:S(2)}, u32[]{:S(2)}) async-start(bf16[16,32,4096]{2,1,0:T(8,128)(2,1)} %broadcast_in_dim.67), calls=%async_computation.1 | async-start | bytes 8388608 | tf_op jit(solution)/shard_map/all_to_all | solution.py:267
  22.2 53.5 %collective-permute-start = (bf16[4096,256]{1,0:T(8,128)(2,1)}, bf16[4096,256]{1,0:T(8,128)(2,1)}, u32[]{:S(2)}, u32[]{:S(2)}) collective-permute-start(bf16[4096,256]{1,0:T(8,128)(2,1)} %param.23), channel_id=1, source_target_pairs={{0,1},{2,3},{4,5},{6,7},{8,9},{10,11},{12,13},{14,15},{16,17},{18,... | collective-permute-start | bytes 6291464 | tf_op jit(solution)/shard_map/ppermute | solution.py:44
  23.3 51.9 %collective-permute-start.1 = (bf16[4096,32]{0,1:T(8,128)(2,1)S(1)}, bf16[4096,32]{0,1:T(8,128)(2,1)S(1)}, u32[]{:S(2)}, u32[]{:S(2)}) collective-permute-start(bf16[4096,32]{0,1:T(8,128)(2,1)S(1)} %copy-done.8), channel_id=1, source_target_pairs={{0,1},{2,3},{4,5},{6,7},{8,9},{10,11},{12,13},{14,15},{16,17},{18,... | collective-permute-start | bytes 786440 | tf_op jit(solution)/shard_map/ppermute | solution.py:44
  24.3 179.2 %collective-permute-start.7 = (bf16[256,4096]{1,0:T(8,128)(2,1)}, bf16[256,4096]{1,0:T(8,128)(2,1)}, u32[]{:S(2)}, u32[]{:S(2)}) collective-permute-start(bf16[256,4096]{1,0:T(8,128)(2,1)} %param.27), channel_id=1, source_target_pairs={{0,65},{2,67},{4,69},{6,71},{8,73},{10,75},{12,77},{14,79},{16,81}... | collective-permute-start | bytes 6291464 | tf_op jit(solution)/shard_map/ppermute | solution.py:44
  82.0 121.4 %collective-permute-start.2 = (bf16[4096,384]{1,0:T(8,128)(2,1)}, bf16[4096,384]{1,0:T(8,128)(2,1)}, u32[]{:S(2)}, u32[]{:S(2)}) collective-permute-start(bf16[4096,384]{1,0:T(8,128)(2,1)} %param.29), channel_id=1, source_target_pairs={{0,1},{2,3},{4,5},{6,7},{8,9},{10,11},{12,13},{14,15},{16,17},{18,... | collective-permute-start | bytes 9437192 | tf_op jit(solution)/shard_map/ppermute | solution.py:44
  83.0 120.4 %collective-permute-start.3 = (bf16[4096,384]{1,0:T(8,128)(2,1)}, bf16[4096,384]{1,0:T(8,128)(2,1)}, u32[]{:S(2)}, u32[]{:S(2)}) collective-permute-start(bf16[4096,384]{1,0:T(8,128)(2,1)} %param.30), channel_id=1, source_target_pairs={{0,65},{2,67},{4,69},{6,71},{8,73},{10,75},{12,77},{14,79},{16,81}... | collective-permute-start | bytes 9437192 | tf_op jit(solution)/shard_map/ppermute | solution.py:44
  85.1 3.4 copy-start
  89.2 71.6 %collective-permute-start.6 = (bf16[2,128,1024]{2,1,0:T(8,128)(2,1)S(1)}, bf16[2,128,1024]{2,1,0:T(8,128)(2,1)S(1)}, u32[]{:S(2)}, u32[]{:S(2)}) collective-permute-start(bf16[2,128,1024]{2,1,0:T(8,128)(2,1)S(1)} %get-tuple-element.23), channel_id=1, source_target_pairs={{0,96},{32,0},{64,32},{96,64},{1,97},{33,1},{65,33},{97,65},{2,98}... | collective-permute-start | bytes 1572872 | tf_op jit(solution)/shard_map/ppermute | solution.py:332
  89.3 99.4 %collective-permute-start.5 = (bf16[2,128,1024]{2,1,0:T(8,128)(2,1)S(1)}, bf16[2,128,1024]{2,1,0:T(8,128)(2,1)}, u32[]{:S(2)}, u32[]{:S(2)}) collective-permute-start(bf16[2,128,1024]{2,1,0:T(8,128)(2,1)S(1)} %get-tuple-element.22), channel_id=1, source_target_pairs={{0,64},{32,96},{64,0},{96,32},{1,65},{33,97},{65,1},{97,33},{2,66}... | collective-permute-start | bytes 1572872 | tf_op jit(solution)/shard_map/ppermute | solution.py:332
  97.9 66.0 %copy-start.4 = (f32[128]{0:T(128)S(1)}, f32[128]{0:T(128)}, u32[]{:S(2)}) copy-start(f32[128]{0:T(128)} %param.25) | copy-start | bytes 1540
  97.9 66.0 %copy-start.5 = (f32[128]{0:T(128)S(1)}, f32[128]{0:T(128)}, u32[]{:S(2)}) copy-start(f32[128]{0:T(128)} %param.26) | copy-start | bytes 1540
  99.0 20.1 %all-to-all-start.2 = ((bf16[16,32,576]{2,1,0:T(8,128)(2,1)}), bf16[16,32,576]{2,1,0:T(8,128)(2,1)S(1)}, u32[]{:S(2)}, u32[]{:S(2)}) async-start(bf16[16,32,576]{2,1,0:T(8,128)(2,1)} %bitcast.5), calls=%async_computation.2 | async-start | bytes 1310720 | tf_op jit(solution)/shard_map/all_to_all | solution.py:267
  160.8 21.2 %copy-start.7 = (bf16[2,128,1024]{2,1,0:T(8,128)(2,1)}, bf16[2,128,1024]{2,1,0:T(8,128)(2,1)S(1)}, u32[]{:S(2)}) copy-start(bf16[2,128,1024]{2,1,0:T(8,128)(2,1)S(1)} %collective-permute-done.6) | copy-start | bytes 1572868
  160.8 27.9 %collective-permute-start.4 = (bf16[2,128,1024]{2,1,0:T(8,128)(2,1)S(1)}, bf16[2,128,1024]{2,1,0:T(8,128)(2,1)}, u32[]{:S(2)}, u32[]{:S(2)}) collective-permute-start(bf16[2,128,1024]{2,1,0:T(8,128)(2,1)S(1)} %get-tuple-element.21), channel_id=1, source_target_pairs={{0,32},{32,64},{64,96},{96,0},{1,33},{33,65},{65,97},{97,1},{2,34}... | collective-permute-start | bytes 1572872 | tf_op jit(solution)/shard_map/ppermute | solution.py:332
  164.0 3.4 copy-start.1
  182.0 18.2 %all-to-all-start.3 = ((bf16[16,32,512]{2,1,0:T(8,128)(2,1)}), bf16[16,32,512]{2,1,0:T(8,128)(2,1)S(1)}, u32[]{:S(2)}, u32[]{:S(2)}) async-start(bf16[16,32,512]{2,1,0:T(8,128)(2,1)} %get-tuple-element.18), calls=%async_computation.3 | async-start | bytes 1048576 | tf_op jit(solution)/shard_map/all_to_all | solution.py:267
  200.2 9.8 %all-to-all-start.5 = ((bf16[4,2,1024]{2,1,0:T(2,128)(2,1)}), bf16[4,2,1024]{2,1,0:T(2,128)(2,1)S(1)}, u32[]{:S(2)}, u32[]{:S(2)}) async-start(bf16[4,2,1024]{2,1,0:T(2,128)(2,1)} %reshape.230), calls=%async_computation.5 | async-start | bytes 32768 | tf_op jit(solution)/shard_map/all_to_all | solution.py:371
  210.0 4.9 %copy-start.12 = (s32[32]{0:T(128)S(1)}, s32[32]{0:T(128)}, u32[]{:S(2)}) copy-start(s32[32]{0:T(128)} %param.19) | copy-start | bytes 388
  210.0 5.1 %copy-start.11 = (bf16[32,8]{0,1:T(8,128)(2,1)S(1)}, bf16[32,8]{0,1:T(8,128)(2,1)}, u32[]{:S(2)}) copy-start(bf16[32,8]{0,1:T(8,128)(2,1)} %param.21) | copy-start | bytes 1540
  210.0 5.1 %copy-start.10 = (s32[32,8]{0,1:T(8,128)S(1)}, s32[32,8]{0,1:T(8,128)}, u32[]{:S(2)}) copy-start(s32[32,8]{0,1:T(8,128)} %param.20) | copy-start | bytes 3076
  210.0 6.3 %copy-start.3 = (s32[32]{0:T(128)S(1)}, s32[32]{0:T(128)}, u32[]{:S(2)}) copy-start(s32[32]{0:T(128)} %lens_ref.1) | copy-start | bytes 388
  210.0 75.6 %all-to-all-start.4 = ((bf16[16,32,4096]{2,1,0:T(8,128)(2,1)}), bf16[16,32,4096]{2,1,0:T(8,128)(2,1)}, u32[]{:S(2)}, u32[]{:S(2)}) async-start(bf16[16,32,4096]{2,1,0:T(8,128)(2,1)} %bitcast.62), calls=%async_computation.4 | async-start | bytes 8388608 | tf_op jit(solution)/shard_map/all_to_all | solution.py:267
  214.8 70.9 %collective-permute-start.8 = (bf16[384,4096]{1,0:T(8,128)(2,1)}, bf16[384,4096]{1,0:T(8,128)(2,1)}, u32[]{:S(2)}, u32[]{:S(2)}) collective-permute-start(bf16[384,4096]{1,0:T(8,128)(2,1)} %param.31), channel_id=1, source_target_pairs={{0,1},{2,3},{4,5},{6,7},{8,9},{10,11},{12,13},{14,15},{16,17},{18,... | collective-permute-start | bytes 9437192 | tf_op jit(solution)/shard_map/ppermute | solution.py:44
  216.4 3.4 copy-start.2
  232.5 56.2 %copy-start.6 = (bf16[32,4096]{1,0:T(8,128)(2,1)S(1)}, bf16[32,4096]{1,0:T(8,128)(2,1)}, u32[]{:S(2)}) copy-start(bf16[32,4096]{1,0:T(8,128)(2,1)} %param.16) | copy-start | bytes 786436
  232.5 62.0 %copy-start.9 = (bf16[4096]{0:T(1024)(128)(2,1)S(1)}, bf16[4096]{0:T(1024)(128)(2,1)}, u32[]{:S(2)}) copy-start(bf16[4096]{0:T(1024)(128)(2,1)} %param.28) | copy-start | bytes 24580
  290.0 10.6 %all-to-all-start.6 = ((f32[4,2,4096]{2,1,0:T(2,128)}), f32[4,2,4096]{2,1,0:T(2,128)S(1)}, u32[]{:S(2)}, u32[]{:S(2)}) async-start(f32[4,2,4096]{2,1,0:T(2,128)} %reshape.244), calls=%async_computation.6 | async-start | bytes 262144 | tf_op jit(solution)/shard_map/all_to_all | solution.py:377
  335.3 13.9 %all-to-all-start.8 = ((bf16[16,4,4096]{2,1,0:T(4,128)(2,1)}), bf16[16,4,4096]{2,1,0:T(4,128)(2,1)S(1)}, u32[]{:S(2)}, u32[]{:S(2)}) async-start(bf16[16,4,4096]{2,1,0:T(4,128)(2,1)} %reshape.220), calls=%async_computation.8 | async-start | bytes 1048576 | tf_op jit(solution)/shard_map/all_to_all | solution.py:267

commit v2 on v1

--- a/solution.py
+++ b/solution.py
@@ -13,6 +13,7 @@
 ROPE_BASE = 1000000.0
 SIDE = 4
 PLANE = SIDE * SIDE
+VMEM_BYTES = 56 * 1024 * 1024
 BF16 = jnp.bfloat16
 F32 = jnp.float32
 
@@ -22,6 +23,17 @@
 
 
 PLANES = [[cut_index(y, x, z) for y in range(SIDE) for x in range(SIDE)] for z in range(2)]
+COLUMNS = [[cut_index(y, x, z) for y in range(SIDE)] for x in range(SIDE) for z in range(2)]
+
+
+def shift(array, dy, dx):
+    moves = [
+        (cut_index(y, x, z), cut_index((y + dy) % SIDE, (x + dx) % SIDE, z))
+        for y in range(SIDE)
+        for x in range(SIDE)
+        for z in range(2)
+    ]
+    return lax.ppermute(array, "cuts", moves)
 
 
 def pair_perm(side):
@@ -144,12 +156,13 @@
                 att_ref[p, :, j * HD : (j + 1) * HD] = os_ref[:, p * per_peer + j, :].astype(BF16)
 
 
-def attend(q_peers, q_width, kv_rows, cache_kv, lengths, q_gain, k_gain):
+def attend(q_peers, q_width, kv_rows, cache_kv, first_row, lengths, q_gain, k_gain):
     peers, rows, sent_width = q_peers.shape
     length_cap, entry_width = cache_kv.shape[1:]
     kv_count = entry_width // (2 * HD)
     heads = peers * q_width // HD
     rows_step = 4
+    first_step = first_row // rows_step
     frequency = ROPE_BASE ** (-2.0 * jnp.arange(HD // 2, dtype=F32) / HD)
     angles = lengths.astype(F32)[:, None] * frequency[None, :]
     cosine = jnp.concatenate([jnp.cos(angles), jnp.cos(angles)], axis=-1)
@@ -169,7 +182,7 @@
                 whole((rows, HD)),
                 whole((1, HD)),
                 whole((1, HD)),
-                pl.BlockSpec((rows_step, length_cap, entry_width), lambda i, lens: (i, 0, 0)),
+                pl.BlockSpec((rows_step, length_cap, entry_width), lambda i, lens: (i + first_step, 0, 0)),
             ],
             out_specs=[whole((peers, rows, q_width)), whole((rows, entry_width))],
             scratch_shapes=[
@@ -183,28 +196,58 @@
             jax.ShapeDtypeStruct((peers, rows, q_width), BF16),
             jax.ShapeDtypeStruct((rows, entry_width), BF16),
         ],
-        compiler_params=pltpu.CompilerParams(vmem_limit_bytes=32 * 1024 * 1024),
+        compiler_params=pltpu.CompilerParams(vmem_limit_bytes=VMEM_BYTES),
         cost_estimate=pl.CostEstimate(
             flops=4 * rows * heads * HD * length_cap,
-            bytes_accessed=cache_kv.size * 2 + q_peers.size * 4,
+            bytes_accessed=rows * length_cap * entry_width * 2 + q_peers.size * 4,
             transcendentals=rows * heads * length_cap,
         ),
         name="attend",
     )(lengths, q_peers, kv_rows, cosine, sine, q_gain[None, :], k_gain[None, :], cache_kv)
 
 
-def place_kernel(lens_ref, arrive_ref, slot_ref, entry_ref, cache_ref, landed_ref, out_ref):
-    row = pl.program_id(0)
-    position = lax.broadcasted_iota(jnp.int32, out_ref.shape[1:], 0)
-    at_length = position == lens_ref[row]
-
-    @pl.when(arrive_ref[row] == 0)
-    def _():
-        out_ref[0] = jnp.where(at_length, entry_ref[0], cache_ref[0])
-
-    @pl.when(arrive_ref[row] != 0)
-    def _():
-        out_ref[0] = jnp.where(at_length, entry_ref[0], landed_ref[0])
+WINDOW = 16
+
+
+def place_kernel(
+    lens_ref, arrive_ref, slot_ref, entry_ref, cache_ref, landed_ref, out_ref,
+    rows_ref, in_sems, out_sems,
+):
+    rows = out_ref.shape[0]
+
+    def copy_in(row, source, source_row):
+        return pltpu.make_async_copy(source.at[source_row], rows_ref.at[row], in_sems.at[row])
+
+    def copy_out(row):
+        return pltpu.make_async_copy(rows_ref.at[row], out_ref.at[row], out_sems.at[row])
+
+    def begin(row, carry):
+        @pl.when(arrive_ref[row] == 0)
+        def _():
+            copy_in(row, cache_ref, row).start()
+
+        @pl.when(arrive_ref[row] != 0)
+        def _():
+            copy_in(row, landed_ref, slot_ref[row]).start()
+
+        return carry
+
+    def renew(row, carry):
+        copy_in(row, cache_ref, row).wait()
+        start = pl.multiple_of(lens_ref[row] // WINDOW * WINDOW, WINDOW)
+        window = rows_ref.at[row, pl.ds(start, WINDOW)]
+        position = lax.broadcasted_iota(jnp.int32, window.shape, 0) + start
+        window[...] = jnp.where(position == lens_ref[row], entry_ref[row], window[...])
+        copy_out(row).start()
+        return carry
+
+    def finish(row, carry):
+        copy_out(row).wait()
+        return carry
+
+    lax.fori_loop(0, rows, begin, 0)
+    lax.fori_loop(0, rows, renew, 0)
+    lax.fori_loop(0, rows, finish, 0)
 
 
 def place_cache(lengths, arriving, landed_slot, entries, cache_kv, landed):
@@ -213,16 +256,21 @@
         place_kernel,
         grid_spec=pltpu.PrefetchScalarGridSpec(
             num_scalar_prefetch=3,
-            grid=(rows,),
+            grid=(1,),
             in_specs=[
-                pl.BlockSpec((1, 1, entry_width), lambda i, a, b, c: (i, 0, 0)),
-                pl.BlockSpec((1, length_cap, entry_width), lambda i, a, b, c: (i, 0, 0)),
-                pl.BlockSpec((1, length_cap, entry_width), lambda i, a, b, c: (c[i], 0, 0)),
-            ],
-            out_specs=pl.BlockSpec((1, length_cap, entry_width), lambda i, a, b, c: (i, 0, 0)),
+                pl.BlockSpec((rows, 1, entry_width), lambda i, a, b, c: (0, 0, 0)),
+                pl.BlockSpec(memory_space=pl.ANY),
+                pl.BlockSpec(memory_space=pl.ANY),
+            ],
+            out_specs=pl.BlockSpec(memory_space=pl.ANY),
+            scratch_shapes=[
+                pltpu.VMEM((rows, length_cap, entry_width), BF16),
+                pltpu.SemaphoreType.DMA((rows,)),
+                pltpu.SemaphoreType.DMA((rows,)),
+            ],
         ),
         out_shape=jax.ShapeDtypeStruct(cache_kv.shape, BF16),
-        compiler_params=pltpu.CompilerParams(vmem_limit_bytes=16 * 1024 * 1024),
+        compiler_params=pltpu.CompilerParams(vmem_limit_bytes=VMEM_BYTES),
         cost_estimate=pl.CostEstimate(
             flops=0, bytes_accessed=cache_kv.size * 4, transcendentals=0
         ),
@@ -253,7 +301,7 @@
         out_shape=[
             jax.ShapeDtypeStruct((count,) + cache_kv.shape[1:], BF16) for k in range(shifts)
         ],
-        compiler_params=pltpu.CompilerParams(vmem_limit_bytes=16 * 1024 * 1024),
+        compiler_params=pltpu.CompilerParams(vmem_limit_bytes=VMEM_BYTES),
         cost_estimate=pl.CostEstimate(
             flops=0,
             bytes_accessed=4 * shifts * count * cache_kv.shape[1] * cache_kv.shape[2],
@@ -263,8 +311,110 @@
     )(slots, *([cache_kv] * shifts))
 
 
-def exchange(array):
-    return lax.all_to_all(array, "cuts", 0, 0, tiled=True, axis_index_groups=PLANES)
+def exchange(array, groups=PLANES):
+    return lax.all_to_all(array, "cuts", 0, 0, tiled=True, axis_index_groups=groups)
+
+
+def behind(array, *marks):
+    return lax.optimization_barrier((array, *marks))[0]
+
+
+def swap_cores(array):
+    return lax.ppermute(array, "inst", [(g, g ^ 1) for g in range(4)])
+
+
+def rows_kernel(places_ref, *refs, counts):
+    weights_ref, out_ref = refs[sum(counts)], refs[-1]
+    first = 0
+    for step, count in enumerate(counts):
+        pieces = refs[first : first + count]
+        first += count
+
+        @pl.when(pl.program_id(0) == step)
+        def _(pieces=pieces):
+            at = 0
+            for piece in pieces:
+                lines, rows, width = piece.shape
+                total = jnp.dot(
+                    piece[...].reshape(lines * rows, width),
+                    weights_ref[...],
+                    preferred_element_type=F32,
+                )
+                out_ref[0, at : at + lines * rows] = total.astype(BF16)
+                at += lines * rows
+
+
+def project_rows(places, groups, weights, into):
+    lines, rows, width = groups[0][0].shape
+    block = (1, sum(piece.shape[0] for piece in groups[0]) * rows, weights.shape[1])
+    pieces = [piece for group in groups for piece in group]
+    whole = lambda shape: pl.BlockSpec(shape, lambda i, places: (0,) * len(shape))
+    operands = [*pieces, weights]
+    in_specs = [whole(operand.shape) for operand in operands]
+    if into is not None:
+        operands.append(into)
+        in_specs.append(pl.BlockSpec(memory_space=pl.ANY))
+    return pl.pallas_call(
+        functools.partial(rows_kernel, counts=[len(group) for group in groups]),
+        grid_spec=pltpu.PrefetchScalarGridSpec(
+            num_scalar_prefetch=1,
+            grid=(len(groups),),
+            in_specs=in_specs,
+            out_specs=pl.BlockSpec(block, lambda i, places: (places[i], 0, 0)),
+        ),
+        out_shape=jax.ShapeDtypeStruct((SIDE,) + block[1:], BF16),
+        input_output_aliases={} if into is None else {len(operands): 0},
+        compiler_params=pltpu.CompilerParams(vmem_limit_bytes=VMEM_BYTES),
+        cost_estimate=pl.CostEstimate(
+            flops=2 * len(groups) * block[1] * width * block[2],
+            bytes_accessed=2 * (len(groups) * block[1] * width + weights.size),
+            transcendentals=0,
+        ),
+        name="project_rows",
+    )(places, *operands)
+
+
+def out_kernel(heads_ref, *refs):
+    out_ref = refs[-1]
+    pieces = (len(refs) - 1) // 2
+    steps = pl.num_programs(0)
+
+    def add_up(weights):
+        total = jnp.dot(heads_ref[0], weights[0][...], preferred_element_type=F32)
+        for piece in range(1, pieces):
+            total += jnp.dot(heads_ref[piece], weights[piece][...], preferred_element_type=F32)
+        out_ref[...] = total.astype(BF16)
+
+    @pl.when(pl.program_id(0) < steps // 2)
+    def _():
+        add_up(refs[:pieces])
+
+    @pl.when(pl.program_id(0) >= steps // 2)
+    def _():
+        add_up(refs[pieces : 2 * pieces])
+
+
+def project_out(heads, mine, other):
+    pieces, rows, depth = heads.shape
+    half = mine[0].shape[1]
+    tile = 512
+    steps = half // tile
+    first = [pl.BlockSpec((depth, tile), lambda i: (0, jnp.minimum(i, steps - 1)))] * pieces
+    second = [pl.BlockSpec((depth, tile), lambda i: (0, jnp.maximum(i - steps, 0)))] * pieces
+    return pl.pallas_call(
+        out_kernel,
+        grid=(2 * steps,),
+        in_specs=[pl.BlockSpec((pieces, rows, depth), lambda i: (0, 0, 0))] + first + second,
+        out_specs=pl.BlockSpec((rows, tile), lambda i: (0, i)),
+        out_shape=jax.ShapeDtypeStruct((rows, 2 * half), BF16),
+        compiler_params=pltpu.CompilerParams(vmem_limit_bytes=VMEM_BYTES),
+        cost_estimate=pl.CostEstimate(
+            flops=4 * rows * pieces * depth * half,
+            bytes_accessed=4 * pieces * depth * half,
+            transcendentals=0,
+        ),
+        name="project_out",
+    )(heads, *mine, *other)
 
 
 def body(
@@ -292,22 +442,71 @@
     group_id = lax.axis_index("inst")
     cut_id = lax.axis_index("cuts")
     low = cut_id % 2 == 0
+    at_x = (cut_id // 2) % SIDE
+    at_y = cut_id // (2 * SIDE)
     slot_ids = jnp.arange(local_rows, dtype=jnp.int32)
     own_rows = (group_id * cut_count + cut_id) * local_rows + slot_ids
-
-    w_query_pair = from_pair(w_query, 0)
-    w_keyval_pair = from_pair(w_keyval, 0)
-    w_out_pair = from_pair(w_out, 1)
-
-    normed = norm_rows(hidden.astype(F32), attn_gain.astype(F32)).astype(BF16)
-    plane_rows = exchange(jnp.broadcast_to(normed[None], (PLANE,) + normed.shape)).reshape(
-        PLANE * local_rows, width
-    )
 
     facts = jnp.stack([mig_source, cache_len]).astype(F32)
     all_facts = lax.all_to_all(
         jnp.broadcast_to(facts[None], (group_count,) + facts.shape), "inst", 0, 0, tiled=True
     )
+
+    w_keyval_pair = from_pair(w_keyval, 0)
+    first_core = group_id % 2 == 0
+    half_depth = width // 2
+    w_query_part = from_pair(
+        lax.dynamic_slice_in_dim(w_query, (group_id % 2) * half_depth, half_depth, 0), 0
+    )
+    w_query_rest = swap_cores(w_query_part)
+
+    normed = norm_rows(hidden.astype(F32), attn_gain.astype(F32)).astype(BF16)
+    half_rows = local_rows // 2
+    after, before = shift(normed, 0, SIDE - 1), shift(normed, 0, 1)
+    across = jnp.concatenate(
+        [shift(after[:half_rows], 0, SIDE - 1), shift(before[half_rows:], 0, 1)]
+    )
+    line = jnp.zeros((SIDE,) + normed.shape, BF16)
+    for offset, rows in enumerate((normed, after, across, before)):
+        line = lax.dynamic_update_slice(line, rows[None], ((at_x + offset) % SIDE, 0, 0))
+    half_line = SIDE // 2
+    after, before = shift(line, SIDE - 1, 0), shift(line, 1, 0)
+    across = [shift(after[:half_line], SIDE - 1, 0), shift(before[half_line:], 1, 0)]
+
+    half_width = width // 2
+    w_mine = lax.dynamic_slice_in_dim(w_out, (group_id % 2) * half_width, half_width, 1)
+    w_here = jnp.concatenate([w_mine, from_pair(w_mine, 1)])
+    depth = w_out.shape[0]
+    w_after, w_before = shift(w_here, 0, SIDE - 1), shift(w_here, 0, 1)
+
+    w_gate, w_up, w_here = lax.optimization_barrier((w_gate, w_up, w_here))
+    one_pair = from_pair(jnp.where(first_core, w_gate, w_up), 1)
+    w_down, w_query_rest = lax.optimization_barrier((w_down, w_query_rest))
+    w_down_pair = from_pair(w_down, 0)
+
+    w_query_pair = jnp.where(
+        first_core,
+        jnp.concatenate([w_query_part, w_query_rest]),
+        jnp.concatenate([w_query_rest, w_query_part]),
+    )
+    w_project = lax.optimization_barrier(
+        jnp.concatenate([w_query, w_query_pair, w_keyval, w_keyval_pair], axis=1)
+    )
+    q_width = 2 * w_query.shape[1]
+    kv_width = w_keyval.shape[1]
+
+    places = (at_y + jnp.arange(SIDE, dtype=jnp.int32)) % SIDE
+    spread = jnp.stack([places[0], places[1], places[3]])
+    projected = project_rows(spread, [[line], [after], [before]], w_project, None)
+    across = [behind(part, projected) for part in across]
+    projected = project_rows(places[2:3], [across], w_project, projected)
+    arrived = exchange(projected.reshape(PLANE, local_rows, -1))
+    w_after, w_before = behind(w_after, projected), behind(w_before, projected)
+    w_across = jnp.concatenate(
+        [shift(w_after[:depth], 0, SIDE - 1), shift(w_before[depth:], 0, 1)]
+    )
+    mine = [w_here, w_after, w_across, w_before]
+
     goes_to = all_facts[:, 0].astype(jnp.int32) == own_rows[None, :]
     lengths = jnp.sum(jnp.where(goes_to, all_facts[:, 1], 0.0), axis=0).astype(jnp.int32)
     targets = jnp.arange(group_count, dtype=jnp.int32)
@@ -338,11 +537,9 @@
     distance = (group_id - source_group) % group_count
     landed_slot = jnp.where(arriving, (distance - 1) * MIG + arrival_rank, 0)
 
-    w_project = jnp.concatenate([w_query, w_query_pair, w_keyval, w_keyval_pair], axis=1)
-    projected = jnp.dot(plane_rows, w_project, preferred_element_type=F32).astype(BF16)
-    arrived = exchange(projected.reshape(PLANE, local_rows, -1))
-    q_width = 2 * w_query.shape[1]
-    kv_width = w_keyval.shape[1]
+    other_pair = swap_cores(behind(one_pair, arrived))
+    other = [swap_cores(part) for part in mine]
+
     own_kv = arrived[:, :, q_width : q_width + kv_width]
     pair_kv = arrived[:, :, q_width + kv_width :]
     kv_rows = jnp.where(
@@ -351,29 +548,28 @@
         jnp.concatenate([pair_kv, own_kv], axis=2),
     )
     kv_rows = jnp.transpose(kv_rows, (1, 0, 2)).reshape(local_rows, -1)
-    attention, entries = attend(arrived, q_width, kv_rows, cache_kv, lengths, q_gain, k_gain)
-
-    w_gate, w_up, w_down, arrived_mark = lax.optimization_barrier(
-        (w_gate, w_up, w_down, w_project)
-    )
-    w_gate_pair = from_pair(w_gate, 0)
-    w_up_pair = from_pair(w_up, 1)
-
-    w_out_both = jnp.concatenate([w_out, w_out_pair])
-    attn_heads = exchange(attention).reshape(PLANE * local_rows, q_width)
-    attn_heads, w_gate_pair, w_up_pair, landed, w_down = lax.optimization_barrier(
-        (attn_heads, w_gate_pair, w_up_pair, landed, w_down)
-    )
-    w_down_pair = from_pair(w_down, 0)
-    partial_value = jnp.dot(attn_heads, w_out_both, preferred_element_type=F32).astype(BF16)
-    sums = exchange(partial_value.reshape(PLANE, local_rows, width))
+    attention, entries = attend(arrived, q_width, kv_rows, cache_kv, 0, lengths, q_gain, k_gain)
+
+    attention = attention.reshape(SIDE, SIDE, local_rows, q_width)
+    attention = lax.dynamic_slice_in_dim(
+        jnp.concatenate([attention, attention], axis=1), at_x, SIDE, 1
+    )
+    heads = exchange(attention, COLUMNS)
+    heads = behind(heads, one_pair, w_down_pair, *picked)
+    heads = jnp.transpose(heads, (1, 0, 2, 3)).reshape(SIDE, SIDE * local_rows, q_width)
+    partial_value = project_out(heads, mine, other)
+    sums = exchange(partial_value.reshape(SIDE, local_rows, width), COLUMNS)
 
     got_entries = lax.all_to_all(entries[send_slot], "inst", 0, 0, tiled=True)
     new_entries = jnp.where(arriving[:, None], got_entries[source_pick, arrival_rank], entries)
-    cache_next = place_cache(cache_len, arriving, landed_slot, new_entries, cache_kv, landed)
-    sums, cache_next, w_down_pair = lax.optimization_barrier((sums, cache_next, w_down_pair))
-
-    mixed_rows = hidden.astype(F32) + jnp.sum(sums.astype(F32), axis=0)
+    sums = behind(sums, new_entries, landed, other_pair)
+
+    attn_out = jnp.sum(sums.astype(F32), axis=0)
+    mine_out, other_out = attn_out[:, :half_width], attn_out[:, half_width:]
+    mixed_rows = hidden.astype(F32) + jnp.concatenate(
+        [jnp.where(first_core, mine_out, other_out), jnp.where(first_core, other_out, mine_out)],
+        axis=1,
+    )
     got_rows = lax.all_to_all(mixed_rows[send_slot], "inst", 0, 0, tiled=True)
     mixed_rows = jnp.where(arriving[:, None], got_rows[source_pick, arrival_rank], mixed_rows)
     moe_local = norm_rows(mixed_rows, moe_gain.astype(F32)).astype(BF16)
@@ -394,15 +590,21 @@
     match = match.reshape(PLANE * MOST, local_rows)
     slab = jnp.dot(match.astype(BF16), moe_local, preferred_element_type=F32).astype(BF16)
     slab_rows = exchange(slab.reshape(PLANE, MOST, width)).reshape(PLANE * MOST, width)
-
-    def expert_half(gate, up, down):
-        gate_part = jnp.dot(slab_rows, gate, preferred_element_type=F32)
-        upward = jnp.dot(slab_rows, up, preferred_element_type=F32)
+    cache_next = place_cache(cache_len, arriving, landed_slot, new_entries, cache_kv, landed)
+    slab_rows = behind(slab_rows, cache_next)
+
+    def expert_half(gate_part, upward, down):
         activation = (jax.nn.silu(gate_part) * upward).astype(BF16)
         return jnp.dot(activation, down, preferred_element_type=F32)
 
+    own_gate = jnp.dot(slab_rows, w_gate, preferred_element_type=F32)
+    own_up = jnp.dot(slab_rows, w_up, preferred_element_type=F32)
+    pair_one = jnp.dot(slab_rows, one_pair, preferred_element_type=F32)
+    pair_other = jnp.dot(slab_rows, other_pair, preferred_element_type=F32)
+    pair_gate = jnp.where(first_core, pair_one, pair_other)
+    pair_up = jnp.where(first_core, pair_other, pair_one)
     expert_out = (
-        expert_half(w_gate, w_up, w_down) + expert_half(w_gate_pair, w_up_pair, w_down_pair)
+        expert_half(own_gate, own_up, w_down) + expert_half(pair_gate, pair_up, w_down_pair)
     ).astype(BF16)
     returned = exchange(expert_out.reshape(PLANE, MOST, width)).reshape(PLANE * MOST, width)
     slot_gate = jnp.where(

time: 352 us -> 279 us (0.79)
  waiting for transfers between devices: 184 us -> 84.7 us
  Pallas kernels: 28.1 us -> 55 us
  blocking collectives: 17.7 us -> 0 us
  local copies, waits for them, and re-layouts: 22.6 us -> 37 us
  matrix products: 28.1 us -> 17.4 us
  starting transfers between devices: 52.4 us -> 60.2 us
  other arithmetic: 16.3 us -> 22 us
    ppermute x6 -> x5, waiting for transfers between devices: 102 us -> 9.94 us  [from_pair(): return lax.ppermute(array, ('inst', 'cuts'), pair_perm(side))]
    ppermute x0 -> x18, waiting for transfers between devices: none -> 44.1 us  [the longest x12 44.1 us: shift(): return lax.ppermute(array, 'cuts', moves)]
    ppermute x3, waiting for transfers between devices: 41.6 us -> 0.94 us  [body(): lax.ppermute(array, 'inst', [(g, (g + shift) % group_count) for g in rang...]
    pallas_call x0 -> x3, Pallas kernels: none -> 25.1 us  [the longest x2 13.9 us: project_rows(): pl.pallas_call(functools.partial(rows_kernel, counts=[len(group) for grou...]
    all_to_all x1 -> x0, blocking collectives: 17.7 us -> none  [exchange(): lax.all_to_all(array, 'cuts', 0, 0, tiled=True, axis_index_groups=PLANES)]
    ppermute x0 -> x18, starting transfers between devices: none -> 15.4 us  [the longest x12 14.4 us: shift(): return lax.ppermute(array, 'cuts', moves)]
    dot_general x4 -> x2, matrix products: 17.9 us -> 4.92 us  [the longest x1 2.46 us: body(): own_gate = jnp.dot(slab_rows, w_gate, preferred_element_type=F32)]
    slice x0 -> x7, local copies, waits for them, and re-layouts: none -> 8.42 us  [the longest x1 2.36 us: body(): w_before[depth:]]
  transfers between devices with their start and end apart: 17 -> 34, of which waited for: 8 -> 13; matrix products, arithmetic and copies ran while one was open for 9% -> 17% of each run, Pallas kernels for 8% -> 20%
where the time goes in v2:
time: 279 us; the launch traced here: 278 us
  waiting for transfers between devices  84.7 us (30%)
  starting transfers between devices  60.2 us (22%)
  Pallas kernels  55 us (20%)
  local copies, waits for them, and re-layouts  37 us (13%)
  other arithmetic  22 us (8%)
  matrix products  17.4 us (6%)
    ppermute x12, waiting for transfers between devices, shift(): return lax.ppermute(array, 'cuts', moves)  44.1 us
    all_to_all x5, waiting for transfers between devices, exchange(): lax.all_to_all(array, 'cuts', 0, 0, tiled=True, axis_index_groups=groups)  23.7 us
    all_to_all x5, starting transfers between devices, exchange(): lax.all_to_all(array, 'cuts', 0, 0, tiled=True, axis_index_groups=groups)  21.5 us
    pallas_call x1, Pallas kernels, attend(): pl.pallas_call(functools.partial(attend_kernel, rows_step=rows_step, kv_c...  18.2 us
    ppermute x12, starting transfers between devices, shift(): return lax.ppermute(array, 'cuts', moves)  14.4 us
    pallas_call x2, Pallas kernels, project_rows(): pl.pallas_call(functools.partial(rows_kernel, counts=[len(group) for grou...  13.9 us
    pallas_call x1, Pallas kernels, project_out(): pl.pallas_call(out_kernel, grid=(2 * steps,), in_specs=[pl.BlockSpec((pie...  11.2 us
    dot_general x2, matrix products, expert_half(): return jnp.dot(activation, down, preferred_element_type=F32)  11 us
  transfers between devices with their start and end apart: 34, of which 13 were waited for; matrix products, arithmetic and copies ran while one was open for 17% of the time, Pallas kernels for 20%

profile of v2, /device:TPU:0, one launch (start us, length us, event | category | flops | bytes accessed | tf_op | source)
XLA Modules:
  0.0 277.6 jit_solution(17705963270973878792)
XLA Ops:
  12.9 4.0 %collective-permute-start.11 = (bf16[256,2048]{1,0:T(8,128)(2,1)}, bf16[256,2048]{1,0:T(8,128)(2,1)}, u32[]{:S(2)}, u32[]{:S(2)}) collective-permute-start(bf16[256,2048]{1,0:T(8,128)(2,1)} %constant_dynamic-slice_fusion), channel_id=1, source_target_pairs={{0,65},{2,67},{4,69},{6,71},{8,73},{10,75},{12,77},{14,79},{16,81}... | collective-permute-start | bytes 3145736 | tf_op jit(solution)/shard_map/ppermute | solution.py:56
  17.5 3.2 %all-to-all-start = ((f32[4,2,32]{2,1,0:T(2,128)}), f32[4,2,32]{2,1,0:T(2,128)S(1)}, u32[]{:S(2)}, u32[]{:S(2)}) async-start(f32[4,2,32]{2,1,0:T(2,128)} %broadcast_in_dim.77), calls=%async_computation | async-start | bytes 8192 | tf_op jit(solution)/shard_map/all_to_all | solution.py:451
  22.6 3.3 %collective-permute-start.1 = (bf16[16,4096]{1,0:T(8,128)(2,1)S(1)}, bf16[16,4096]{1,0:T(8,128)(2,1)S(1)}, u32[]{:S(2)}, u32[]{:S(2)}) collective-permute-start(bf16[16,4096]{1,0:T(8,128)(2,1)S(1)} %slice.75), channel_id=1, source_target_pairs={{0,6},{1,7},{2,0},{3,1},{4,2},{5,3},{6,4},{7,5},{8,14},{9,15},{10,... | collective-permute-start | bytes 393224 | tf_op jit(solution)/shard_map/ppermute | solution.py:36
  29.3 3.5 %collective-permute-done.3 = bf16[16,4096]{1,0:T(8,128)(2,1)S(1)} collective-permute-done((bf16[16,4096]{1,0:T(8,128)(2,1)S(1)}, bf16[16,4096]{1,0:T(8,128)(2,1)S(1)}, u32[]{:S(2)}, u32[]{:S(2)}) %collective-permute-start.3) | collective-permute-done | bytes 131104 | tf_op jit(solution)/shard_map/ppermute | solution.py:36
  32.8 3.1 %collective-permute-start.4 = (bf16[4,32,4096]{2,1,0:T(8,128)(2,1)S(1)}, bf16[4,32,4096]{2,1,0:T(8,128)(2,1)S(1)}, u32[]{:S(2)}, u32[]{:S(2)}) collective-permute-start(bf16[4,32,4096]{2,1,0:T(8,128)(2,1)S(1)} %bitcast_dynamic-update-slice_fusion.refs_0_), channel_id=1, source_target_pairs={{0,24},{1,25},{2,26},{3,27},{4,28},{5,29},{6,30},{7,31},{8,0},{9,1... | collective-permute-start | bytes 3145736 | tf_op jit(solution)/shard_map/ppermute | solution.py:36
  35.9 3.6 %collective-permute-done.11 = bf16[256,2048]{1,0:T(8,128)(2,1)} collective-permute-done((bf16[256,2048]{1,0:T(8,128)(2,1)}, bf16[256,2048]{1,0:T(8,128)(2,1)}, u32[]{:S(2)}, u32[]{:S(2)}) %collective-permute-start.11) | collective-permute-done | bytes 1048608 | tf_op jit(solution)/shard_map/ppermute | solution.py:56
  41.4 3.0 %collective-permute-start.14 = (bf16[512,2048]{1,0:T(8,128)(2,1)S(1)}, bf16[512,2048]{1,0:T(8,128)(2,1)}, u32[]{:S(2)}, u32[]{:S(2)}) collective-permute-start(bf16[512,2048]{1,0:T(8,128)(2,1)S(1)} %pad_maximum_fusion.1.refs_0_), channel_id=1, source_target_pairs={{0,6},{1,7},{2,0},{3,1},{4,2},{5,3},{6,4},{7,5},{8,14},{9,15},{10,... | collective-permute-start | bytes 6291464 | tf_op jit(solution)/shard_map/ppermute | solution.py:36
  46.6 14.8 %collective-permute-done.6.refs_2_ = bf16[4,32,4096]{2,1,0:T(8,128)(2,1)S(1)} collective-permute-done((bf16[4,32,4096]{2,1,0:T(8,128)(2,1)S(1)}, bf16[4,32,4096]{2,1,0:T(8,128)(2,1)S(1)}, u32[]{:S(2)}, u32[]{:S(2)}) %collective-permute-start.6) | collective-permute-done | bytes 1048608 | tf_op jit(solution)/shard_map/ppermute | solution.py:36
  73.7 3.9 %collective-permute-done.10.refs_1_ = bf16[2,32,4096]{2,1,0:T(8,128)(2,1)} collective-permute-done((bf16[2,32,4096]{2,1,0:T(8,128)(2,1)}, bf16[2,32,4096]{2,1,0:T(8,128)(2,1)}, u32[]{:S(2)}, u32[]{:S(2)}) %collective-permute-start.10) | collective-permute-done | bytes 524320 | tf_op jit(solution)/shard_map/ppermute | solution.py:36
  77.7 4.0 %pad_maximum_fusion.refs_3_.refs_2_ = bf16[4096,576]{1,0:T(8,128)(2,1)} fusion(bf16[4096,32]{1,0:T(8,128)(2,1)S(1)} %copy-done.8, bf16[4096,32]{1,0:T(8,128)(2,1)S(1)} %copy.63, bf16[4096,256]{1,0:T(8,128)(2,1)S(1)} %maximum_select_fusion, bf16[4096,256]{1,0:T(8,128)(2,1)S(1)} %copy-done.5), kind=kLoop, calls=%fused_computation.5 | loop fusion | flops 18874368 | bytes 9437184 | tf_op jit(solution)/shard_map/concatenate | solution.py:493
  81.7 7.9 %project_rows.2.refs_3_ = bf16[4,128,576]{2,1,0:T(8,128)(2,1)} custom-call(s32[3]{0:T(128)} %pad_add_fusion.places_ref, bf16[4,32,4096]{2,1,0:T(8,128)(2,1)} %copy-done.7, bf16[4,32,4096]{2,1,0:T(8,128)(2,1)} %copy-done.9, bf16[4,32,4096]{2,1,0:T(8,128)(2,1)} %copy-done.10, bf16[4096,576]{1,0:T(8,128)(2,1)} %pad_maximum_fusion.refs_3_.refs_2_), custom_call_target="tpu_custom_call" | custom-call | flops 1811939328 | bytes 7864320 | tf_op jit(solution)/shard_map/project_rows/pallas_call | solution.py:357
  90.3 6.0 %project_rows.3 = bf16[4,128,576]{2,1,0:T(8,128)(2,1)} custom-call(s32[1]{0:T(128)} %get-tuple-element.60.places_ref, bf16[2,32,4096]{2,1,0:T(8,128)(2,1)} %copy-done.13, bf16[2,32,4096]{2,1,0:T(8,128)(2,1)} %collective-permute-done.10.refs_1_, bf16[4096,576]{1,0:T(8,128)(2,1)} %pad_maximum_fusion.refs_3_.refs_2_, ...), custom_call_target="tpu_custom_call", output_to_operand_aliasing={{}: (4, {})} | custom-call | flops 603979776 | bytes 5767168 | tf_op jit(solution)/shard_map/project_rows/pallas_call | solution.py:357
  104.5 4.9 %all-to-all-start.1 = ((bf16[16,32,576]{2,1,0:T(8,128)(2,1)}), bf16[16,32,576]{2,1,0:T(8,128)(2,1)S(1)}, u32[]{:S(2)}, u32[]{:S(2)}) async-start(bf16[16,32,576]{2,1,0:T(8,128)(2,1)} %bitcast.8), calls=%async_computation.1 | async-start | bytes 1310720 | tf_op jit(solution)/shard_map/all_to_all | solution.py:315
  109.6 15.4 %collective-permute-done.15 = bf16[256,2048]{1,0:T(8,128)(2,1)} collective-permute-done((bf16[256,2048]{1,0:T(8,128)(2,1)}, bf16[256,2048]{1,0:T(8,128)(2,1)}, u32[]{:S(2)}, u32[]{:S(2)}) %collective-permute-start.15) | collective-permute-done | bytes 1048608 | tf_op jit(solution)/shard_map/ppermute | solution.py:36
  127.4 4.1 %collective-permute-done.17 = bf16[256,2048]{1,0:T(8,128)(2,1)} collective-permute-done((bf16[256,2048]{1,0:T(8,128)(2,1)}, bf16[256,2048]{1,0:T(8,128)(2,1)}, u32[]{:S(2)}, u32[]{:S(2)}) %collective-permute-start.17) | collective-permute-done | bytes 1048608 | tf_op jit(solution)/shard_map/ppermute | solution.py:36
  137.1 18.2 %attend.1 = (bf16[16,32,512]{2,1,0:T(8,128)(2,1)}, bf16[32,1024]{1,0:T(8,128)(2,1)}) custom-call(s32[32]{0:T(128)} %get-tuple-element.58.lens_ref, bf16[16,32,576]{2,1,0:T(8,128)(2,1)} %copy-done.6, bf16[32,1024]{1,0:T(8,128)(2,1)} %reshape.213.kv_ref, f32[32,128]{1,0:T(8,128)} %get-tuple-element.61.cos_ref, f32[32,128]{1,0:T(8,128)} %get-tuple-element.62.sin_ref, ...), custom_call_target="tpu_custom_call" | custom-call | flops 134217728 | bytes 9568256 | tf_op jit(solution)/shard_map/attend/pallas_call | solution.py:171
  157.4 3.5 %all-to-all-start.2 = ((bf16[4,4,32,512]{3,2,1,0:T(8,128)(2,1)}), bf16[4,4,32,512]{3,2,1,0:T(8,128)(2,1)S(1)}, u32[]{:S(2)}, u32[]{:S(2)}) async-start(bf16[4,4,32,512]{3,2,1,0:T(8,128)(2,1)} %fusion.7), calls=%async_computation.2 | async-start | bytes 1048576 | tf_op jit(solution)/shard_map/all_to_all | solution.py:315
  162.2 3.2 %pick_caches.1 = (bf16[2,128,1024]{2,1,0:T(8,128)(2,1)}, bf16[2,128,1024]{2,1,0:T(8,128)(2,1)}, bf16[2,128,1024]{2,1,0:T(8,128)(2,1)}) custom-call(s32[3,2]{1,0:T(4,128)} %gather_fusion, bf16[32,128,1024]{2,1,0:T(8,128)(2,1)} %cache_ref.3, bf16[32,128,1024]{2,1,0:T(8,128)(2,1)} %cache_ref.3, bf16[32,128,1024]{2,1,0:T(8,128)(2,1)} %cache_ref.3), custom_call_target="tpu_custom_call" | custom-call | bytes 3145728 | tf_op jit(solution)/shard_map/pick_caches/pallas_call | solution.py:290
  165.6 6.3 %collective-permute-done.13 = bf16[384,4096]{1,0:T(8,128)(2,1)} collective-permute-done((bf16[384,4096]{1,0:T(8,128)(2,1)}, bf16[384,4096]{1,0:T(8,128)(2,1)}, u32[]{:S(2)}, u32[]{:S(2)}) %collective-permute-start.13) | collective-permute-done | bytes 3145760 | tf_op jit(solution)/shard_map/ppermute | solution.py:56
  173.1 4.5 %all-to-all-start.4 = ((bf16[4,2,1024]{2,1,0:T(2,128)(2,1)}), bf16[4,2,1024]{2,1,0:T(2,128)(2,1)S(1)}, u32[]{:S(2)}, u32[]{:S(2)}) async-start(bf16[4,2,1024]{2,1,0:T(2,128)(2,1)} %reshape.229), calls=%async_computation.4 | async-start | bytes 32768 | tf_op jit(solution)/shard_map/all_to_all | solution.py:563
  178.5 3.5 %collective-permute-start.23 = (bf16[2,128,1024]{2,1,0:T(8,128)(2,1)}, bf16[2,128,1024]{2,1,0:T(8,128)(2,1)S(1)}, u32[]{:S(2)}, u32[]{:S(2)}) collective-permute-start(bf16[2,128,1024]{2,1,0:T(8,128)(2,1)} %get-tuple-element.28), channel_id=1, source_target_pairs={{0,64},{32,96},{64,0},{96,32},{1,65},{33,97},{65,1},{97,33},{2,66}... | collective-permute-start | bytes 1572872 | tf_op jit(solution)/shard_map/ppermute | solution.py:531
  182.0 11.2 %project_out.1 = bf16[128,4096]{1,0:T(8,128)(2,1)} custom-call(bf16[4,128,512]{2,1,0:T(8,128)(2,1)} %bitcast.68, bf16[512,2048]{1,0:T(8,128)(2,1)} %copy-done.4, bf16[512,2048]{1,0:T(8,128)(2,1)} %collective-permute-done.14.refs_1_, bf16[512,2048]{1,0:T(8,128)(2,1)} %constant_dynamic-update-slice_fusion.refs_2_, ...), custom_call_target="tpu_custom_call" | custom-call | flops 2147483648 | bytes 16777216 | tf_op jit(solution)/shard_map/project_out/pallas_call | solution.py:404
  193.3 3.5 %all-to-all-start.3 = ((bf16[4,32,4096]{2,1,0:T(8,128)(2,1)}), bf16[4,32,4096]{2,1,0:T(8,128)(2,1)S(1)}, u32[]{:S(2)}, u32[]{:S(2)}) async-start(bf16[4,32,4096]{2,1,0:T(8,128)(2,1)} %bitcast.67), calls=%async_computation.3 | async-start | bytes 2097152 | tf_op jit(solution)/shard_map/all_to_all | solution.py:315
  201.1 11.7 %all-to-all-done.3 = bf16[4,32,4096]{2,1,0:T(8,128)(2,1)S(1)} async-done(((bf16[4,32,4096]{2,1,0:T(8,128)(2,1)}), bf16[4,32,4096]{2,1,0:T(8,128)(2,1)S(1)}, u32[]{:S(2)}, u32[]{:S(2)}) %all-to-all-start.3) | async-done | bytes 1048608 | tf_op jit(solution)/shard_map/all_to_all | solution.py:315
  214.4 3.3 %all-to-all-start.5 = ((f32[4,2,4096]{2,1,0:T(2,128)}), f32[4,2,4096]{2,1,0:T(2,128)S(1)}, u32[]{:S(2)}, u32[]{:S(2)}) async-start(f32[4,2,4096]{2,1,0:T(2,128)} %reshape.243), calls=%async_computation.5 | async-start | bytes 262144 | tf_op jit(solution)/shard_map/all_to_all | solution.py:573
  217.9 6.0 %all-to-all-done.5 = f32[4,2,4096]{2,1,0:T(2,128)S(1)} async-done(((f32[4,2,4096]{2,1,0:T(2,128)}), f32[4,2,4096]{2,1,0:T(2,128)S(1)}, u32[]{:S(2)}, u32[]{:S(2)}) %all-to-all-start.5) | async-done | bytes 131104 | tf_op jit(solution)/shard_map/all_to_all | solution.py:573
  226.9 3.9 %all-to-all-start.6 = ((bf16[16,4,4096]{2,1,0:T(4,128)(2,1)}), bf16[16,4,4096]{2,1,0:T(4,128)(2,1)S(1)}, u32[]{:S(2)}, u32[]{:S(2)}) async-start(bf16[16,4,4096]{2,1,0:T(4,128)(2,1)} %reshape.217), calls=%async_computation.6 | async-start | bytes 1048576 | tf_op jit(solution)/shard_map/all_to_all | solution.py:315
  232.1 8.5 %place_cache.1 = bf16[32,128,1024]{2,1,0:T(8,128)(2,1)} custom-call(s32[32]{0:T(128)} %lens_ref.1, s32[32]{0:T(128)} %get-tuple-element.38.arrive_ref, s32[32]{0:T(128)} %fusion.34.slot_ref, bf16[32,1,1024]{2,1,0:T(2,128)(2,1)} %copy.69.entry_ref, bf16[32,128,1024]{2,1,0:T(8,128)(2,1)} %cache_ref.3, ...), custom_call_target="tpu_custom_call" | custom-call | bytes 16777216 | tf_op jit(solution)/shard_map/place_cache/pallas_call | solution.py:255
  246.9 5.4 %fusion.18 = f32[64,4096]{1,0:T(8,128)} fusion(bf16[384,4096]{1,0:T(8,128)(2,1)} %collective-permute-done.13, f32[64,384]{1,0:T(8,128)S(1)} %fusion.57, pred[]{:T(512)S(6)} %eq.100, bf16[64,4096]{1,0:T(8,128)(2,1)S(1)} %reshape.218, bf16[4096,384]{1,0:T(8,128)(2,1)} %collective-permute-done.25), kind=kOutput, calls=%fused_computation.51 | convolution fusion | flops 402849792 | bytes 7962625 | tf_op jit(solution)/shard_map/dot_general | solution.py:598
  252.3 5.5 %fusion = bf16[64,4096]{1,0:T(8,128)(2,1)} fusion(f32[64,4096]{1,0:T(8,128)} %fusion.18, bf16[384,4096]{1,0:T(8,128)(2,1)} %param.31, bf16[64,4096]{1,0:T(8,128)(2,1)S(1)} %reshape.218, bf16[4096,384]{1,0:T(8,128)(2,1)} %param.30, f32[64,384]{1,0:T(8,128)S(1)} %fusion.56), kind=kOutput, calls=%fused_computation.7 | convolution fusion | flops 403324928 | bytes 8486912 | tf_op jit(solution)/shard_map/dot_general | solution.py:598
  259.9 5.8 %all-to-all-start.7 = ((bf16[16,4,4096]{2,1,0:T(4,128)(2,1)}), bf16[16,4,4096]{2,1,0:T(4,128)(2,1)S(1)}, u32[]{:S(2)}, u32[]{:S(2)}) async-start(bf16[16,4,4096]{2,1,0:T(4,128)(2,1)} %reshape.219), calls=%async_computation.7 | async-start | bytes 1048576 | tf_op jit(solution)/shard_map/all_to_all | solution.py:315
  265.7 10.7 %all-to-all-done.7 = bf16[16,4,4096]{2,1,0:T(4,128)(2,1)S(1)} async-done(((bf16[16,4,4096]{2,1,0:T(4,128)(2,1)}), bf16[16,4,4096]{2,1,0:T(4,128)(2,1)S(1)}, u32[]{:S(2)}, u32[]{:S(2)}) %all-to-all-start.7) | async-done | bytes 524320 | tf_op jit(solution)/shard_map/all_to_all | solution.py:315
  (181 shorter events, 76.6 us)
Async XLA Ops:
  4.6 16.9 %collective-permute-start = (bf16[32,4096]{1,0:T(8,128)(2,1)}, bf16[32,4096]{1,0:T(8,128)(2,1)}, u32[]{:S(2)}, u32[]{:S(2)}) collective-permute-start(bf16[32,4096]{1,0:T(8,128)(2,1)} %get-tuple-element.47), channel_id=1, source_target_pairs={{0,6},{1,7},{2,0},{3,1},{4,2},{5,3},{6,4},{7,5},{8,14},{9,15},{10,... | collective-permute-start | bytes 786440 | tf_op jit(solution)/shard_map/ppermute | solution.py:36
  7.5 18.4 %collective-permute-start.2 = (bf16[32,4096]{1,0:T(8,128)(2,1)}, bf16[32,4096]{1,0:T(8,128)(2,1)S(1)}, u32[]{:S(2)}, u32[]{:S(2)}) collective-permute-start(bf16[32,4096]{1,0:T(8,128)(2,1)} %get-tuple-element.47), channel_id=1, source_target_pairs={{0,2},{1,3},{2,4},{3,5},{4,6},{5,7},{6,0},{7,1},{8,10},{9,11},{10,... | collective-permute-start | bytes 786440 | tf_op jit(solution)/shard_map/ppermute | solution.py:36
  9.7 34.7 %collective-permute-start.7 = (bf16[2048,256]{1,0:T(8,128)(2,1)}, bf16[2048,256]{1,0:T(8,128)(2,1)}, u32[]{:S(2)}, u32[]{:S(2)}) collective-permute-start(bf16[2048,256]{1,0:T(8,128)(2,1)} %constant_dynamic-slice_fusion.1), channel_id=1, source_target_pairs={{0,1},{2,3},{4,5},{6,7},{8,9},{10,11},{12,13},{14,15},{16,17},{18,... | collective-permute-start | bytes 3145736 | tf_op jit(solution)/shard_map/ppermute | solution.py:56
  11.6 32.7 %collective-permute-start.9 = (bf16[4096,32]{0,1:T(8,128)(2,1)}, bf16[4096,32]{0,1:T(8,128)(2,1)}, u32[]{:S(2)}, u32[]{:S(2)}) collective-permute-start(bf16[4096,32]{0,1:T(8,128)(2,1)} %param.24), channel_id=1, source_target_pairs={{0,1},{2,3},{4,5},{6,7},{8,9},{10,11},{12,13},{14,15},{16,17},{18,... | collective-permute-start | bytes 786440 | tf_op jit(solution)/shard_map/ppermute | solution.py:56
  12.9 26.7 %collective-permute-start.11 = (bf16[256,2048]{1,0:T(8,128)(2,1)}, bf16[256,2048]{1,0:T(8,128)(2,1)}, u32[]{:S(2)}, u32[]{:S(2)}) collective-permute-start(bf16[256,2048]{1,0:T(8,128)(2,1)} %constant_dynamic-slice_fusion), channel_id=1, source_target_pairs={{0,65},{2,67},{4,69},{6,71},{8,73},{10,75},{12,77},{14,79},{16,81}... | collective-permute-start | bytes 3145736 | tf_op jit(solution)/shard_map/ppermute | solution.py:56
  17.5 86.9 %all-to-all-start = ((f32[4,2,32]{2,1,0:T(2,128)}), f32[4,2,32]{2,1,0:T(2,128)S(1)}, u32[]{:S(2)}, u32[]{:S(2)}) async-start(f32[4,2,32]{2,1,0:T(2,128)} %broadcast_in_dim.77), calls=%async_computation | async-start | bytes 8192 | tf_op jit(solution)/shard_map/all_to_all | solution.py:451
  32.8 31.8 %collective-permute-start.4 = (bf16[4,32,4096]{2,1,0:T(8,128)(2,1)S(1)}, bf16[4,32,4096]{2,1,0:T(8,128)(2,1)S(1)}, u32[]{:S(2)}, u32[]{:S(2)}) collective-permute-start(bf16[4,32,4096]{2,1,0:T(8,128)(2,1)S(1)} %bitcast_dynamic-update-slice_fusion.refs_0_), channel_id=1, source_target_pairs={{0,24},{1,25},{2,26},{3,27},{4,28},{5,29},{6,30},{7,31},{8,0},{9,1... | collective-permute-start | bytes 3145736 | tf_op jit(solution)/shard_map/ppermute | solution.py:36
  35.9 25.5 %collective-permute-start.6 = (bf16[4,32,4096]{2,1,0:T(8,128)(2,1)S(1)}, bf16[4,32,4096]{2,1,0:T(8,128)(2,1)S(1)}, u32[]{:S(2)}, u32[]{:S(2)}) collective-permute-start(bf16[4,32,4096]{2,1,0:T(8,128)(2,1)S(1)} %bitcast_dynamic-update-slice_fusion.refs_0_), channel_id=1, source_target_pairs={{0,8},{1,9},{2,10},{3,11},{4,12},{5,13},{6,14},{7,15},{8,16},{9,17... | collective-permute-start | bytes 3145736 | tf_op jit(solution)/shard_map/ppermute | solution.py:36
  41.4 55.0 %collective-permute-start.14 = (bf16[512,2048]{1,0:T(8,128)(2,1)S(1)}, bf16[512,2048]{1,0:T(8,128)(2,1)}, u32[]{:S(2)}, u32[]{:S(2)}) collective-permute-start(bf16[512,2048]{1,0:T(8,128)(2,1)S(1)} %pad_maximum_fusion.1.refs_0_), channel_id=1, source_target_pairs={{0,6},{1,7},{2,0},{3,1},{4,2},{5,3},{6,4},{7,5},{8,14},{9,15},{10,... | collective-permute-start | bytes 6291464 | tf_op jit(solution)/shard_map/ppermute | solution.py:36
  44.4 55.1 %collective-permute-start.16 = (bf16[512,2048]{1,0:T(8,128)(2,1)S(1)}, bf16[512,2048]{1,0:T(8,128)(2,1)}, u32[]{:S(2)}, u32[]{:S(2)}) collective-permute-start(bf16[512,2048]{1,0:T(8,128)(2,1)S(1)} %pad_maximum_fusion.1.refs_0_), channel_id=1, source_target_pairs={{0,2},{1,3},{2,4},{3,5},{4,6},{5,7},{6,0},{7,1},{8,10},{9,11},{10,... | collective-permute-start | bytes 6291464 | tf_op jit(solution)/shard_map/ppermute | solution.py:36
  44.4 26.4 %collective-permute-start.8 = (bf16[2048,256]{1,0:T(8,128)(2,1)}, bf16[2048,256]{1,0:T(8,128)(2,1)}, u32[]{:S(2)}, u32[]{:S(2)}) collective-permute-start(bf16[2048,256]{1,0:T(8,128)(2,1)} %collective-permute-done.7), channel_id=1, source_target_pairs={{0,32},{32,0},{64,96},{96,64},{1,33},{33,1},{65,97},{97,65},{2,34}... | collective-permute-start | bytes 3145736 | tf_op jit(solution)/shard_map/ppermute | solution.py:323
  61.4 72.4 %collective-permute-start.12 = (bf16[4096,384]{1,0:T(8,128)(2,1)}, bf16[4096,384]{1,0:T(8,128)(2,1)}, u32[]{:S(2)}, u32[]{:S(2)}) collective-permute-start(bf16[4096,384]{1,0:T(8,128)(2,1)} %broadcast_select_fusion), channel_id=1, source_target_pairs={{0,65},{2,67},{4,69},{6,71},{8,73},{10,75},{12,77},{14,79},{16,81}... | collective-permute-start | bytes 9437192 | tf_op jit(solution)/shard_map/ppermute | solution.py:56
  64.6 13.1 %collective-permute-start.10 = (bf16[2,32,4096]{2,1,0:T(8,128)(2,1)}, bf16[2,32,4096]{2,1,0:T(8,128)(2,1)}, u32[]{:S(2)}, u32[]{:S(2)}) collective-permute-start(bf16[2,32,4096]{2,1,0:T(8,128)(2,1)} %slice.78), channel_id=1, source_target_pairs={{0,8},{1,9},{2,10},{3,11},{4,12},{5,13},{6,14},{7,15},{8,16},{9,17... | collective-permute-start | bytes 1572872 | tf_op jit(solution)/shard_map/ppermute | solution.py:36
  70.8 63.5 %collective-permute-start.18 = (bf16[512,2048]{1,0:T(8,128)(2,1)S(1)}, bf16[512,2048]{1,0:T(8,128)(2,1)}, u32[]{:S(2)}, u32[]{:S(2)}) collective-permute-start(bf16[512,2048]{1,0:T(8,128)(2,1)S(1)} %pad_maximum_fusion.1.refs_0_), channel_id=1, source_target_pairs={{0,32},{32,0},{64,96},{96,64},{1,33},{33,1},{65,97},{97,65},{2,34}... | collective-permute-start | bytes 6291464 | tf_op jit(solution)/shard_map/ppermute | solution.py:323
  77.7 11.8 %collective-permute-start.5 = (bf16[2,32,4096]{2,1,0:T(8,128)(2,1)S(1)}, bf16[2,32,4096]{2,1,0:T(8,128)(2,1)S(1)}, u32[]{:S(2)}, u32[]{:S(2)}) collective-permute-start(bf16[2,32,4096]{2,1,0:T(8,128)(2,1)S(1)} %slice.77), channel_id=1, source_target_pairs={{0,24},{1,25},{2,26},{3,27},{4,28},{5,29},{6,30},{7,31},{8,0},{9,1... | collective-permute-start | bytes 1572872 | tf_op jit(solution)/shard_map/ppermute | solution.py:36
  98.6 26.4 %collective-permute-start.15 = (bf16[256,2048]{1,0:T(8,128)(2,1)}, bf16[256,2048]{1,0:T(8,128)(2,1)}, u32[]{:S(2)}, u32[]{:S(2)}) collective-permute-start(bf16[256,2048]{1,0:T(8,128)(2,1)} %slice.59), channel_id=1, source_target_pairs={{0,6},{1,7},{2,0},{3,1},{4,2},{5,3},{6,4},{7,5},{8,14},{9,15},{10,... | collective-permute-start | bytes 3145736 | tf_op jit(solution)/shard_map/ppermute | solution.py:36
  101.9 29.6 %collective-permute-start.17 = (bf16[256,2048]{1,0:T(8,128)(2,1)}, bf16[256,2048]{1,0:T(8,128)(2,1)}, u32[]{:S(2)}, u32[]{:S(2)}) collective-permute-start(bf16[256,2048]{1,0:T(8,128)(2,1)} %slice.60), channel_id=1, source_target_pairs={{0,2},{1,3},{2,4},{3,5},{4,6},{5,7},{6,0},{7,1},{8,10},{9,11},{10,... | collective-permute-start | bytes 3145736 | tf_op jit(solution)/shard_map/ppermute | solution.py:36
  103.3 68.6 %collective-permute-start.13 = (bf16[384,4096]{1,0:T(8,128)(2,1)}, bf16[384,4096]{1,0:T(8,128)(2,1)}, u32[]{:S(2)}, u32[]{:S(2)}) collective-permute-start(bf16[384,4096]{1,0:T(8,128)(2,1)} %param.31), channel_id=1, source_target_pairs={{0,1},{2,3},{4,5},{6,7},{8,9},{10,11},{12,13},{14,15},{16,17},{18,... | collective-permute-start | bytes 9437192 | tf_op jit(solution)/shard_map/ppermute | solution.py:56
  104.5 29.8 %all-to-all-start.1 = ((bf16[16,32,576]{2,1,0:T(8,128)(2,1)}), bf16[16,32,576]{2,1,0:T(8,128)(2,1)S(1)}, u32[]{:S(2)}, u32[]{:S(2)}) async-start(bf16[16,32,576]{2,1,0:T(8,128)(2,1)} %bitcast.8), calls=%async_computation.1 | async-start | bytes 1310720 | tf_op jit(solution)/shard_map/all_to_all | solution.py:315
  125.1 53.4 %collective-permute-start.19 = (bf16[512,2048]{1,0:T(8,128)(2,1)}, bf16[512,2048]{1,0:T(8,128)(2,1)}, u32[]{:S(2)}, u32[]{:S(2)}) collective-permute-start(bf16[512,2048]{1,0:T(8,128)(2,1)} %collective-permute-done.14.refs_1_), channel_id=1, source_target_pairs={{0,32},{32,0},{64,96},{96,64},{1,33},{33,1},{65,97},{97,65},{2,34}... | collective-permute-start | bytes 6291464 | tf_op jit(solution)/shard_map/ppermute | solution.py:323
  131.5 50.6 %collective-permute-start.21 = (bf16[512,2048]{1,0:T(8,128)(2,1)}, bf16[512,2048]{1,0:T(8,128)(2,1)}, u32[]{:S(2)}, u32[]{:S(2)}) collective-permute-start(bf16[512,2048]{1,0:T(8,128)(2,1)} %collective-permute-done.16.refs_3_), channel_id=1, source_target_pairs={{0,32},{32,0},{64,96},{96,64},{1,33},{33,1},{65,97},{97,65},{2,34}... | collective-permute-start | bytes 6291464 | tf_op jit(solution)/shard_map/ppermute | solution.py:323
  133.8 48.3 %collective-permute-start.20 = (bf16[512,2048]{1,0:T(8,128)(2,1)}, bf16[512,2048]{1,0:T(8,128)(2,1)}, u32[]{:S(2)}, u32[]{:S(2)}) collective-permute-start(bf16[512,2048]{1,0:T(8,128)(2,1)} %constant_dynamic-update-slice_fusion.refs_2_), channel_id=1, source_target_pairs={{0,32},{32,0},{64,96},{96,64},{1,33},{33,1},{65,97},{97,65},{2,34}... | collective-permute-start | bytes 6291464 | tf_op jit(solution)/shard_map/ppermute | solution.py:323
  134.3 78.5 %collective-permute-start.25 = (bf16[4096,384]{1,0:T(8,128)(2,1)}, bf16[4096,384]{1,0:T(8,128)(2,1)}, u32[]{:S(2)}, u32[]{:S(2)}) collective-permute-start(bf16[4096,384]{1,0:T(8,128)(2,1)} %collective-permute-done.12), channel_id=1, source_target_pairs={{0,32},{32,0},{64,96},{96,64},{1,33},{33,1},{65,97},{97,65},{2,34}... | collective-permute-start | bytes 9437192 | tf_op jit(solution)/shard_map/ppermute | solution.py:323
  157.4 15.8 %all-to-all-start.2 = ((bf16[4,4,32,512]{3,2,1,0:T(8,128)(2,1)}), bf16[4,4,32,512]{3,2,1,0:T(8,128)(2,1)S(1)}, u32[]{:S(2)}, u32[]{:S(2)}) async-start(bf16[4,4,32,512]{3,2,1,0:T(8,128)(2,1)} %fusion.7), calls=%async_computation.2 | async-start | bytes 1048576 | tf_op jit(solution)/shard_map/all_to_all | solution.py:315
  171.9 24.9 %collective-permute-start.22 = (bf16[2,128,1024]{2,1,0:T(8,128)(2,1)}, bf16[2,128,1024]{2,1,0:T(8,128)(2,1)S(1)}, u32[]{:S(2)}, u32[]{:S(2)}) collective-permute-start(bf16[2,128,1024]{2,1,0:T(8,128)(2,1)} %get-tuple-element.27), channel_id=1, source_target_pairs={{0,32},{32,64},{64,96},{96,0},{1,33},{33,65},{65,97},{97,1},{2,34}... | collective-permute-start | bytes 1572872 | tf_op jit(solution)/shard_map/ppermute | solution.py:531
  173.1 20.1 %all-to-all-start.4 = ((bf16[4,2,1024]{2,1,0:T(2,128)(2,1)}), bf16[4,2,1024]{2,1,0:T(2,128)(2,1)S(1)}, u32[]{:S(2)}, u32[]{:S(2)}) async-start(bf16[4,2,1024]{2,1,0:T(2,128)(2,1)} %reshape.229), calls=%async_computation.4 | async-start | bytes 32768 | tf_op jit(solution)/shard_map/all_to_all | solution.py:563
  178.5 19.2 %collective-permute-start.23 = (bf16[2,128,1024]{2,1,0:T(8,128)(2,1)}, bf16[2,128,1024]{2,1,0:T(8,128)(2,1)S(1)}, u32[]{:S(2)}, u32[]{:S(2)}) collective-permute-start(bf16[2,128,1024]{2,1,0:T(8,128)(2,1)} %get-tuple-element.28), channel_id=1, source_target_pairs={{0,64},{32,96},{64,0},{96,32},{1,65},{33,97},{65,1},{97,33},{2,66}... | collective-permute-start | bytes 1572872 | tf_op jit(solution)/shard_map/ppermute | solution.py:531
  182.0 17.4 %collective-permute-start.24 = (bf16[2,128,1024]{2,1,0:T(8,128)(2,1)}, bf16[2,128,1024]{2,1,0:T(8,128)(2,1)S(1)}, u32[]{:S(2)}, u32[]{:S(2)}) collective-permute-start(bf16[2,128,1024]{2,1,0:T(8,128)(2,1)} %get-tuple-element.29), channel_id=1, source_target_pairs={{0,96},{32,0},{64,32},{96,64},{1,97},{33,1},{65,33},{97,65},{2,98}... | collective-permute-start | bytes 1572872 | tf_op jit(solution)/shard_map/ppermute | solution.py:531
  193.3 19.5 %all-to-all-start.3 = ((bf16[4,32,4096]{2,1,0:T(8,128)(2,1)}), bf16[4,32,4096]{2,1,0:T(8,128)(2,1)S(1)}, u32[]{:S(2)}, u32[]{:S(2)}) async-start(bf16[4,32,4096]{2,1,0:T(8,128)(2,1)} %bitcast.67), calls=%async_computation.3 | async-start | bytes 2097152 | tf_op jit(solution)/shard_map/all_to_all | solution.py:315
  214.4 9.4 %all-to-all-start.5 = ((f32[4,2,4096]{2,1,0:T(2,128)}), f32[4,2,4096]{2,1,0:T(2,128)S(1)}, u32[]{:S(2)}, u32[]{:S(2)}) async-start(f32[4,2,4096]{2,1,0:T(2,128)} %reshape.243), calls=%async_computation.5 | async-start | bytes 262144 | tf_op jit(solution)/shard_map/all_to_all | solution.py:573
  226.9 15.0 %all-to-all-start.6 = ((bf16[16,4,4096]{2,1,0:T(4,128)(2,1)}), bf16[16,4,4096]{2,1,0:T(4,128)(2,1)S(1)}, u32[]{:S(2)}, u32[]{:S(2)}) async-start(bf16[16,4,4096]{2,1,0:T(4,128)(2,1)} %reshape.217), calls=%async_computation.6 | async-start | bytes 1048576 | tf_op jit(solution)/shard_map/all_to_all | solution.py:315
  259.9 16.5 %all-to-all-start.7 = ((bf16[16,4,4096]{2,1,0:T(4,128)(2,1)}), bf16[16,4,4096]{2,1,0:T(4,128)(2,1)S(1)}, u32[]{:S(2)}, u32[]{:S(2)}) async-start(bf16[16,4,4096]{2,1,0:T(4,128)(2,1)} %reshape.219), calls=%async_computation.7 | async-start | bytes 1048576 | tf_op jit(solution)/shard_map/all_to_all | solution.py:315
  (22 other events, 302.5 us)

commit v3 on v2

v3 whole, which is shorter than its diff:
```python
import functools
import jax
import jax.numpy as jnp
from jax import lax
from jax.experimental import pallas as pl
from jax.experimental.pallas import tpu as pltpu
from jax.sharding import PartitionSpec as P

HD = 128
MIG = 2
MOST = 4
EPSILON = 1e-06
ROPE_BASE = 1000000.0
SIDE = 4
PLANE = SIDE * SIDE
VMEM_BYTES = 56 * 1024 * 1024
BF16 = jnp.bfloat16
F32 = jnp.float32


def cut_index(y, x, z):
    return (y * SIDE + x) * 2 + z


PLANES = [[cut_index(y, x, z) for y in range(SIDE) for x in range(SIDE)] for z in range(2)]
BLOCKS = [
    [cut_index(y, x, z) for y in range(SIDE) for x in (first, first + 1)]
    for first in (0, 2)
    for z in range(2)
]


def shift(array, dy, dx):
    moves = [
        (cut_index(y, x, z), cut_index((y + dy) % SIDE, (x + dx) % SIDE, z))
        for y in range(SIDE)
        for x in range(SIDE)
        for z in range(2)
    ]
    return lax.ppermute(array, "cuts", moves)


def mirror(array):
    moves = [
        (cut_index(y, x, z), cut_index(y, SIDE - 1 - x, z))
        for y in range(SIDE)
        for x in range(SIDE)
        for z in range(2)
    ]
    return lax.ppermute(array, "cuts", moves)


def pair_perm(side):
    out = []
    for z in range(4):
        for core in range(2):
            way = (side + core) % 2
            other = z ^ 1 if way == 0 else (z + 1 if z % 2 else z - 1) % 4
            for y in range(SIDE):
                for x in range(SIDE):
                    out.append(
                        (
                            ((z // 2) * 2 + core) * 32 + cut_index(y, x, z % 2),
                            ((other // 2) * 2 + core) * 32 + cut_index(y, x, other % 2),
                        )
                    )
    return out


def from_pair(array, side):
    return lax.ppermute(array, ("inst", "cuts"), pair_perm(side))


def norm_rows(values, gain_vec):
    mean_square = jnp.mean(values * values, axis=-1, keepdims=True)
    return values * lax.rsqrt(mean_square + EPSILON) * gain_vec


def attend_kernel(
    lens_ref, q_ref, kv_ref, gcos_ref, gsin_ref, kcos_ref, ksin_ref, turn_ref, cache_ref,
    att_ref, entry_ref, qs_ref, es_ref, os_ref, *, rows_step, kv_count, group_size,
):
    step = pl.program_id(0)
    peers, rows = q_ref.shape[:2]
    per_peer = att_ref.shape[2] // HD
    length_cap = cache_ref.shape[1]
    width = kv_count * HD
    ones = jnp.ones((HD, HD), BF16)

    @pl.when(step == 0)
    def _():
        def prepare(heads, cosine, sine):
            stacked = jnp.concatenate(heads, axis=0)
            values = stacked.astype(F32)
            squares = values * values
            high = squares.astype(BF16)
            low = (squares - high.astype(F32)).astype(BF16)
            total = jnp.dot(high, ones, preferred_element_type=F32)
            total += jnp.dot(low, ones, preferred_element_type=F32)
            turned = jnp.dot(stacked, turn_ref[...], preferred_element_type=F32)
            inverse = lax.rsqrt(total * (1.0 / HD) + EPSILON)
            count = len(heads)
            cosine = jnp.concatenate([cosine] * count, axis=0)
            sine = jnp.concatenate([sine] * count, axis=0)
            return (values * cosine + turned * sine) * inverse

        gcos, gsin = gcos_ref[...], gsin_ref[...]
        for p in range(peers):
            heads = [q_ref[p, :, j * HD : (j + 1) * HD] for j in range(per_peer)]
            ready = prepare(heads, gcos, gsin)
            for j in range(per_peer):
                qs_ref[:, p * per_peer + j, :] = ready[j * rows : (j + 1) * rows]
        heads = [kv_ref[:, k * HD : (k + 1) * HD] for k in range(kv_count)]
        keys = prepare(heads, kcos_ref[...], ksin_ref[...]).astype(BF16)
        for k in range(kv_count):
            key = keys[k * rows : (k + 1) * rows]
            entry_ref[:, k * HD : (k + 1) * HD] = key
            es_ref[:, k, :] = key.astype(F32)
            value = kv_ref[:, width + k * HD : width + (k + 1) * HD]
            entry_ref[:, width + k * HD : width + (k + 1) * HD] = value
            es_ref[:, kv_count + k, :] = value.astype(F32)

    scale = HD ** (-0.5)
    heads = kv_count * group_size
    positions = lax.broadcasted_iota(jnp.int32, (heads, length_cap), 1)
    places = lax.broadcasted_iota(jnp.int32, (length_cap, 2 * width), 0)
    spans = [slice(k * group_size, (k + 1) * group_size) for k in range(kv_count)]
    first = step * rows_step
    blocks, scores, weights, results = [], [], [], []
    for i in range(rows_step):
        entry = es_ref[first + i]
        entry = jnp.concatenate(
            [entry[k : k + 1] for k in range(2 * kv_count)], axis=1
        ).astype(BF16)
        blocks.append(jnp.where(places == lens_ref[first + i], entry, cache_ref[i]))
    for i in range(rows_step):
        queries = qs_ref[first + i].astype(BF16)
        scores.append(
            jnp.concatenate(
                [
                    lax.dot_general(
                        queries[spans[k]], blocks[i][:, k * HD : (k + 1) * HD],
                        (((1,), (1,)), ((), ())), preferred_element_type=F32,
                    )
                    for k in range(kv_count)
                ],
                axis=0,
            )
        )
    for i in range(rows_step):
        score = jnp.where(positions <= lens_ref[first + i], scores[i] * scale, -1e30)
        peak = jnp.max(score, axis=1, keepdims=True)
        weights.append(jnp.exp(score - peak).astype(BF16))
    for i in range(rows_step):
        total = jnp.dot(weights[i], ones, preferred_element_type=F32)
        summed = jnp.concatenate(
            [
                jnp.dot(
                    weights[i][spans[k]],
                    blocks[i][:, width + k * HD : width + (k + 1) * HD],
                    preferred_element_type=F32,
                )
                for k in range(kv_count)
            ],
            axis=0,
        )
        results.append(summed / total)
    for i in range(rows_step):
        os_ref[first + i] = results[i]

    @pl.when(step == pl.num_programs(0) - 1)
    def _():
        for p in range(peers):
            for j in range(per_peer):
                att_ref[p, :, j * HD : (j + 1) * HD] = os_ref[:, p * per_peer + j, :].astype(BF16)


def attend(q_peers, q_width, kv_rows, cache_kv, lengths, q_gain, k_gain):
    peers, rows, sent_width = q_peers.shape
    length_cap, entry_width = cache_kv.shape[1:]
    kv_count = entry_width // (2 * HD)
    heads = peers * q_width // HD
    rows_step = 8
    half = HD // 2
    frequency = ROPE_BASE ** (-2.0 * jnp.arange(half, dtype=F32) / HD)
    angles = lengths.astype(F32)[:, None] * frequency[None, :]
    cosine = jnp.concatenate([jnp.cos(angles), jnp.cos(angles)], axis=-1)
    sine = jnp.concatenate([jnp.sin(angles), jnp.sin(angles)], axis=-1)
    turn = (jnp.eye(HD, k=half) - jnp.eye(HD, k=-half)).astype(BF16)
    tables = [
        table * gain[None, :]
        for gain in (q_gain, k_gain)
        for table, gain in ((cosine, gain), (sine, jnp.roll(gain, half)))
    ]
    whole = lambda shape: pl.BlockSpec(shape, lambda i, lens: (0,) * len(shape))
    return pl.pallas_call(
        functools.partial(
            attend_kernel, rows_step=rows_step, kv_count=kv_count, group_size=heads // kv_count
        ),
        grid_spec=pltpu.PrefetchScalarGridSpec(
            num_scalar_prefetch=1,
            grid=(rows // rows_step,),
            in_specs=[
                whole((peers, rows, sent_width)),
                whole((rows, entry_width)),
                whole((rows, HD)),
                whole((rows, HD)),
                whole((rows, HD)),
                whole((rows, HD)),
                whole((HD, HD)),
                pl.BlockSpec((rows_step, length_cap, entry_width), lambda i, lens: (i, 0, 0)),
            ],
            out_specs=[whole((peers, rows, q_width)), whole((rows, entry_width))],
            scratch_shapes=[
                pltpu.VMEM((rows, heads, HD), F32),
                pltpu.VMEM((rows, 2 * kv_count, HD), F32),
                pltpu.VMEM((rows, heads, HD), F32),
            ],
        ),
        out_shape=[
            jax.ShapeDtypeStruct((peers, rows, q_width), BF16),
            jax.ShapeDtypeStruct((rows, entry_width), BF16),
        ],
        compiler_params=pltpu.CompilerParams(vmem_limit_bytes=VMEM_BYTES),
        cost_estimate=pl.CostEstimate(
            flops=4 * rows * heads * HD * length_cap,
            bytes_accessed=cache_kv.size * 2 + q_peers.size * 4,
            transcendentals=rows * heads * length_cap,
        ),
        name="attend",
    )(lengths, q_peers, kv_rows, *tables, turn, cache_kv)


WINDOW = 16


def place_kernel(
    lens_ref, distance_ref, rank_ref, entry_ref, cache_ref, *refs,
):
    *landed_refs, out_ref, rows_ref, in_sems, out_sems = refs
    rows = out_ref.shape[0]

    def copy_in(row, source, source_row):
        return pltpu.make_async_copy(source.at[source_row], rows_ref.at[row], in_sems.at[row])

    def copy_out(row):
        return pltpu.make_async_copy(rows_ref.at[row], out_ref.at[row], out_sems.at[row])

    def begin(row, carry):
        @pl.when(distance_ref[row] == 0)
        def _():
            copy_in(row, cache_ref, row).start()

        for distance, landed_ref in enumerate(landed_refs, 1):

            @pl.when(distance_ref[row] == distance)
            def _(landed_ref=landed_ref):
                copy_in(row, landed_ref, rank_ref[row]).start()

        return carry

    def renew(row, carry):
        copy_in(row, cache_ref, row).wait()
        start = pl.multiple_of(lens_ref[row] // WINDOW * WINDOW, WINDOW)
        window = rows_ref.at[row, pl.ds(start, WINDOW)]
        position = lax.broadcasted_iota(jnp.int32, window.shape, 0) + start
        window[...] = jnp.where(position == lens_ref[row], entry_ref[row], window[...])
        copy_out(row).start()
        return carry

    def finish(row, carry):
        copy_out(row).wait()
        return carry

    lax.fori_loop(0, rows, begin, 0)
    lax.fori_loop(0, rows, renew, 0)
    lax.fori_loop(0, rows, finish, 0)


def place_cache(lengths, distance, rank, entries, cache_kv, landed):
    rows, length_cap, entry_width = cache_kv.shape
    return pl.pallas_call(
        place_kernel,
        grid_spec=pltpu.PrefetchScalarGridSpec(
            num_scalar_prefetch=3,
            grid=(1,),
            in_specs=[
                pl.BlockSpec((rows, 1, entry_width), lambda i, a, b, c: (0, 0, 0)),
            ]
            + [pl.BlockSpec(memory_space=pl.ANY)] * (1 + len(landed)),
            out_specs=pl.BlockSpec(memory_space=pl.ANY),
            scratch_shapes=[
                pltpu.VMEM((rows, length_cap, entry_width), BF16),
                pltpu.SemaphoreType.DMA((rows,)),
                pltpu.SemaphoreType.DMA((rows,)),
            ],
        ),
        out_shape=jax.ShapeDtypeStruct(cache_kv.shape, BF16),
        compiler_params=pltpu.CompilerParams(vmem_limit_bytes=VMEM_BYTES),
        cost_estimate=pl.CostEstimate(
            flops=0, bytes_accessed=cache_kv.size * 4, transcendentals=0
        ),
        name="place_cache",
    )(lengths, distance, rank, entries[:, None, :], cache_kv, *landed)


def pick_kernel(slot_ref, *refs):
    count = len(refs) // 2
    for source, target in zip(refs[:count], refs[count:]):
        target[...] = source[...]


def pick_caches(slots, cache_kv):
    shifts, count = slots.shape
    block = (1,) + cache_kv.shape[1:]
    return pl.pallas_call(
        pick_kernel,
        grid_spec=pltpu.PrefetchScalarGridSpec(
            num_scalar_prefetch=1,
            grid=(count,),
            in_specs=[
                pl.BlockSpec(block, lambda i, slots, k=k: (slots[k, i], 0, 0))
                for k in range(shifts)
            ],
            out_specs=[pl.BlockSpec(block, lambda i, slots: (i, 0, 0)) for k in range(shifts)],
        ),
        out_shape=[
            jax.ShapeDtypeStruct((count,) + cache_kv.shape[1:], BF16) for k in range(shifts)
        ],
        compiler_params=pltpu.CompilerParams(vmem_limit_bytes=VMEM_BYTES),
        cost_estimate=pl.CostEstimate(
            flops=0,
            bytes_accessed=4 * shifts * count * cache_kv.shape[1] * cache_kv.shape[2],
            transcendentals=0,
        ),
        name="pick_caches",
    )(slots, *([cache_kv] * shifts))


def exchange(array, groups=PLANES):
    return lax.all_to_all(array, "cuts", 0, 0, tiled=True, axis_index_groups=groups)


def behind(array, *marks):
    return lax.optimization_barrier((array, *marks))[0]


def swap_cores(array):
    return lax.ppermute(array, "inst", [(g, g ^ 1) for g in range(4)])


def rows_kernel(places_ref, *refs):
    *pieces, weights_ref, out_ref, rows_ref, total_ref = refs
    step = pl.program_id(0)
    at = 0
    for piece in pieces:
        count = piece.shape[0] * piece.shape[1]
        rows_ref[at : at + count] = piece[...].reshape(count, piece.shape[2])
        at += count
    part = jnp.dot(rows_ref[...], weights_ref[...], preferred_element_type=F32)

    @pl.when(step == 0)
    def _():
        total_ref[...] = part

    @pl.when(step > 0)
    def _():
        total_ref[...] += part

    @pl.when(step == pl.num_programs(0) - 1)
    def _():
        lines = out_ref.shape[1]
        for line in range(out_ref.shape[0]):
            out_ref[places_ref[line]] = total_ref[line * lines : (line + 1) * lines].astype(BF16)


def project_rows(places, pieces, weights):
    rows = sum(piece.shape[0] * piece.shape[1] for piece in pieces)
    width, columns = weights.shape
    depth = width // 4
    out = (SIDE, rows // SIDE, columns)
    return pl.pallas_call(
        rows_kernel,
        grid_spec=pltpu.PrefetchScalarGridSpec(
            num_scalar_prefetch=1,
            grid=(width // depth,),
            in_specs=[
                pl.BlockSpec(piece.shape[:2] + (depth,), lambda i, places: (0, 0, i))
                for piece in pieces
            ]
            + [pl.BlockSpec((depth, columns), lambda i, places: (i, 0))],
            out_specs=pl.BlockSpec(out, lambda i, places: (0, 0, 0)),
            scratch_shapes=[pltpu.VMEM((rows, depth), BF16), pltpu.VMEM((rows, columns), F32)],
        ),
        out_shape=jax.ShapeDtypeStruct(out, BF16),
        compiler_params=pltpu.CompilerParams(vmem_limit_bytes=VMEM_BYTES),
        cost_estimate=pl.CostEstimate(
            flops=2 * rows * width * columns,
            bytes_accessed=2 * (rows * width + weights.size),
            transcendentals=0,
        ),
        name="project_rows",
    )(places, *pieces, weights)


def out_kernel(heads_ref, *refs, spots):
    out_ref = refs[-1]
    sources, _, rows, _ = heads_ref.shape
    steps = pl.num_programs(0)

    def add_up(weights):
        total = 0.0
        for (offset, first), piece in zip(spots, weights):
            depth = piece.shape[0]
            heads = heads_ref[:, offset].reshape(sources * rows, -1)[:, first : first + depth]
            total += jnp.dot(heads, piece[...], preferred_element_type=F32)
        out_ref[...] = total.astype(BF16)

    @pl.when(pl.program_id(0) < steps // 2)
    def _():
        add_up(refs[: len(spots)])

    @pl.when(pl.program_id(0) >= steps // 2)
    def _():
        add_up(refs[len(spots) : 2 * len(spots)])


def project_out(heads, spots, mine, other):
    sources, _, rows, _ = heads.shape
    half = mine[0].shape[1]
    tile = 512
    steps = half // tile
    first = [
        pl.BlockSpec((part.shape[0], tile), lambda i: (0, jnp.minimum(i, steps - 1)))
        for part in mine
    ]
    second = [
        pl.BlockSpec((part.shape[0], tile), lambda i: (0, jnp.maximum(i - steps, 0)))
        for part in other
    ]
    return pl.pallas_call(
        functools.partial(out_kernel, spots=spots),
        grid=(2 * steps,),
        in_specs=[pl.BlockSpec(heads.shape, lambda i: (0, 0, 0, 0))] + first + second,
        out_specs=pl.BlockSpec((sources * rows, tile), lambda i: (0, i)),
        out_shape=jax.ShapeDtypeStruct((sources * rows, 2 * half), BF16),
        compiler_params=pltpu.CompilerParams(vmem_limit_bytes=VMEM_BYTES),
        cost_estimate=pl.CostEstimate(
            flops=2 * heads.size * 2 * half,
            bytes_accessed=4 * sum(part.size for part in mine),
            transcendentals=0,
        ),
        name="project_out",
    )(heads, *mine, *other)


def body(
    hidden,
    cache_kv,
    cache_len,
    mig_source,
    expert_ids,
    gate_w,
    attn_gain,
    w_query,
    w_keyval,
    q_gain,
    k_gain,
    w_out,
    moe_gain,
    w_gate,
    w_up,
    w_down,
):
    group_count = lax.axis_size("inst")
    cut_count = lax.axis_size("cuts")
    local_rows, width = hidden.shape
    group_total = local_rows * cut_count
    group_id = lax.axis_index("inst")
    cut_id = lax.axis_index("cuts")
    low = cut_id % 2 == 0
    at_x = (cut_id // 2) % SIDE
    at_y = cut_id // (2 * SIDE)
    slot_ids = jnp.arange(local_rows, dtype=jnp.int32)
    own_rows = (group_id * cut_count + cut_id) * local_rows + slot_ids

    facts = jnp.stack([mig_source, cache_len]).astype(F32)
    all_facts = lax.all_to_all(
        jnp.broadcast_to(facts[None], (group_count,) + facts.shape), "inst", 0, 0, tiled=True
    )

    w_keyval_pair = from_pair(w_keyval, 0)
    first_core = group_id % 2 == 0
    half_depth = width // 2
    w_query_part = from_pair(
        lax.dynamic_slice_in_dim(w_query, (group_id % 2) * half_depth, half_depth, 0), 0
    )
    w_query_rest = swap_cores(w_query_part)

    normed = norm_rows(hidden.astype(F32), attn_gain.astype(F32)).astype(BF16)
    half_rows = local_rows // 2
    after, before = shift(normed, 0, SIDE - 1), shift(normed, 0, 1)
    across = jnp.concatenate(
        [shift(after[:half_rows], 0, SIDE - 1), shift(before[half_rows:], 0, 1)]
    )
    line = jnp.zeros((SIDE,) + normed.shape, BF16)
    for offset, rows in enumerate((normed, after, across, before)):
        line = lax.dynamic_update_slice(line, rows[None], ((at_x + offset) % SIDE, 0, 0))
    half_line = SIDE // 2
    after, before = shift(line, SIDE - 1, 0), shift(line, 1, 0)
    across = [shift(after[:half_line], SIDE - 1, 0), shift(before[half_line:], 1, 0)]

    half_width = width // 2
    w_mine = lax.dynamic_slice_in_dim(w_out, (group_id % 2) * half_width, half_width, 1)
    w_here = jnp.concatenate([w_mine, from_pair(w_mine, 1)])
    w_there = mirror(w_here)

    w_gate, w_up, w_here = lax.optimization_barrier((w_gate, w_up, w_here))
    one_pair = from_pair(jnp.where(first_core, w_gate, w_up), 1)
    w_down, w_query_rest = lax.optimization_barrier((w_down, w_query_rest))
    w_down_pair = from_pair(w_down, 0)

    w_query_pair = jnp.where(
        first_core,
        jnp.concatenate([w_query_part, w_query_rest]),
        jnp.concatenate([w_query_rest, w_query_part]),
    )
    w_project = lax.optimization_barrier(
        jnp.concatenate([w_query, w_query_pair, w_keyval, w_keyval_pair], axis=1)
    )
    q_width = 2 * w_query.shape[1]
    kv_width = w_keyval.shape[1]

    places = (at_y + jnp.arange(SIDE, dtype=jnp.int32)) % SIDE
    projected = project_rows(places, [line, after, *across, before], w_project)
    arrived = exchange(projected.reshape(PLANE, local_rows, -1))

    goes_to = all_facts[:, 0].astype(jnp.int32) == own_rows[None, :]
    lengths = jnp.sum(jnp.where(goes_to, all_facts[:, 1], 0.0), axis=0).astype(jnp.int32)
    targets = jnp.arange(group_count, dtype=jnp.int32)
    leaving = goes_to & (targets[:, None] != group_id)
    leave_rank = jnp.cumsum(leaving.astype(jnp.int32), axis=1) - 1
    chosen = leaving[:, None, :] & (
        leave_rank[:, None, :] == jnp.arange(MIG, dtype=jnp.int32)[None, :, None]
    )
    send_slot = jnp.sum(jnp.where(chosen, slot_ids[None, None, :], 0), axis=2)
    source_group = mig_source // group_total
    arriving = source_group != group_id
    from_group = (source_group[None, :] == targets[:, None]) & arriving[None, :]
    arrival_rank = jnp.sum(
        jnp.where(from_group, jnp.cumsum(from_group.astype(jnp.int32), axis=1) - 1, 0), axis=0
    )
    source_pick = jnp.where(arriving, source_group, 0)


    own_kv = arrived[:, :, q_width : q_width + kv_width]
    pair_kv = arrived[:, :, q_width + kv_width :]
    kv_rows = jnp.where(
        low,
        jnp.concatenate([own_kv, pair_kv], axis=2),
        jnp.concatenate([pair_kv, own_kv], axis=2),
    )
    kv_rows = jnp.transpose(kv_rows, (1, 0, 2)).reshape(local_rows, -1)
    attention, entries = attend(arrived, q_width, kv_rows, cache_kv, lengths, q_gain, k_gain)

    attention = attention.reshape(SIDE, 2, 2, local_rows, q_width)
    left = at_x < 2
    near = jnp.where(left, attention[:, 0], attention[:, 1])
    far = jnp.where(left, attention[:, 1], attention[:, 0])[:, ::-1]
    attention = jnp.stack([near, far], axis=2).reshape(2 * SIDE, 2, local_rows, q_width)
    heads = exchange(attention, BLOCKS)
    heads = behind(heads, w_down_pair)
    other_pair = swap_cores(behind(one_pair, heads))
    mine = [w_here, w_there]
    other = [swap_cores(behind(part, projected)) for part in mine]
    partial_value = project_out(heads, [(0, 0), (1, 0)], mine, other)
    sums = exchange(partial_value.reshape(2 * SIDE, local_rows, width), BLOCKS)

    sums = behind(sums, other_pair)

    attn_out = jnp.sum(sums.astype(F32), axis=0)
    mine_out, other_out = attn_out[:, :half_width], attn_out[:, half_width:]
    mixed_rows = hidden.astype(F32) + jnp.concatenate(
        [jnp.where(first_core, mine_out, other_out), jnp.where(first_core, other_out, mine_out)],
        axis=1,
    )
    rows_entries = jnp.concatenate([mixed_rows, entries.astype(F32)], axis=1)
    got_rows = lax.all_to_all(rows_entries[send_slot], "inst", 0, 0, tiled=True)
    rows_entries = jnp.where(
        arriving[:, None], got_rows[source_pick, arrival_rank], rows_entries
    )
    mixed_rows = rows_entries[:, :width]
    new_entries = rows_entries[:, width:].astype(BF16)

    shifts = jnp.arange(1, group_count, dtype=jnp.int32)
    picked = pick_caches(
        behind(send_slot, got_rows)[(group_id + shifts) % group_count], cache_kv
    )
    landed = [
        lax.ppermute(
            array, "inst", [(g, (g + distance) % group_count) for g in range(group_count)]
        )
        for distance, array in zip(range(1, group_count), picked)
    ]
    distance = (group_id - source_group) % group_count
    cache_next = place_cache(cache_len, distance, arrival_rank, new_entries, cache_kv, landed)

    moe_local = norm_rows(mixed_rows, moe_gain.astype(F32)).astype(BF16)

    expert_range = jnp.arange(PLANE, dtype=jnp.int32)
    combine = jnp.sum(
        jnp.where(
            expert_ids[:, :, None] == expert_range[None, None, :],
            gate_w.astype(F32)[:, :, None],
            0.0,
        ),
        axis=1,
    )
    flags = jnp.transpose(combine) > 0.0
    rank = jnp.cumsum(flags.astype(jnp.int32), axis=1) - 1
    slot_range = jnp.arange(MOST, dtype=jnp.int32)
    match = flags[:, None, :] & (rank[:, None, :] == slot_range[None, :, None])
    match = match.reshape(PLANE * MOST, local_rows)
    slab = jnp.dot(match.astype(BF16), moe_local, preferred_element_type=F32).astype(BF16)
    slab_rows = exchange(slab.reshape(PLANE, MOST, width)).reshape(PLANE * MOST, width)
    slab_rows = behind(slab_rows, *picked)

    def expert_half(gate_part, upward, down):
        activation = (jax.nn.silu(gate_part) * upward).astype(BF16)
        return jnp.dot(activation, down, preferred_element_type=F32)

    own_gate = jnp.dot(slab_rows, w_gate, preferred_element_type=F32)
    own_up = jnp.dot(slab_rows, w_up, preferred_element_type=F32)
    pair_one = jnp.dot(slab_rows, one_pair, preferred_element_type=F32)
    pair_other = jnp.dot(slab_rows, other_pair, preferred_element_type=F32)
    pair_gate = jnp.where(first_core, pair_one, pair_other)
    pair_up = jnp.where(first_core, pair_other, pair_one)
    expert_out = (
        expert_half(own_gate, own_up, w_down) + expert_half(pair_gate, pair_up, w_down_pair)
    ).astype(BF16)
    returned = exchange(expert_out.reshape(PLANE, MOST, width)).reshape(PLANE * MOST, width)
    returned = behind(returned, cache_next)
    slot_gate = jnp.where(
        match, jnp.repeat(jnp.transpose(combine), MOST, axis=0), 0.0
    ).astype(BF16)
    moe_out = lax.dot_general(
        slot_gate, returned, (((0,), (0,)), ((), ())), preferred_element_type=F32
    )
    hidden_next = (mixed_rows + moe_out).astype(BF16)
    return (hidden_next, cache_next)


def solution(mesh):
    in_specs = (
        P(("inst", "cuts"), None),
        P(("inst", "cuts"), None, None),
        P(("inst", "cuts")),
        P(("inst", "cuts")),
        P(("inst", "cuts"), None),
        P(("inst", "cuts"), None),
        P(),
        P(None, "cuts"),
        P(None, "cuts"),
        P(),
        P(),
        P("cuts", None),
        P(),
        P(None, "cuts"),
        P(None, "cuts"),
        P("cuts", None),
    )
    out_specs = (P(("inst", "cuts"), None), P(("inst", "cuts"), None, None))
    return jax.shard_map(body, mesh=mesh, in_specs=in_specs, out_specs=out_specs, check_vma=False)
```

time: 279 us -> 237 us (0.85)
  local copies, waits for them, and re-layouts: 37 us -> 20.8 us
  Pallas kernels: 55 us -> 39.9 us
  blocking collectives: 0 us -> 11.8 us
  waiting for transfers between devices: 84.7 us -> 73.2 us
  starting transfers between devices: 60.2 us -> 50.8 us
    ppermute x12 -> x8, waiting for transfers between devices: 44.1 us -> 19.2 us  [shift(): return lax.ppermute(array, 'cuts', moves)]
    all_to_all x5 -> x4, waiting for transfers between devices: 23.7 us -> 41.2 us  [exchange(): lax.all_to_all(array, 'cuts', 0, 0, tiled=True, axis_index_groups=groups)]
    all_to_all x0 -> x1, blocking collectives: none -> 11.8 us  [exchange(): lax.all_to_all(array, 'cuts', 0, 0, tiled=True, axis_index_groups=groups)]
    ppermute x5, waiting for transfers between devices: 9.94 us -> 0.01 us  [from_pair(): return lax.ppermute(array, ('inst', 'cuts'), pair_perm(side))]
    pallas_call x3 -> x2, Pallas kernels: 25.1 us -> 17.5 us  [the longest x1 9.17 us: project_out(): pl.pallas_call(functools.partial(out_kernel, spots=spots), grid=(2 * step...]
    pallas_call x1, Pallas kernels: 18.2 us -> 10.7 us  [attend(): pl.pallas_call(functools.partial(attend_kernel, rows_step=rows_step, kv_c...]
    all_to_all x5 -> x4, starting transfers between devices: 21.5 us -> 15.1 us  [exchange(): lax.all_to_all(array, 'cuts', 0, 0, tiled=True, axis_index_groups=groups)]
    all_to_all x1, waiting for transfers between devices: 0.01 us -> 6.34 us  [body(): lax.all_to_all(jnp.broadcast_to(facts[None], (group_count,) + facts.shape...]
  transfers between devices with their start and end apart: 34 -> 27, of which waited for: 13 -> 9; matrix products, arithmetic and copies ran while one was open for 17% -> 20% of each run, Pallas kernels for 20% -> 17%
where the time goes in v3:
time: 237 us; the launch traced here: 236 us
  waiting for transfers between devices  73.2 us (31%)
  starting transfers between devices  50.8 us (21%)
  Pallas kernels  39.9 us (17%)
  other arithmetic  22.1 us (9%)
  local copies, waits for them, and re-layouts  20.8 us (9%)
  matrix products  16 us (7%)
  blocking collectives  11.8 us (5%)
    all_to_all x4, waiting for transfers between devices, exchange(): lax.all_to_all(array, 'cuts', 0, 0, tiled=True, axis_index_groups=groups)  41.2 us
    ppermute x8, waiting for transfers between devices, shift(): return lax.ppermute(array, 'cuts', moves)  19.2 us
    all_to_all x4, starting transfers between devices, exchange(): lax.all_to_all(array, 'cuts', 0, 0, tiled=True, axis_index_groups=groups)  15.1 us
    ppermute x8, starting transfers between devices, shift(): return lax.ppermute(array, 'cuts', moves)  13.2 us
    all_to_all x1, blocking collectives, exchange(): lax.all_to_all(array, 'cuts', 0, 0, tiled=True, axis_index_groups=groups)  11.8 us
    pallas_call x1, Pallas kernels, attend(): pl.pallas_call(functools.partial(attend_kernel, rows_step=rows_step, kv_c...  10.7 us
    pallas_call x1, Pallas kernels, project_out(): pl.pallas_call(functools.partial(out_kernel, spots=spots), grid=(2 * step...  9.17 us
    dot_general x2, matrix products, expert_half(): return jnp.dot(activation, down, preferred_element_type=F32)  8.76 us
  transfers between devices with their start and end apart: 27, of which 9 were waited for; matrix products, arithmetic and copies ran while one was open for 20% of the time, Pallas kernels for 17%

profile of v3, /device:TPU:0, one launch (start us, length us, event | category | flops | bytes accessed | tf_op | source)
XLA Modules:
  0.0 235.9 jit_solution(2438108268655546167)
XLA Ops:
  4.6 2.8 %collective-permute-start = (bf16[32,4096]{1,0:T(8,128)(2,1)}, bf16[32,4096]{1,0:T(8,128)(2,1)}, u32[]{:S(2)}, u32[]{:S(2)}) collective-permute-start(bf16[32,4096]{1,0:T(8,128)(2,1)} %get-tuple-element.43), channel_id=1, source_target_pairs={{0,6},{1,7},{2,0},{3,1},{4,2},{5,3},{6,4},{7,5},{8,14},{9,15},{10,... | collective-permute-start | bytes 786440 | tf_op jit(solution)/shard_map/ppermute | solution.py:40
  12.3 4.9 %all-to-all-start = ((f32[4,2,32]{2,1,0:T(2,128)}), f32[4,2,32]{2,1,0:T(2,128)S(1)}, u32[]{:S(2)}, u32[]{:S(2)}) async-start(f32[4,2,32]{2,1,0:T(2,128)} %broadcast_in_dim.60), calls=%async_computation | async-start | bytes 8192 | tf_op jit(solution)/shard_map/all_to_all | solution.py:488
  18.2 4.1 %collective-permute-start.12 = (bf16[256,2048]{1,0:T(8,128)(2,1)}, bf16[256,2048]{1,0:T(8,128)(2,1)}, u32[]{:S(2)}, u32[]{:S(2)}) collective-permute-start(bf16[256,2048]{1,0:T(8,128)(2,1)} %constant_dynamic-slice_fusion), channel_id=1, source_target_pairs={{0,65},{2,67},{4,69},{6,71},{8,73},{10,75},{12,77},{14,79},{16,81}... | collective-permute-start | bytes 3145736 | tf_op jit(solution)/shard_map/ppermute | solution.py:71
  26.2 6.3 %all-to-all-done = f32[4,2,32]{2,1,0:T(2,128)S(1)} async-done(((f32[4,2,32]{2,1,0:T(2,128)}), f32[4,2,32]{2,1,0:T(2,128)S(1)}, u32[]{:S(2)}, u32[]{:S(2)}) %all-to-all-start) | async-done | bytes 1056 | tf_op jit(solution)/shard_map/all_to_all | solution.py:488
  34.3 2.6 %collective-permute-start.1 = (bf16[16,4096]{1,0:T(8,128)(2,1)S(1)}, bf16[16,4096]{1,0:T(8,128)(2,1)S(1)}, u32[]{:S(2)}, u32[]{:S(2)}) collective-permute-start(bf16[16,4096]{1,0:T(8,128)(2,1)S(1)} %slice.86), channel_id=1, source_target_pairs={{0,6},{1,7},{2,0},{3,1},{4,2},{5,3},{6,4},{7,5},{8,14},{9,15},{10,... | collective-permute-start | bytes 393224 | tf_op jit(solution)/shard_map/ppermute | solution.py:40
  40.2 3.1 %collective-permute-start.4 = (bf16[4,32,4096]{2,1,0:T(8,128)(2,1)S(1)}, bf16[4,32,4096]{2,1,0:T(8,128)(2,1)S(1)}, u32[]{:S(2)}, u32[]{:S(2)}) collective-permute-start(bf16[4,32,4096]{2,1,0:T(8,128)(2,1)S(1)} %bitcast_dynamic-update-slice_fusion.refs_0_), channel_id=1, source_target_pairs={{0,24},{1,25},{2,26},{3,27},{4,28},{5,29},{6,30},{7,31},{8,0},{9,1... | collective-permute-start | bytes 3145736 | tf_op jit(solution)/shard_map/ppermute | solution.py:40
  45.1 3.2 %collective-permute-start.13 = (bf16[512,2048]{1,0:T(8,128)(2,1)S(1)}, bf16[512,2048]{1,0:T(8,128)(2,1)}, u32[]{:S(2)}, u32[]{:S(2)}) collective-permute-start(bf16[512,2048]{1,0:T(8,128)(2,1)S(1)} %pad_maximum_fusion.1.refs_0_), channel_id=1, source_target_pairs={{0,6},{1,7},{2,4},{3,5},{4,2},{5,3},{6,0},{7,1},{8,14},{9,15},{10,... | collective-permute-start | bytes 6291464 | tf_op jit(solution)/shard_map/ppermute | solution.py:50
  48.4 3.9 %broadcast_select_fusion = bf16[4096,384]{1,0:T(8,128)(2,1)} fusion(bf16[4096,384]{1,0:T(8,128)(2,1)} %param.29, bf16[4096,384]{1,0:T(8,128)(2,1)} %param.30, pred[]{:T(512)S(6)} %eq.101), kind=kLoop, calls=%fused_computation.10 | loop fusion | flops 1572864 | bytes 9437185 | tf_op jit(solution)/shard_map/jit(_where)/select_n | solution.py:519
  53.4 12.0 %collective-permute-done.4.refs_1_ = bf16[4,32,4096]{2,1,0:T(8,128)(2,1)S(1)} collective-permute-done((bf16[4,32,4096]{2,1,0:T(8,128)(2,1)S(1)}, bf16[4,32,4096]{2,1,0:T(8,128)(2,1)S(1)}, u32[]{:S(2)}, u32[]{:S(2)}) %collective-permute-start.4) | collective-permute-done | bytes 1048608 | tf_op jit(solution)/shard_map/ppermute | solution.py:40
  65.5 3.8 %collective-permute-start.5 = (bf16[2,32,4096]{2,1,0:T(8,128)(2,1)S(1)}, bf16[2,32,4096]{2,1,0:T(8,128)(2,1)S(1)}, u32[]{:S(2)}, u32[]{:S(2)}) collective-permute-start(bf16[2,32,4096]{2,1,0:T(8,128)(2,1)S(1)} %slice.88), channel_id=1, source_target_pairs={{0,24},{1,25},{2,26},{3,27},{4,28},{5,29},{6,30},{7,31},{8,0},{9,1... | collective-permute-start | bytes 1572872 | tf_op jit(solution)/shard_map/ppermute | solution.py:40
  71.7 4.0 %pad_maximum_fusion.refs_5_ = bf16[4096,576]{1,0:T(8,128)(2,1)} fusion(bf16[4096,32]{1,0:T(8,128)(2,1)S(1)} %copy-done.7, bf16[4096,32]{1,0:T(8,128)(2,1)S(1)} %copy-done.6, bf16[4096,256]{1,0:T(8,128)(2,1)S(1)} %maximum_select_fusion, bf16[4096,256]{1,0:T(8,128)(2,1)S(1)} %copy-done.3), kind=kLoop, calls=%fused_computation.3 | loop fusion | flops 18874368 | bytes 9437184 | tf_op jit(solution)/shard_map/concatenate | solution.py:529
  75.6 3.6 %collective-permute-done.5.refs_2_ = bf16[2,32,4096]{2,1,0:T(8,128)(2,1)S(1)} collective-permute-done((bf16[2,32,4096]{2,1,0:T(8,128)(2,1)S(1)}, bf16[2,32,4096]{2,1,0:T(8,128)(2,1)S(1)}, u32[]{:S(2)}, u32[]{:S(2)}) %collective-permute-start.5) | collective-permute-done | bytes 524320 | tf_op jit(solution)/shard_map/ppermute | solution.py:40
  79.3 3.5 %collective-permute-done.7.refs_3_ = bf16[2,32,4096]{2,1,0:T(8,128)(2,1)S(1)} collective-permute-done((bf16[2,32,4096]{2,1,0:T(8,128)(2,1)S(1)}, bf16[2,32,4096]{2,1,0:T(8,128)(2,1)S(1)}, u32[]{:S(2)}, u32[]{:S(2)}) %collective-permute-start.7) | collective-permute-done | bytes 524320 | tf_op jit(solution)/shard_map/ppermute | solution.py:40
  83.6 8.3 %project_rows.1 = bf16[4,128,576]{2,1,0:T(8,128)(2,1)} custom-call(s32[4]{0:T(128)} %and_select_fusion.2.places_ref, bf16[4,32,4096]{2,1,0:T(8,128)(2,1)} %copy-done.5, bf16[4,32,4096]{2,1,0:T(8,128)(2,1)} %copy-done.8, bf16[2,32,4096]{2,1,0:T(8,128)(2,1)} %copy-done.11, bf16[2,32,4096]{2,1,0:T(8,128)(2,1)} %copy-done.12, bf16[4,32,4096]{2,1,0:T(8,128)(2,1)} %copy-done.9, ...), custom_call_target="tpu_custom_call" | custom-call | flops 2415919104 | bytes 8912896 | tf_op jit(solution)/shard_map/project_rows/pallas_call | solution.py:382
  91.9 3.9 %all-to-all-start.1 = ((bf16[16,32,576]{2,1,0:T(8,128)(2,1)}), bf16[16,32,576]{2,1,0:T(8,128)(2,1)S(1)}, u32[]{:S(2)}, u32[]{:S(2)}) async-start(bf16[16,32,576]{2,1,0:T(8,128)(2,1)} %bitcast.77), calls=%async_computation.1 | async-start | bytes 1310720 | tf_op jit(solution)/shard_map/all_to_all | solution.py:341
  97.7 8.9 %all-to-all-done.1.q_ref = bf16[16,32,576]{2,1,0:T(8,128)(2,1)S(1)} async-done(((bf16[16,32,576]{2,1,0:T(8,128)(2,1)}), bf16[16,32,576]{2,1,0:T(8,128)(2,1)S(1)}, u32[]{:S(2)}, u32[]{:S(2)}) %all-to-all-start.1) | async-done | bytes 589856 | tf_op jit(solution)/shard_map/all_to_all | solution.py:341
  107.7 10.7 %attend.1 = (bf16[16,32,512]{2,1,0:T(8,128)(2,1)}, bf16[32,1024]{1,0:T(8,128)(2,1)}) custom-call(s32[32]{0:T(128)} %get-tuple-element.65.lens_ref, bf16[16,32,576]{2,1,0:T(8,128)(2,1)} %copy-done.4, bf16[32,1024]{1,0:T(8,128)(2,1)} %reshape.239.kv_ref, f32[32,128]{1,0:T(8,128)} %get-tuple-element.66.gcos_ref, f32[32,128]{1,0:T(8,128)} %get-tuple-element.53.gsin_ref, ...), custom_call_target="tpu_custom_call" | custom-call | flops 134217728 | bytes 9568256 | tf_op jit(solution)/shard_map/attend/pallas_call | solution.py:196
  119.7 11.8 %all_to_all.35.heads_ref = bf16[8,2,32,512]{3,2,1,0:T(8,128)(2,1)} all-to-all(bf16[8,2,32,512]{3,2,1,0:T(8,128)(2,1)S(1)} %pad_maximum_fusion.3), channel_id=1, replica_groups={{0,2,8,10,16,18,24,26},{1,3,9,11,17,19,25,27},{4,6,12,14,20,22,28,30},{..., dimensions={0} | all-to-all | bytes 1048576 | tf_op jit(solution)/shard_map/all_to_all | solution.py:341
  132.1 9.2 %project_out.1 = bf16[256,4096]{1,0:T(8,128)(2,1)} custom-call(bf16[8,2,32,512]{3,2,1,0:T(8,128)(2,1)} %all_to_all.35.heads_ref, bf16[512,2048]{1,0:T(8,128)(2,1)} %copy-done.2, bf16[512,2048]{1,0:T(8,128)(2,1)} %collective-permute-done.13.refs_1_, bf16[512,2048]{1,0:T(8,128)(2,1)} %collective-permute-done.14.refs_2_, ...), custom_call_target="tpu_custom_call" | custom-call | flops 2147483648 | bytes 8388608 | tf_op jit(solution)/shard_map/project_out/pallas_call | solution.py:441
  141.3 3.7 %all-to-all-start.3 = ((bf16[8,32,4096]{2,1,0:T(8,128)(2,1)}), bf16[8,32,4096]{2,1,0:T(8,128)(2,1)S(1)}, u32[]{:S(2)}, u32[]{:S(2)}) async-start(bf16[8,32,4096]{2,1,0:T(8,128)(2,1)} %bitcast.76), calls=%async_computation.3 | async-start | bytes 4194304 | tf_op jit(solution)/shard_map/all_to_all | solution.py:341
  146.4 26.5 %all-to-all-done.3 = bf16[8,32,4096]{2,1,0:T(8,128)(2,1)S(1)} async-done(((bf16[8,32,4096]{2,1,0:T(8,128)(2,1)}), bf16[8,32,4096]{2,1,0:T(8,128)(2,1)S(1)}, u32[]{:S(2)}, u32[]{:S(2)}) %all-to-all-start.3) | async-done | bytes 2097184 | tf_op jit(solution)/shard_map/all_to_all | solution.py:341
  174.7 3.3 %all-to-all-start.4 = ((f32[4,2,5120]{2,1,0:T(2,128)}), f32[4,2,5120]{2,1,0:T(2,128)S(1)}, u32[]{:S(2)}, u32[]{:S(2)}) async-start(f32[4,2,5120]{2,1,0:T(2,128)} %reshape.248), calls=%async_computation.4 | async-start | bytes 327680 | tf_op jit(solution)/shard_map/all_to_all | solution.py:588
  178.1 6.4 %all-to-all-done.4 = f32[4,2,5120]{2,1,0:T(2,128)S(1)} async-done(((f32[4,2,5120]{2,1,0:T(2,128)}), f32[4,2,5120]{2,1,0:T(2,128)S(1)}, u32[]{:S(2)}, u32[]{:S(2)}) %all-to-all-start.4) | async-done | bytes 163872 | tf_op jit(solution)/shard_map/all_to_all | solution.py:588
  187.8 3.7 %all-to-all-start.5 = ((bf16[16,4,4096]{2,1,0:T(4,128)(2,1)}), bf16[16,4,4096]{2,1,0:T(4,128)(2,1)S(1)}, u32[]{:S(2)}, u32[]{:S(2)}) async-start(bf16[16,4,4096]{2,1,0:T(4,128)(2,1)} %reshape.243), calls=%async_computation.5 | async-start | bytes 1048576 | tf_op jit(solution)/shard_map/all_to_all | solution.py:341
  192.8 3.1 %pick_caches.1 = (bf16[2,128,1024]{2,1,0:T(8,128)(2,1)}, bf16[2,128,1024]{2,1,0:T(8,128)(2,1)}, bf16[2,128,1024]{2,1,0:T(8,128)(2,1)}) custom-call(s32[3,2]{1,0:T(4,128)} %gather_fusion.2, bf16[32,128,1024]{2,1,0:T(8,128)(2,1)} %cache_ref.3, bf16[32,128,1024]{2,1,0:T(8,128)(2,1)} %cache_ref.3, bf16[32,128,1024]{2,1,0:T(8,128)(2,1)} %cache_ref.3), custom_call_target="tpu_custom_call" | custom-call | bytes 3145728 | tf_op jit(solution)/shard_map/pick_caches/pallas_call | solution.py:316
  196.2 2.9 %collective-permute-start.20 = (bf16[2,128,1024]{2,1,0:T(8,128)(2,1)}, bf16[2,128,1024]{2,1,0:T(8,128)(2,1)}, u32[]{:S(2)}, u32[]{:S(2)}) collective-permute-start(bf16[2,128,1024]{2,1,0:T(8,128)(2,1)} %get-tuple-element.35), channel_id=1, source_target_pairs={{0,96},{32,0},{64,32},{96,64},{1,97},{33,1},{65,33},{97,65},{2,98}... | collective-permute-start | bytes 1572872 | tf_op jit(solution)/shard_map/ppermute | solution.py:600
  199.2 3.5 %all-to-all-done.5 = bf16[16,4,4096]{2,1,0:T(4,128)(2,1)S(1)} async-done(((bf16[16,4,4096]{2,1,0:T(4,128)(2,1)}), bf16[16,4,4096]{2,1,0:T(4,128)(2,1)S(1)}, u32[]{:S(2)}, u32[]{:S(2)}) %all-to-all-start.5) | async-done | bytes 524320 | tf_op jit(solution)/shard_map/all_to_all | solution.py:341
  202.8 2.5 %fusion.50 = f32[64,384]{1,0:T(8,128)S(1)} fusion(bf16[64,4096]{1,0:T(8,128)(2,1)S(1)} %reshape.244, bf16[4096,384]{1,0:T(8,128)(2,1)} %param.29), kind=kOutput, calls=%fused_computation.136 | convolution fusion | flops 201326592 | bytes 3768320 | tf_op jit(solution)/shard_map/dot_general | solution.py:632
  207.7 4.4 %fusion.16 = f32[64,4096]{1,0:T(8,128)S(1)} fusion(bf16[384,4096]{1,0:T(8,128)(2,1)} %collective-permute-done.11, f32[64,384]{1,0:T(8,128)S(1)} %fusion.51, pred[]{:T(512)S(6)} %eq.101, bf16[64,4096]{1,0:T(8,128)(2,1)S(1)} %reshape.244, bf16[4096,384]{1,0:T(8,128)(2,1)} %collective-permute-done.17), kind=kOutput, calls=%fused_computation.54 | convolution fusion | flops 402849792 | bytes 7962625 | tf_op jit(solution)/shard_map/dot_general | solution.py:630
  212.1 4.4 %fusion = bf16[64,4096]{1,0:T(8,128)(2,1)S(1)} fusion(f32[64,4096]{1,0:T(8,128)S(1)} %fusion.16, bf16[384,4096]{1,0:T(8,128)(2,1)} %param.31, bf16[64,4096]{1,0:T(8,128)(2,1)S(1)} %reshape.244, bf16[4096,384]{1,0:T(8,128)(2,1)} %param.30, f32[64,384]{1,0:T(8,128)S(1)} %fusion.50), kind=kOutput, calls=%fused_computation.5 | convolution fusion | flops 403324928 | bytes 8486912 | tf_op jit(solution)/shard_map/dot_general | solution.py:630
  217.5 3.7 %all-to-all-start.6 = ((bf16[16,4,4096]{2,1,0:T(4,128)(2,1)}), bf16[16,4,4096]{2,1,0:T(4,128)(2,1)S(1)}, u32[]{:S(2)}, u32[]{:S(2)}) async-start(bf16[16,4,4096]{2,1,0:T(4,128)(2,1)} %reshape.245), calls=%async_computation.6 | async-start | bytes 1048576 | tf_op jit(solution)/shard_map/all_to_all | solution.py:341
  222.0 8.6 %place_cache.1 = bf16[32,128,1024]{2,1,0:T(8,128)(2,1)} custom-call(s32[32]{0:T(128)} %lens_ref.1, s32[32]{0:T(128)} %get-tuple-element.38.distance_ref, s32[32]{0:T(128)} %copy-done.17, bf16[32,1,1024]{2,1,0:T(2,128)(2,1)} %copy.64.entry_ref, bf16[32,128,1024]{2,1,0:T(8,128)(2,1)} %cache_ref.3, bf16[2,128,1024]{2,1,0:T(8,128)(2,1)} %collective-permute-done.18.refs_0_, ...), custom_call_target="tpu_custom_call" | custom-call | bytes 16777216 | tf_op jit(solution)/shard_map/place_cache/pallas_call | solution.py:282
  (170 shorter events, 47.0 us)
Async XLA Ops:
  2.7 20.3 %copy-start.15 = (f32[128]{0:T(128)S(1)}, f32[128]{0:T(128)}, u32[]{:S(2)}) copy-start(f32[128]{0:T(128)} %param.26) | copy-start | bytes 1540
  2.7 20.3 %copy-start.16 = (f32[128]{0:T(128)S(1)}, f32[128]{0:T(128)}, u32[]{:S(2)}) copy-start(f32[128]{0:T(128)} %param.25) | copy-start | bytes 1540
  4.6 28.8 %collective-permute-start = (bf16[32,4096]{1,0:T(8,128)(2,1)}, bf16[32,4096]{1,0:T(8,128)(2,1)}, u32[]{:S(2)}, u32[]{:S(2)}) collective-permute-start(bf16[32,4096]{1,0:T(8,128)(2,1)} %get-tuple-element.43), channel_id=1, source_target_pairs={{0,6},{1,7},{2,0},{3,1},{4,2},{5,3},{6,4},{7,5},{8,14},{9,15},{10,... | collective-permute-start | bytes 786440 | tf_op jit(solution)/shard_map/ppermute | solution.py:40
  7.4 25.1 %collective-permute-start.2 = (bf16[32,4096]{1,0:T(8,128)(2,1)}, bf16[32,4096]{1,0:T(8,128)(2,1)S(1)}, u32[]{:S(2)}, u32[]{:S(2)}) collective-permute-start(bf16[32,4096]{1,0:T(8,128)(2,1)} %get-tuple-element.43), channel_id=1, source_target_pairs={{0,2},{1,3},{2,4},{3,5},{4,6},{5,7},{6,0},{7,1},{8,10},{9,11},{10,... | collective-permute-start | bytes 786440 | tf_op jit(solution)/shard_map/ppermute | solution.py:40
  9.7 38.6 %collective-permute-start.8 = (bf16[2048,256]{1,0:T(8,128)(2,1)}, bf16[2048,256]{1,0:T(8,128)(2,1)}, u32[]{:S(2)}, u32[]{:S(2)}) collective-permute-start(bf16[2048,256]{1,0:T(8,128)(2,1)} %constant_dynamic-slice_fusion.1), channel_id=1, source_target_pairs={{0,1},{2,3},{4,5},{6,7},{8,9},{10,11},{12,13},{14,15},{16,17},{18,... | collective-permute-start | bytes 3145736 | tf_op jit(solution)/shard_map/ppermute | solution.py:71
  12.3 20.3 %all-to-all-start = ((f32[4,2,32]{2,1,0:T(2,128)}), f32[4,2,32]{2,1,0:T(2,128)S(1)}, u32[]{:S(2)}, u32[]{:S(2)}) async-start(f32[4,2,32]{2,1,0:T(2,128)} %broadcast_in_dim.60), calls=%async_computation | async-start | bytes 8192 | tf_op jit(solution)/shard_map/all_to_all | solution.py:488
  17.1 20.8 %collective-permute-start.10 = (bf16[4096,32]{0,1:T(8,128)(2,1)}, bf16[4096,32]{0,1:T(8,128)(2,1)}, u32[]{:S(2)}, u32[]{:S(2)}) collective-permute-start(bf16[4096,32]{0,1:T(8,128)(2,1)} %param.24), channel_id=1, source_target_pairs={{0,1},{2,3},{4,5},{6,7},{8,9},{10,11},{12,13},{14,15},{16,17},{18,... | collective-permute-start | bytes 786440 | tf_op jit(solution)/shard_map/ppermute | solution.py:71
  18.2 25.1 %collective-permute-start.12 = (bf16[256,2048]{1,0:T(8,128)(2,1)}, bf16[256,2048]{1,0:T(8,128)(2,1)}, u32[]{:S(2)}, u32[]{:S(2)}) collective-permute-start(bf16[256,2048]{1,0:T(8,128)(2,1)} %constant_dynamic-slice_fusion), channel_id=1, source_target_pairs={{0,65},{2,67},{4,69},{6,71},{8,73},{10,75},{12,77},{14,79},{16,81}... | collective-permute-start | bytes 3145736 | tf_op jit(solution)/shard_map/ppermute | solution.py:71
  32.6 7.6 %collective-permute-start.3 = (bf16[16,4096]{1,0:T(8,128)(2,1)S(1)}, bf16[16,4096]{1,0:T(8,128)(2,1)S(1)}, u32[]{:S(2)}, u32[]{:S(2)}) collective-permute-start(bf16[16,4096]{1,0:T(8,128)(2,1)S(1)} %slice.87), channel_id=1, source_target_pairs={{0,2},{1,3},{2,4},{3,5},{4,6},{5,7},{6,0},{7,1},{8,10},{9,11},{10,... | collective-permute-start | bytes 393224 | tf_op jit(solution)/shard_map/ppermute | solution.py:40
  34.3 5.8 %collective-permute-start.1 = (bf16[16,4096]{1,0:T(8,128)(2,1)S(1)}, bf16[16,4096]{1,0:T(8,128)(2,1)S(1)}, u32[]{:S(2)}, u32[]{:S(2)}) collective-permute-start(bf16[16,4096]{1,0:T(8,128)(2,1)S(1)} %slice.86), channel_id=1, source_target_pairs={{0,6},{1,7},{2,0},{3,1},{4,2},{5,3},{6,4},{7,5},{8,14},{9,15},{10,... | collective-permute-start | bytes 393224 | tf_op jit(solution)/shard_map/ppermute | solution.py:40
  40.2 25.2 %collective-permute-start.4 = (bf16[4,32,4096]{2,1,0:T(8,128)(2,1)S(1)}, bf16[4,32,4096]{2,1,0:T(8,128)(2,1)S(1)}, u32[]{:S(2)}, u32[]{:S(2)}) collective-permute-start(bf16[4,32,4096]{2,1,0:T(8,128)(2,1)S(1)} %bitcast_dynamic-update-slice_fusion.refs_0_), channel_id=1, source_target_pairs={{0,24},{1,25},{2,26},{3,27},{4,28},{5,29},{6,30},{7,31},{8,0},{9,1... | collective-permute-start | bytes 3145736 | tf_op jit(solution)/shard_map/ppermute | solution.py:40
  43.3 25.9 %collective-permute-start.6 = (bf16[4,32,4096]{2,1,0:T(8,128)(2,1)S(1)}, bf16[4,32,4096]{2,1,0:T(8,128)(2,1)S(1)}, u32[]{:S(2)}, u32[]{:S(2)}) collective-permute-start(bf16[4,32,4096]{2,1,0:T(8,128)(2,1)S(1)} %bitcast_dynamic-update-slice_fusion.refs_0_), channel_id=1, source_target_pairs={{0,8},{1,9},{2,10},{3,11},{4,12},{5,13},{6,14},{7,15},{8,16},{9,17... | collective-permute-start | bytes 3145736 | tf_op jit(solution)/shard_map/ppermute | solution.py:40
  45.1 52.1 %copy-start.2 = (bf16[512,2048]{1,0:T(8,128)(2,1)}, bf16[512,2048]{1,0:T(8,128)(2,1)S(1)}, u32[]{:S(2)}) copy-start(bf16[512,2048]{1,0:T(8,128)(2,1)S(1)} %pad_maximum_fusion.1.refs_0_) | copy-start | bytes 6291460
  45.1 52.1 %collective-permute-start.13 = (bf16[512,2048]{1,0:T(8,128)(2,1)S(1)}, bf16[512,2048]{1,0:T(8,128)(2,1)}, u32[]{:S(2)}, u32[]{:S(2)}) collective-permute-start(bf16[512,2048]{1,0:T(8,128)(2,1)S(1)} %pad_maximum_fusion.1.refs_0_), channel_id=1, source_target_pairs={{0,6},{1,7},{2,4},{3,5},{4,2},{5,3},{6,0},{7,1},{8,14},{9,15},{10,... | collective-permute-start | bytes 6291464 | tf_op jit(solution)/shard_map/ppermute | solution.py:50
  48.4 21.0 %collective-permute-start.9 = (bf16[2048,256]{1,0:T(8,128)(2,1)}, bf16[2048,256]{1,0:T(8,128)(2,1)S(1)}, u32[]{:S(2)}, u32[]{:S(2)}) collective-permute-start(bf16[2048,256]{1,0:T(8,128)(2,1)} %collective-permute-done.8), channel_id=1, source_target_pairs={{0,32},{32,0},{64,96},{96,64},{1,33},{33,1},{65,97},{97,65},{2,34}... | collective-permute-start | bytes 3145736 | tf_op jit(solution)/shard_map/ppermute | solution.py:349
  52.3 79.1 %collective-permute-start.16 = (bf16[4096,384]{1,0:T(8,128)(2,1)}, bf16[4096,384]{1,0:T(8,128)(2,1)}, u32[]{:S(2)}, u32[]{:S(2)}) collective-permute-start(bf16[4096,384]{1,0:T(8,128)(2,1)} %broadcast_select_fusion), channel_id=1, source_target_pairs={{0,65},{2,67},{4,69},{6,71},{8,73},{10,75},{12,77},{14,79},{16,81}... | collective-permute-start | bytes 9437192 | tf_op jit(solution)/shard_map/ppermute | solution.py:71
  65.5 13.8 %collective-permute-start.5 = (bf16[2,32,4096]{2,1,0:T(8,128)(2,1)S(1)}, bf16[2,32,4096]{2,1,0:T(8,128)(2,1)S(1)}, u32[]{:S(2)}, u32[]{:S(2)}) collective-permute-start(bf16[2,32,4096]{2,1,0:T(8,128)(2,1)S(1)} %slice.88), channel_id=1, source_target_pairs={{0,24},{1,25},{2,26},{3,27},{4,28},{5,29},{6,30},{7,31},{8,0},{9,1... | collective-permute-start | bytes 1572872 | tf_op jit(solution)/shard_map/ppermute | solution.py:40
  69.3 13.5 %collective-permute-start.7 = (bf16[2,32,4096]{2,1,0:T(8,128)(2,1)S(1)}, bf16[2,32,4096]{2,1,0:T(8,128)(2,1)S(1)}, u32[]{:S(2)}, u32[]{:S(2)}) collective-permute-start(bf16[2,32,4096]{2,1,0:T(8,128)(2,1)S(1)} %slice.89), channel_id=1, source_target_pairs={{0,8},{1,9},{2,10},{3,11},{4,12},{5,13},{6,14},{7,15},{8,16},{9,17... | collective-permute-start | bytes 1572872 | tf_op jit(solution)/shard_map/ppermute | solution.py:40
  69.3 62.1 %collective-permute-start.11 = (bf16[384,4096]{1,0:T(8,128)(2,1)}, bf16[384,4096]{1,0:T(8,128)(2,1)}, u32[]{:S(2)}, u32[]{:S(2)}) collective-permute-start(bf16[384,4096]{1,0:T(8,128)(2,1)} %param.31), channel_id=1, source_target_pairs={{0,1},{2,3},{4,5},{6,7},{8,9},{10,11},{12,13},{14,15},{16,17},{18,... | collective-permute-start | bytes 9437192 | tf_op jit(solution)/shard_map/ppermute | solution.py:71
  91.9 14.7 %all-to-all-start.1 = ((bf16[16,32,576]{2,1,0:T(8,128)(2,1)}), bf16[16,32,576]{2,1,0:T(8,128)(2,1)S(1)}, u32[]{:S(2)}, u32[]{:S(2)}) async-start(bf16[16,32,576]{2,1,0:T(8,128)(2,1)} %bitcast.77), calls=%async_computation.1 | async-start | bytes 1310720 | tf_op jit(solution)/shard_map/all_to_all | solution.py:341
  97.2 34.9 %collective-permute-start.14 = (bf16[512,2048]{1,0:T(8,128)(2,1)S(1)}, bf16[512,2048]{1,0:T(8,128)(2,1)}, u32[]{:S(2)}, u32[]{:S(2)}) collective-permute-start(bf16[512,2048]{1,0:T(8,128)(2,1)S(1)} %pad_maximum_fusion.1.refs_0_), channel_id=1, source_target_pairs={{0,32},{32,0},{64,96},{96,64},{1,33},{33,1},{65,97},{97,65},{2,34}... | collective-permute-start | bytes 6291464 | tf_op jit(solution)/shard_map/ppermute | solution.py:349
  97.2 34.9 %collective-permute-start.15 = (bf16[512,2048]{1,0:T(8,128)(2,1)}, bf16[512,2048]{1,0:T(8,128)(2,1)}, u32[]{:S(2)}, u32[]{:S(2)}) collective-permute-start(bf16[512,2048]{1,0:T(8,128)(2,1)} %collective-permute-done.13.refs_1_), channel_id=1, source_target_pairs={{0,32},{32,0},{64,96},{96,64},{1,33},{33,1},{65,97},{97,65},{2,34}... | collective-permute-start | bytes 6291464 | tf_op jit(solution)/shard_map/ppermute | solution.py:349
  131.4 41.5 %collective-permute-start.17 = (bf16[4096,384]{1,0:T(8,128)(2,1)}, bf16[4096,384]{1,0:T(8,128)(2,1)}, u32[]{:S(2)}, u32[]{:S(2)}) collective-permute-start(bf16[4096,384]{1,0:T(8,128)(2,1)} %collective-permute-done.16), channel_id=1, source_target_pairs={{0,32},{32,0},{64,96},{96,64},{1,33},{33,1},{65,97},{97,65},{2,34}... | collective-permute-start | bytes 9437192 | tf_op jit(solution)/shard_map/ppermute | solution.py:349
  141.3 32.0 %copy-start.10 = (bf16[32,4096]{1,0:T(8,128)(2,1)S(1)}, bf16[32,4096]{1,0:T(8,128)(2,1)}, u32[]{:S(2)}) copy-start(bf16[32,4096]{1,0:T(8,128)(2,1)} %param.16) | copy-start | bytes 786436
  141.3 31.6 %all-to-all-start.3 = ((bf16[8,32,4096]{2,1,0:T(8,128)(2,1)}), bf16[8,32,4096]{2,1,0:T(8,128)(2,1)S(1)}, u32[]{:S(2)}, u32[]{:S(2)}) async-start(bf16[8,32,4096]{2,1,0:T(8,128)(2,1)} %bitcast.76), calls=%async_computation.3 | async-start | bytes 4194304 | tf_op jit(solution)/shard_map/all_to_all | solution.py:341
  145.6 32.5 %copy-start.17 = (s32[32]{0:T(128)}, s32[32]{0:T(128)S(1)}, u32[]{:S(2)}) copy-start(s32[32]{0:T(128)S(1)} %select_reduce_fusion.2.rank_ref) | copy-start | bytes 388
  174.7 9.8 %all-to-all-start.4 = ((f32[4,2,5120]{2,1,0:T(2,128)}), f32[4,2,5120]{2,1,0:T(2,128)S(1)}, u32[]{:S(2)}, u32[]{:S(2)}) async-start(f32[4,2,5120]{2,1,0:T(2,128)} %reshape.248), calls=%async_computation.4 | async-start | bytes 327680 | tf_op jit(solution)/shard_map/all_to_all | solution.py:588
  187.8 14.9 %all-to-all-start.5 = ((bf16[16,4,4096]{2,1,0:T(4,128)(2,1)}), bf16[16,4,4096]{2,1,0:T(4,128)(2,1)S(1)}, u32[]{:S(2)}, u32[]{:S(2)}) async-start(bf16[16,4,4096]{2,1,0:T(4,128)(2,1)} %reshape.243), calls=%async_computation.5 | async-start | bytes 1048576 | tf_op jit(solution)/shard_map/all_to_all | solution.py:341
  195.8 26.1 %collective-permute-start.18 = (bf16[2,128,1024]{2,1,0:T(8,128)(2,1)}, bf16[2,128,1024]{2,1,0:T(8,128)(2,1)}, u32[]{:S(2)}, u32[]{:S(2)}) collective-permute-start(bf16[2,128,1024]{2,1,0:T(8,128)(2,1)} %get-tuple-element.33), channel_id=1, source_target_pairs={{0,32},{32,64},{64,96},{96,0},{1,33},{33,65},{65,97},{97,1},{2,34}... | collective-permute-start | bytes 1572872 | tf_op jit(solution)/shard_map/ppermute | solution.py:600
  195.8 26.1 %collective-permute-start.19 = (bf16[2,128,1024]{2,1,0:T(8,128)(2,1)}, bf16[2,128,1024]{2,1,0:T(8,128)(2,1)}, u32[]{:S(2)}, u32[]{:S(2)}) collective-permute-start(bf16[2,128,1024]{2,1,0:T(8,128)(2,1)} %get-tuple-element.34), channel_id=1, source_target_pairs={{0,64},{32,96},{64,0},{96,32},{1,65},{33,97},{65,1},{97,33},{2,66}... | collective-permute-start | bytes 1572872 | tf_op jit(solution)/shard_map/ppermute | solution.py:600
  196.2 25.7 %collective-permute-start.20 = (bf16[2,128,1024]{2,1,0:T(8,128)(2,1)}, bf16[2,128,1024]{2,1,0:T(8,128)(2,1)}, u32[]{:S(2)}, u32[]{:S(2)}) collective-permute-start(bf16[2,128,1024]{2,1,0:T(8,128)(2,1)} %get-tuple-element.35), channel_id=1, source_target_pairs={{0,96},{32,0},{64,32},{96,64},{1,97},{33,1},{65,33},{97,65},{2,98}... | collective-permute-start | bytes 1572872 | tf_op jit(solution)/shard_map/ppermute | solution.py:600
  217.5 15.5 %all-to-all-start.6 = ((bf16[16,4,4096]{2,1,0:T(4,128)(2,1)}), bf16[16,4,4096]{2,1,0:T(4,128)(2,1)S(1)}, u32[]{:S(2)}, u32[]{:S(2)}) async-start(bf16[16,4,4096]{2,1,0:T(4,128)(2,1)} %reshape.245), calls=%async_computation.6 | async-start | bytes 1048576 | tf_op jit(solution)/shard_map/all_to_all | solution.py:341
  (17 other events, 175.8 us)

commit v4 on v3

--- a/solution.py
+++ b/solution.py
@@ -484,19 +484,6 @@
     slot_ids = jnp.arange(local_rows, dtype=jnp.int32)
     own_rows = (group_id * cut_count + cut_id) * local_rows + slot_ids
 
-    facts = jnp.stack([mig_source, cache_len]).astype(F32)
-    all_facts = lax.all_to_all(
-        jnp.broadcast_to(facts[None], (group_count,) + facts.shape), "inst", 0, 0, tiled=True
-    )
-
-    w_keyval_pair = from_pair(w_keyval, 0)
-    first_core = group_id % 2 == 0
-    half_depth = width // 2
-    w_query_part = from_pair(
-        lax.dynamic_slice_in_dim(w_query, (group_id % 2) * half_depth, half_depth, 0), 0
-    )
-    w_query_rest = swap_cores(w_query_part)
-
     normed = norm_rows(hidden.astype(F32), attn_gain.astype(F32)).astype(BF16)
     half_rows = local_rows // 2
     after, before = shift(normed, 0, SIDE - 1), shift(normed, 0, 1)
@@ -510,6 +497,19 @@
     after, before = shift(line, SIDE - 1, 0), shift(line, 1, 0)
     across = [shift(after[:half_line], SIDE - 1, 0), shift(before[half_line:], 1, 0)]
 
+    facts = behind(jnp.stack([mig_source, cache_len]).astype(F32), line)
+    all_facts = lax.all_to_all(
+        jnp.broadcast_to(facts[None], (group_count,) + facts.shape), "inst", 0, 0, tiled=True
+    )
+
+    w_keyval_pair = from_pair(w_keyval, 0)
+    first_core = group_id % 2 == 0
+    half_depth = width // 2
+    w_query_part = from_pair(
+        lax.dynamic_slice_in_dim(w_query, (group_id % 2) * half_depth, half_depth, 0), 0
+    )
+    w_query_rest = swap_cores(w_query_part)
+
     half_width = width // 2
     w_mine = lax.dynamic_slice_in_dim(w_out, (group_id % 2) * half_width, half_width, 1)
     w_here = jnp.concatenate([w_mine, from_pair(w_mine, 1)])
@@ -526,7 +526,9 @@
         jnp.concatenate([w_query_rest, w_query_part]),
     )
     w_project = lax.optimization_barrier(
-        jnp.concatenate([w_query, w_query_pair, w_keyval, w_keyval_pair], axis=1)
+        jnp.concatenate(
+            [w_query, w_query_pair, behind(w_keyval, after), behind(w_keyval_pair, after)], axis=1
+        )
     )
     q_width = 2 * w_query.shape[1]
     kv_width = w_keyval.shape[1]
@@ -535,6 +537,7 @@
     projected = project_rows(places, [line, after, *across, before], w_project)
     arrived = exchange(projected.reshape(PLANE, local_rows, -1))
 
+    all_facts = behind(all_facts, projected)
     goes_to = all_facts[:, 0].astype(jnp.int32) == own_rows[None, :]
     lengths = jnp.sum(jnp.where(goes_to, all_facts[:, 1], 0.0), axis=0).astype(jnp.int32)
     targets = jnp.arange(group_count, dtype=jnp.int32)

time: 237 us -> 235 us (level)
  waiting for transfers between devices: 73.2 us -> 61.6 us
  starting transfers between devices: 50.8 us -> 57.9 us
    ppermute x8, waiting for transfers between devices: 19.2 us -> 4.07 us  [shift(): return lax.ppermute(array, 'cuts', moves)]
    ppermute x5, waiting for transfers between devices: 0.01 us -> 7.39 us  [from_pair(): return lax.ppermute(array, ('inst', 'cuts'), pair_perm(side))]
    ppermute x1, waiting for transfers between devices: 0.01 us -> 7.35 us  [mirror(): return lax.ppermute(array, 'cuts', moves)]
    all_to_all x1, waiting for transfers between devices: 6.34 us -> 0.01 us  [body(): lax.all_to_all(jnp.broadcast_to(facts[None], (group_count,) + facts.shape...]
    all_to_all x4, starting transfers between devices: 15.1 us -> 20.9 us  [exchange(): lax.all_to_all(array, 'cuts', 0, 0, tiled=True, axis_index_groups=groups)]
    all_to_all x4, waiting for transfers between devices: 41.2 us -> 36.3 us  [exchange(): lax.all_to_all(array, 'cuts', 0, 0, tiled=True, axis_index_groups=groups)]
    unnamed x45 -> x36, local copies, waits for them, and re-layouts: 3.17 us -> 0.08 us
    optimization_barrier x1 -> x3, local copies, waits for them, and re-layouts: 0.09 us -> 2.83 us  [behind(): return lax.optimization_barrier((array, *marks))[0]]
  transfers between devices with their start and end apart: 27 -> 27, of which waited for: 9 -> 10; matrix products, arithmetic and copies ran while one was open for 20% -> 21% of each run, Pallas kernels for 17% -> 17%
where the time goes in v4:
time: 235 us; the launch traced here: 233 us
  waiting for transfers between devices  61.6 us (26%)
  starting transfers between devices  57.9 us (25%)
  Pallas kernels  39.9 us (17%)
  other arithmetic  22.9 us (10%)
  local copies, waits for them, and re-layouts  21.8 us (9%)
  matrix products  16 us (7%)
  blocking collectives  11.8 us (5%)
    all_to_all x4, waiting for transfers between devices, exchange(): lax.all_to_all(array, 'cuts', 0, 0, tiled=True, axis_index_groups=groups)  36.3 us
    all_to_all x4, starting transfers between devices, exchange(): lax.all_to_all(array, 'cuts', 0, 0, tiled=True, axis_index_groups=groups)  20.9 us
    ppermute x8, starting transfers between devices, shift(): return lax.ppermute(array, 'cuts', moves)  12.3 us
    all_to_all x1, blocking collectives, exchange(): lax.all_to_all(array, 'cuts', 0, 0, tiled=True, axis_index_groups=groups)  11.8 us
    pallas_call x1, Pallas kernels, attend(): pl.pallas_call(functools.partial(attend_kernel, rows_step=rows_step, kv_c...  10.7 us
    ppermute x5, starting transfers between devices, from_pair(): return lax.ppermute(array, ('inst', 'cuts'), pair_perm(side))  9.6 us
    pallas_call x1, Pallas kernels, project_out(): pl.pallas_call(functools.partial(out_kernel, spots=spots), grid=(2 * step...  9.17 us
    dot_general x2, matrix products, expert_half(): return jnp.dot(activation, down, preferred_element_type=F32)  8.76 us
  transfers between devices with their start and end apart: 27, of which 10 were waited for; matrix products, arithmetic and copies ran while one was open for 21% of the time, Pallas kernels for 17%

profile of v4, /device:TPU:0, one launch (start us, length us, event | category | flops | bytes accessed | tf_op | source)
XLA Modules:
  0.0 233.2 jit_solution(16352828649210148659)
XLA Ops:
  4.6 2.8 %collective-permute-start = (bf16[32,4096]{1,0:T(8,128)(2,1)}, bf16[32,4096]{1,0:T(8,128)(2,1)}, u32[]{:S(2)}, u32[]{:S(2)}) collective-permute-start(bf16[32,4096]{1,0:T(8,128)(2,1)} %get-tuple-element.51), channel_id=1, source_target_pairs={{0,6},{1,7},{2,0},{3,1},{4,2},{5,3},{6,4},{7,5},{8,14},{9,15},{10,... | collective-permute-start | bytes 786440 | tf_op jit(solution)/shard_map/ppermute | solution.py:40
  12.8 4.0 %collective-permute-start.12 = (bf16[256,2048]{1,0:T(8,128)(2,1)}, bf16[256,2048]{1,0:T(8,128)(2,1)}, u32[]{:S(2)}, u32[]{:S(2)}) collective-permute-start(bf16[256,2048]{1,0:T(8,128)(2,1)} %constant_dynamic-slice_fusion), channel_id=1, source_target_pairs={{0,65},{2,67},{4,69},{6,71},{8,73},{10,75},{12,77},{14,79},{16,81}... | collective-permute-start | bytes 3145736 | tf_op jit(solution)/shard_map/ppermute | solution.py:71
  20.3 2.6 %collective-permute-start.1 = (bf16[16,4096]{1,0:T(8,128)(2,1)S(1)}, bf16[16,4096]{1,0:T(8,128)(2,1)S(1)}, u32[]{:S(2)}, u32[]{:S(2)}) collective-permute-start(bf16[16,4096]{1,0:T(8,128)(2,1)S(1)} %slice.84), channel_id=1, source_target_pairs={{0,6},{1,7},{2,0},{3,1},{4,2},{5,3},{6,4},{7,5},{8,14},{9,15},{10,... | collective-permute-start | bytes 393224 | tf_op jit(solution)/shard_map/ppermute | solution.py:40
  25.5 3.1 %collective-permute-start.4 = (bf16[4,32,4096]{2,1,0:T(8,128)(2,1)S(1)}, bf16[4,32,4096]{2,1,0:T(8,128)(2,1)}, u32[]{:S(2)}, u32[]{:S(2)}) collective-permute-start(bf16[4,32,4096]{2,1,0:T(8,128)(2,1)S(1)} %bitcast_dynamic-update-slice_fusion.refs_0_), channel_id=1, source_target_pairs={{0,24},{1,25},{2,26},{3,27},{4,28},{5,29},{6,30},{7,31},{8,0},{9,1... | collective-permute-start | bytes 3145736 | tf_op jit(solution)/shard_map/ppermute | solution.py:40
  29.1 3.2 %all-to-all-start = ((f32[4,2,32]{2,1,0:T(2,128)}), f32[4,2,32]{2,1,0:T(2,128)S(1)}, u32[]{:S(2)}, u32[]{:S(2)}) async-start(f32[4,2,32]{2,1,0:T(2,128)} %broadcast_in_dim.69), calls=%async_computation | async-start | bytes 8192 | tf_op jit(solution)/shard_map/all_to_all | solution.py:501
  32.4 7.4 %collective-permute-done.12 = bf16[256,2048]{1,0:T(8,128)(2,1)} collective-permute-done((bf16[256,2048]{1,0:T(8,128)(2,1)}, bf16[256,2048]{1,0:T(8,128)(2,1)}, u32[]{:S(2)}, u32[]{:S(2)}) %collective-permute-start.12) | collective-permute-done | bytes 1048608 | tf_op jit(solution)/shard_map/ppermute | solution.py:71
  41.6 3.0 %collective-permute-start.13 = (bf16[512,2048]{1,0:T(8,128)(2,1)S(1)}, bf16[512,2048]{1,0:T(8,128)(2,1)}, u32[]{:S(2)}, u32[]{:S(2)}) collective-permute-start(bf16[512,2048]{1,0:T(8,128)(2,1)S(1)} %pad_maximum_fusion.1.refs_0_), channel_id=1, source_target_pairs={{0,6},{1,7},{2,4},{3,5},{4,2},{5,3},{6,0},{7,1},{8,14},{9,15},{10,... | collective-permute-start | bytes 6291464 | tf_op jit(solution)/shard_map/ppermute | solution.py:50
  44.6 4.0 %broadcast_select_fusion = bf16[4096,384]{1,0:T(8,128)(2,1)} fusion(bf16[4096,384]{1,0:T(8,128)(2,1)} %param.29, bf16[4096,384]{1,0:T(8,128)(2,1)} %param.30, pred[]{:T(512)S(6)} %eq.101), kind=kLoop, calls=%fused_computation.10 | loop fusion | flops 1572864 | bytes 9437185 | tf_op jit(solution)/shard_map/jit(_where)/select_n | solution.py:519
  48.6 3.1 %collective-permute-start.16 = (bf16[4096,384]{1,0:T(8,128)(2,1)}, bf16[4096,384]{1,0:T(8,128)(2,1)}, u32[]{:S(2)}, u32[]{:S(2)}) collective-permute-start(bf16[4096,384]{1,0:T(8,128)(2,1)} %broadcast_select_fusion), channel_id=1, source_target_pairs={{0,65},{2,67},{4,69},{6,71},{8,73},{10,75},{12,77},{14,79},{16,81}... | collective-permute-start | bytes 9437192 | tf_op jit(solution)/shard_map/ppermute | solution.py:71
  53.5 3.0 %collective-permute-start.5 = (bf16[2,32,4096]{2,1,0:T(8,128)(2,1)}, bf16[2,32,4096]{2,1,0:T(8,128)(2,1)}, u32[]{:S(2)}, u32[]{:S(2)}) collective-permute-start(bf16[2,32,4096]{2,1,0:T(8,128)(2,1)} %slice.86), channel_id=1, source_target_pairs={{0,24},{1,25},{2,26},{3,27},{4,28},{5,29},{6,30},{7,31},{8,0},{9,1... | collective-permute-start | bytes 1572872 | tf_op jit(solution)/shard_map/ppermute | solution.py:40
  61.7 2.9 %maximum_select_fusion = bf16[4096,256]{1,0:T(8,128)(2,1)S(1)} fusion(bf16[2048,256]{1,0:T(8,128)(2,1)} %collective-permute-done.9, bf16[2048,256]{1,0:T(8,128)(2,1)} %collective-permute-done.8, pred[]{:T(512)S(6)} %eq.101), kind=kLoop, calls=%fused_computation.11 | loop fusion | flops 9437184 | bytes 4194305 | tf_op jit(solution)/shard_map/jit(_where)/select_n | solution.py:523
  64.6 4.0 %pad_maximum_fusion.refs_5_ = bf16[4096,576]{1,0:T(8,128)(2,1)} fusion(bf16[4096,32]{1,0:T(8,128)(2,1)S(1)} %copy.58, bf16[4096,32]{1,0:T(8,128)(2,1)S(1)} %copy-done.6, bf16[4096,256]{1,0:T(8,128)(2,1)S(1)} %maximum_select_fusion, bf16[4096,256]{1,0:T(8,128)(2,1)S(1)} %copy-done.3), kind=kLoop, calls=%fused_computation.3 | loop fusion | flops 18874368 | bytes 9437184 | tf_op jit(solution)/shard_map/concatenate | solution.py:529
  68.5 2.5 %collective-permute-done.7.refs_3_ = bf16[2,32,4096]{2,1,0:T(8,128)(2,1)} collective-permute-done((bf16[2,32,4096]{2,1,0:T(8,128)(2,1)}, bf16[2,32,4096]{2,1,0:T(8,128)(2,1)}, u32[]{:S(2)}, u32[]{:S(2)}) %collective-permute-start.7) | collective-permute-done | bytes 524320 | tf_op jit(solution)/shard_map/ppermute | solution.py:40
  71.0 8.3 %project_rows.1 = bf16[4,128,576]{2,1,0:T(8,128)(2,1)} custom-call(s32[4]{0:T(128)} %and_select_fusion.2.places_ref, bf16[4,32,4096]{2,1,0:T(8,128)(2,1)} %copy-done.5, bf16[4,32,4096]{2,1,0:T(8,128)(2,1)} %collective-permute-done.4.refs_1_, bf16[2,32,4096]{2,1,0:T(8,128)(2,1)} %collective-permute-done.5.refs_2_, ...), custom_call_target="tpu_custom_call" | custom-call | flops 2415919104 | bytes 8912896 | tf_op jit(solution)/shard_map/project_rows/pallas_call | solution.py:382
  79.4 6.5 %all-to-all-start.1 = ((bf16[16,32,576]{2,1,0:T(8,128)(2,1)}), bf16[16,32,576]{2,1,0:T(8,128)(2,1)S(1)}, u32[]{:S(2)}, u32[]{:S(2)}) async-start(bf16[16,32,576]{2,1,0:T(8,128)(2,1)} %bitcast.77), calls=%async_computation.1 | async-start | bytes 1310720 | tf_op jit(solution)/shard_map/all_to_all | solution.py:341
  87.2 7.3 %collective-permute-done.13.refs_1_ = bf16[512,2048]{1,0:T(8,128)(2,1)} collective-permute-done((bf16[512,2048]{1,0:T(8,128)(2,1)S(1)}, bf16[512,2048]{1,0:T(8,128)(2,1)}, u32[]{:S(2)}, u32[]{:S(2)}) %collective-permute-start.13) | collective-permute-done | bytes 2097184 | tf_op jit(solution)/shard_map/ppermute | solution.py:50
  94.6 4.1 %all-to-all-done.1.q_ref = bf16[16,32,576]{2,1,0:T(8,128)(2,1)S(1)} async-done(((bf16[16,32,576]{2,1,0:T(8,128)(2,1)}), bf16[16,32,576]{2,1,0:T(8,128)(2,1)S(1)}, u32[]{:S(2)}, u32[]{:S(2)}) %all-to-all-start.1) | async-done | bytes 589856 | tf_op jit(solution)/shard_map/all_to_all | solution.py:341
  99.8 10.7 %attend.1 = (bf16[16,32,512]{2,1,0:T(8,128)(2,1)}, bf16[32,1024]{1,0:T(8,128)(2,1)}) custom-call(s32[32]{0:T(128)} %get-tuple-element.73.lens_ref, bf16[16,32,576]{2,1,0:T(8,128)(2,1)} %copy-done.4, bf16[32,1024]{1,0:T(8,128)(2,1)} %reshape.223.kv_ref, f32[32,128]{1,0:T(8,128)} %get-tuple-element.74.gcos_ref, f32[32,128]{1,0:T(8,128)} %get-tuple-element.61.gsin_ref, ...), custom_call_target="tpu_custom_call" | custom-call | flops 134217728 | bytes 9568256 | tf_op jit(solution)/shard_map/attend/pallas_call | solution.py:196
  111.7 11.8 %all_to_all.35.heads_ref = bf16[8,2,32,512]{3,2,1,0:T(8,128)(2,1)} all-to-all(bf16[8,2,32,512]{3,2,1,0:T(8,128)(2,1)S(1)} %pad_maximum_fusion.3), channel_id=1, replica_groups={{0,2,8,10,16,18,24,26},{1,3,9,11,17,19,25,27},{4,6,12,14,20,22,28,30},{..., dimensions={0} | all-to-all | bytes 1048576 | tf_op jit(solution)/shard_map/all_to_all | solution.py:341
  124.2 9.2 %project_out.1 = bf16[256,4096]{1,0:T(8,128)(2,1)} custom-call(bf16[8,2,32,512]{3,2,1,0:T(8,128)(2,1)} %all_to_all.35.heads_ref, bf16[512,2048]{1,0:T(8,128)(2,1)} %copy-done.2, bf16[512,2048]{1,0:T(8,128)(2,1)} %collective-permute-done.13.refs_1_, bf16[512,2048]{1,0:T(8,128)(2,1)} %collective-permute-done.14.refs_2_, ...), custom_call_target="tpu_custom_call" | custom-call | flops 2147483648 | bytes 8388608 | tf_op jit(solution)/shard_map/project_out/pallas_call | solution.py:441
  133.4 3.7 %all-to-all-start.3 = ((bf16[8,32,4096]{2,1,0:T(8,128)(2,1)}), bf16[8,32,4096]{2,1,0:T(8,128)(2,1)S(1)}, u32[]{:S(2)}, u32[]{:S(2)}) async-start(bf16[8,32,4096]{2,1,0:T(8,128)(2,1)} %bitcast.76), calls=%async_computation.3 | async-start | bytes 4194304 | tf_op jit(solution)/shard_map/all_to_all | solution.py:341
  138.5 26.5 %all-to-all-done.3 = bf16[8,32,4096]{2,1,0:T(8,128)(2,1)S(1)} async-done(((bf16[8,32,4096]{2,1,0:T(8,128)(2,1)}), bf16[8,32,4096]{2,1,0:T(8,128)(2,1)S(1)}, u32[]{:S(2)}, u32[]{:S(2)}) %all-to-all-start.3) | async-done | bytes 2097184 | tf_op jit(solution)/shard_map/all_to_all | solution.py:341
  166.8 5.4 %all-to-all-start.4 = ((f32[4,2,5120]{2,1,0:T(2,128)}), f32[4,2,5120]{2,1,0:T(2,128)S(1)}, u32[]{:S(2)}, u32[]{:S(2)}) async-start(f32[4,2,5120]{2,1,0:T(2,128)} %reshape.232), calls=%async_computation.4 | async-start | bytes 327680 | tf_op jit(solution)/shard_map/all_to_all | solution.py:591
  172.2 6.5 %all-to-all-done.4 = f32[4,2,5120]{2,1,0:T(2,128)S(1)} async-done(((f32[4,2,5120]{2,1,0:T(2,128)}), f32[4,2,5120]{2,1,0:T(2,128)S(1)}, u32[]{:S(2)}, u32[]{:S(2)}) %all-to-all-start.4) | async-done | bytes 163872 | tf_op jit(solution)/shard_map/all_to_all | solution.py:591
  181.9 6.9 %all-to-all-start.5 = ((bf16[16,4,4096]{2,1,0:T(4,128)(2,1)}), bf16[16,4,4096]{2,1,0:T(4,128)(2,1)S(1)}, u32[]{:S(2)}, u32[]{:S(2)}) async-start(bf16[16,4,4096]{2,1,0:T(4,128)(2,1)} %reshape.227), calls=%async_computation.5 | async-start | bytes 1048576 | tf_op jit(solution)/shard_map/all_to_all | solution.py:341
  190.1 3.1 %pick_caches.1 = (bf16[2,128,1024]{2,1,0:T(8,128)(2,1)}, bf16[2,128,1024]{2,1,0:T(8,128)(2,1)}, bf16[2,128,1024]{2,1,0:T(8,128)(2,1)}) custom-call(s32[3,2]{1,0:T(4,128)} %gather_fusion.2, bf16[32,128,1024]{2,1,0:T(8,128)(2,1)} %cache_ref.3, bf16[32,128,1024]{2,1,0:T(8,128)(2,1)} %cache_ref.3, bf16[32,128,1024]{2,1,0:T(8,128)(2,1)} %cache_ref.3), custom_call_target="tpu_custom_call" | custom-call | bytes 3145728 | tf_op jit(solution)/shard_map/pick_caches/pallas_call | solution.py:316
  193.5 2.9 %collective-permute-start.20 = (bf16[2,128,1024]{2,1,0:T(8,128)(2,1)}, bf16[2,128,1024]{2,1,0:T(8,128)(2,1)}, u32[]{:S(2)}, u32[]{:S(2)}) collective-permute-start(bf16[2,128,1024]{2,1,0:T(8,128)(2,1)} %get-tuple-element.43), channel_id=1, source_target_pairs={{0,96},{32,0},{64,32},{96,64},{1,97},{33,1},{65,33},{97,65},{2,98}... | collective-permute-start | bytes 1572872 | tf_op jit(solution)/shard_map/ppermute | solution.py:603
  196.4 3.4 %all-to-all-done.5 = bf16[16,4,4096]{2,1,0:T(4,128)(2,1)S(1)} async-done(((bf16[16,4,4096]{2,1,0:T(4,128)(2,1)}), bf16[16,4,4096]{2,1,0:T(4,128)(2,1)S(1)}, u32[]{:S(2)}, u32[]{:S(2)}) %all-to-all-start.5) | async-done | bytes 524320 | tf_op jit(solution)/shard_map/all_to_all | solution.py:341
  204.9 4.4 %fusion.16 = f32[64,4096]{1,0:T(8,128)S(1)} fusion(bf16[384,4096]{1,0:T(8,128)(2,1)} %collective-permute-done.11, f32[64,384]{1,0:T(8,128)S(1)} %fusion.51, pred[]{:T(512)S(6)} %eq.101, bf16[64,4096]{1,0:T(8,128)(2,1)S(1)} %reshape.228, bf16[4096,384]{1,0:T(8,128)(2,1)} %collective-permute-done.17), kind=kOutput, calls=%fused_computation.54 | convolution fusion | flops 402849792 | bytes 7962625 | tf_op jit(solution)/shard_map/dot_general | solution.py:633
  209.3 4.4 %fusion = bf16[64,4096]{1,0:T(8,128)(2,1)S(1)} fusion(f32[64,4096]{1,0:T(8,128)S(1)} %fusion.16, bf16[384,4096]{1,0:T(8,128)(2,1)} %param.31, bf16[64,4096]{1,0:T(8,128)(2,1)S(1)} %reshape.228, bf16[4096,384]{1,0:T(8,128)(2,1)} %param.30, f32[64,384]{1,0:T(8,128)S(1)} %fusion.50), kind=kOutput, calls=%fused_computation.5 | convolution fusion | flops 403324928 | bytes 8486912 | tf_op jit(solution)/shard_map/dot_general | solution.py:633
  214.7 3.8 %all-to-all-start.6 = ((bf16[16,4,4096]{2,1,0:T(4,128)(2,1)}), bf16[16,4,4096]{2,1,0:T(4,128)(2,1)S(1)}, u32[]{:S(2)}, u32[]{:S(2)}) async-start(bf16[16,4,4096]{2,1,0:T(4,128)(2,1)} %reshape.229), calls=%async_computation.6 | async-start | bytes 1048576 | tf_op jit(solution)/shard_map/all_to_all | solution.py:341
  219.3 8.6 %place_cache.1 = bf16[32,128,1024]{2,1,0:T(8,128)(2,1)} custom-call(s32[32]{0:T(128)} %lens_ref.1, s32[32]{0:T(128)} %get-tuple-element.46.distance_ref, s32[32]{0:T(128)} %copy-done.13, bf16[32,1,1024]{2,1,0:T(2,128)(2,1)} %copy.64.entry_ref, bf16[32,128,1024]{2,1,0:T(8,128)(2,1)} %cache_ref.3, bf16[2,128,1024]{2,1,0:T(8,128)(2,1)} %collective-permute-done.18.refs_0_, ...), custom_call_target="tpu_custom_call" | custom-call | bytes 16777216 | tf_op jit(solution)/shard_map/place_cache/pallas_call | solution.py:282
  (162 shorter events, 48.8 us)
Async XLA Ops:
  1.5 16.1 %copy-start.17 = (s32[32]{0:T(128)S(1)}, s32[32]{0:T(128)}, u32[]{:S(2)}) copy-start(s32[32]{0:T(128)} %param.19) | copy-start | bytes 388
  4.6 14.8 %collective-permute-start = (bf16[32,4096]{1,0:T(8,128)(2,1)}, bf16[32,4096]{1,0:T(8,128)(2,1)}, u32[]{:S(2)}, u32[]{:S(2)}) collective-permute-start(bf16[32,4096]{1,0:T(8,128)(2,1)} %get-tuple-element.51), channel_id=1, source_target_pairs={{0,6},{1,7},{2,0},{3,1},{4,2},{5,3},{6,4},{7,5},{8,14},{9,15},{10,... | collective-permute-start | bytes 786440 | tf_op jit(solution)/shard_map/ppermute | solution.py:40
  7.5 11.1 %collective-permute-start.2 = (bf16[32,4096]{1,0:T(8,128)(2,1)}, bf16[32,4096]{1,0:T(8,128)(2,1)S(1)}, u32[]{:S(2)}, u32[]{:S(2)}) collective-permute-start(bf16[32,4096]{1,0:T(8,128)(2,1)} %get-tuple-element.51), channel_id=1, source_target_pairs={{0,2},{1,3},{2,4},{3,5},{4,6},{5,7},{6,0},{7,1},{8,10},{9,11},{10,... | collective-permute-start | bytes 786440 | tf_op jit(solution)/shard_map/ppermute | solution.py:40
  9.7 34.9 %collective-permute-start.8 = (bf16[2048,256]{1,0:T(8,128)(2,1)}, bf16[2048,256]{1,0:T(8,128)(2,1)}, u32[]{:S(2)}, u32[]{:S(2)}) collective-permute-start(bf16[2048,256]{1,0:T(8,128)(2,1)} %constant_dynamic-slice_fusion.1), channel_id=1, source_target_pairs={{0,1},{2,3},{4,5},{6,7},{8,9},{10,11},{12,13},{14,15},{16,17},{18,... | collective-permute-start | bytes 3145736 | tf_op jit(solution)/shard_map/ppermute | solution.py:71
  11.6 46.8 %collective-permute-start.10 = (bf16[4096,32]{0,1:T(8,128)(2,1)}, bf16[4096,32]{0,1:T(8,128)(2,1)}, u32[]{:S(2)}, u32[]{:S(2)}) collective-permute-start(bf16[4096,32]{0,1:T(8,128)(2,1)} %param.24), channel_id=1, source_target_pairs={{0,1},{2,3},{4,5},{6,7},{8,9},{10,11},{12,13},{14,15},{16,17},{18,... | collective-permute-start | bytes 786440 | tf_op jit(solution)/shard_map/ppermute | solution.py:71
  12.8 26.9 %collective-permute-start.12 = (bf16[256,2048]{1,0:T(8,128)(2,1)}, bf16[256,2048]{1,0:T(8,128)(2,1)}, u32[]{:S(2)}, u32[]{:S(2)}) collective-permute-start(bf16[256,2048]{1,0:T(8,128)(2,1)} %constant_dynamic-slice_fusion), channel_id=1, source_target_pairs={{0,65},{2,67},{4,69},{6,71},{8,73},{10,75},{12,77},{14,79},{16,81}... | collective-permute-start | bytes 3145736 | tf_op jit(solution)/shard_map/ppermute | solution.py:71
  18.6 6.2 %collective-permute-start.3 = (bf16[16,4096]{1,0:T(8,128)(2,1)S(1)}, bf16[16,4096]{1,0:T(8,128)(2,1)S(1)}, u32[]{:S(2)}, u32[]{:S(2)}) collective-permute-start(bf16[16,4096]{1,0:T(8,128)(2,1)S(1)} %slice.85), channel_id=1, source_target_pairs={{0,2},{1,3},{2,4},{3,5},{4,6},{5,7},{6,0},{7,1},{8,10},{9,11},{10,... | collective-permute-start | bytes 393224 | tf_op jit(solution)/shard_map/ppermute | solution.py:40
  20.3 5.1 %collective-permute-start.1 = (bf16[16,4096]{1,0:T(8,128)(2,1)S(1)}, bf16[16,4096]{1,0:T(8,128)(2,1)S(1)}, u32[]{:S(2)}, u32[]{:S(2)}) collective-permute-start(bf16[16,4096]{1,0:T(8,128)(2,1)S(1)} %slice.84), channel_id=1, source_target_pairs={{0,6},{1,7},{2,0},{3,1},{4,2},{5,3},{6,4},{7,5},{8,14},{9,15},{10,... | collective-permute-start | bytes 393224 | tf_op jit(solution)/shard_map/ppermute | solution.py:40
  25.4 23.1 %copy-start.5 = (bf16[4,32,4096]{2,1,0:T(8,128)(2,1)}, bf16[4,32,4096]{2,1,0:T(8,128)(2,1)S(1)}, u32[]{:S(2)}) copy-start(bf16[4,32,4096]{2,1,0:T(8,128)(2,1)S(1)} %bitcast_dynamic-update-slice_fusion.refs_0_) | copy-start | bytes 3145732
  25.5 23.1 %collective-permute-start.4 = (bf16[4,32,4096]{2,1,0:T(8,128)(2,1)S(1)}, bf16[4,32,4096]{2,1,0:T(8,128)(2,1)}, u32[]{:S(2)}, u32[]{:S(2)}) collective-permute-start(bf16[4,32,4096]{2,1,0:T(8,128)(2,1)S(1)} %bitcast_dynamic-update-slice_fusion.refs_0_), channel_id=1, source_target_pairs={{0,24},{1,25},{2,26},{3,27},{4,28},{5,29},{6,30},{7,31},{8,0},{9,1... | collective-permute-start | bytes 3145736 | tf_op jit(solution)/shard_map/ppermute | solution.py:40
  28.5 25.0 %collective-permute-start.6 = (bf16[4,32,4096]{2,1,0:T(8,128)(2,1)S(1)}, bf16[4,32,4096]{2,1,0:T(8,128)(2,1)}, u32[]{:S(2)}, u32[]{:S(2)}) collective-permute-start(bf16[4,32,4096]{2,1,0:T(8,128)(2,1)S(1)} %bitcast_dynamic-update-slice_fusion.refs_0_), channel_id=1, source_target_pairs={{0,8},{1,9},{2,10},{3,11},{4,12},{5,13},{6,14},{7,15},{8,16},{9,17... | collective-permute-start | bytes 3145736 | tf_op jit(solution)/shard_map/ppermute | solution.py:40
  29.1 50.2 %all-to-all-start = ((f32[4,2,32]{2,1,0:T(2,128)}), f32[4,2,32]{2,1,0:T(2,128)S(1)}, u32[]{:S(2)}, u32[]{:S(2)}) async-start(f32[4,2,32]{2,1,0:T(2,128)} %broadcast_in_dim.69), calls=%async_computation | async-start | bytes 8192 | tf_op jit(solution)/shard_map/all_to_all | solution.py:501
  41.6 44.8 %copy-start.2 = (bf16[512,2048]{1,0:T(8,128)(2,1)}, bf16[512,2048]{1,0:T(8,128)(2,1)S(1)}, u32[]{:S(2)}) copy-start(bf16[512,2048]{1,0:T(8,128)(2,1)S(1)} %pad_maximum_fusion.1.refs_0_) | copy-start | bytes 6291460
  41.6 53.0 %collective-permute-start.13 = (bf16[512,2048]{1,0:T(8,128)(2,1)S(1)}, bf16[512,2048]{1,0:T(8,128)(2,1)}, u32[]{:S(2)}, u32[]{:S(2)}) collective-permute-start(bf16[512,2048]{1,0:T(8,128)(2,1)S(1)} %pad_maximum_fusion.1.refs_0_), channel_id=1, source_target_pairs={{0,6},{1,7},{2,4},{3,5},{4,2},{5,3},{6,0},{7,1},{8,14},{9,15},{10,... | collective-permute-start | bytes 6291464 | tf_op jit(solution)/shard_map/ppermute | solution.py:50
  44.6 16.6 %collective-permute-start.9 = (bf16[2048,256]{1,0:T(8,128)(2,1)}, bf16[2048,256]{1,0:T(8,128)(2,1)}, u32[]{:S(2)}, u32[]{:S(2)}) collective-permute-start(bf16[2048,256]{1,0:T(8,128)(2,1)} %collective-permute-done.8), channel_id=1, source_target_pairs={{0,32},{32,0},{64,96},{96,64},{1,33},{33,1},{65,97},{97,65},{2,34}... | collective-permute-start | bytes 3145736 | tf_op jit(solution)/shard_map/ppermute | solution.py:349
  48.6 74.9 %collective-permute-start.16 = (bf16[4096,384]{1,0:T(8,128)(2,1)}, bf16[4096,384]{1,0:T(8,128)(2,1)}, u32[]{:S(2)}, u32[]{:S(2)}) collective-permute-start(bf16[4096,384]{1,0:T(8,128)(2,1)} %broadcast_select_fusion), channel_id=1, source_target_pairs={{0,65},{2,67},{4,69},{6,71},{8,73},{10,75},{12,77},{14,79},{16,81}... | collective-permute-start | bytes 9437192 | tf_op jit(solution)/shard_map/ppermute | solution.py:71
  53.5 15.0 %collective-permute-start.5 = (bf16[2,32,4096]{2,1,0:T(8,128)(2,1)}, bf16[2,32,4096]{2,1,0:T(8,128)(2,1)}, u32[]{:S(2)}, u32[]{:S(2)}) collective-permute-start(bf16[2,32,4096]{2,1,0:T(8,128)(2,1)} %slice.86), channel_id=1, source_target_pairs={{0,24},{1,25},{2,26},{3,27},{4,28},{5,29},{6,30},{7,31},{8,0},{9,1... | collective-permute-start | bytes 1572872 | tf_op jit(solution)/shard_map/ppermute | solution.py:40
  58.4 12.6 %collective-permute-start.7 = (bf16[2,32,4096]{2,1,0:T(8,128)(2,1)}, bf16[2,32,4096]{2,1,0:T(8,128)(2,1)}, u32[]{:S(2)}, u32[]{:S(2)}) collective-permute-start(bf16[2,32,4096]{2,1,0:T(8,128)(2,1)} %slice.87), channel_id=1, source_target_pairs={{0,8},{1,9},{2,10},{3,11},{4,12},{5,13},{6,14},{7,15},{8,16},{9,17... | collective-permute-start | bytes 1572872 | tf_op jit(solution)/shard_map/ppermute | solution.py:40
  61.2 62.3 %collective-permute-start.11 = (bf16[384,4096]{1,0:T(8,128)(2,1)}, bf16[384,4096]{1,0:T(8,128)(2,1)}, u32[]{:S(2)}, u32[]{:S(2)}) collective-permute-start(bf16[384,4096]{1,0:T(8,128)(2,1)} %param.31), channel_id=1, source_target_pairs={{0,1},{2,3},{4,5},{6,7},{8,9},{10,11},{12,13},{14,15},{16,17},{18,... | collective-permute-start | bytes 9437192 | tf_op jit(solution)/shard_map/ppermute | solution.py:71
  79.4 19.4 %all-to-all-start.1 = ((bf16[16,32,576]{2,1,0:T(8,128)(2,1)}), bf16[16,32,576]{2,1,0:T(8,128)(2,1)S(1)}, u32[]{:S(2)}, u32[]{:S(2)}) async-start(bf16[16,32,576]{2,1,0:T(8,128)(2,1)} %bitcast.77), calls=%async_computation.1 | async-start | bytes 1310720 | tf_op jit(solution)/shard_map/all_to_all | solution.py:341
  86.4 37.7 %collective-permute-start.14 = (bf16[512,2048]{1,0:T(8,128)(2,1)S(1)}, bf16[512,2048]{1,0:T(8,128)(2,1)}, u32[]{:S(2)}, u32[]{:S(2)}) collective-permute-start(bf16[512,2048]{1,0:T(8,128)(2,1)S(1)} %pad_maximum_fusion.1.refs_0_), channel_id=1, source_target_pairs={{0,32},{32,0},{64,96},{96,64},{1,33},{33,1},{65,97},{97,65},{2,34}... | collective-permute-start | bytes 6291464 | tf_op jit(solution)/shard_map/ppermute | solution.py:349
  94.6 29.6 %collective-permute-start.15 = (bf16[512,2048]{1,0:T(8,128)(2,1)}, bf16[512,2048]{1,0:T(8,128)(2,1)}, u32[]{:S(2)}, u32[]{:S(2)}) collective-permute-start(bf16[512,2048]{1,0:T(8,128)(2,1)} %collective-permute-done.13.refs_1_), channel_id=1, source_target_pairs={{0,32},{32,0},{64,96},{96,64},{1,33},{33,1},{65,97},{97,65},{2,34}... | collective-permute-start | bytes 6291464 | tf_op jit(solution)/shard_map/ppermute | solution.py:349
  123.5 41.5 %collective-permute-start.17 = (bf16[4096,384]{1,0:T(8,128)(2,1)}, bf16[4096,384]{1,0:T(8,128)(2,1)}, u32[]{:S(2)}, u32[]{:S(2)}) collective-permute-start(bf16[4096,384]{1,0:T(8,128)(2,1)} %collective-permute-done.16), channel_id=1, source_target_pairs={{0,32},{32,0},{64,96},{96,64},{1,33},{33,1},{65,97},{97,65},{2,34}... | collective-permute-start | bytes 9437192 | tf_op jit(solution)/shard_map/ppermute | solution.py:349
  133.3 32.0 %copy-start.7 = (bf16[32,4096]{1,0:T(8,128)(2,1)S(1)}, bf16[32,4096]{1,0:T(8,128)(2,1)}, u32[]{:S(2)}) copy-start(bf16[32,4096]{1,0:T(8,128)(2,1)} %param.16) | copy-start | bytes 786436
  133.4 31.6 %all-to-all-start.3 = ((bf16[8,32,4096]{2,1,0:T(8,128)(2,1)}), bf16[8,32,4096]{2,1,0:T(8,128)(2,1)S(1)}, u32[]{:S(2)}, u32[]{:S(2)}) async-start(bf16[8,32,4096]{2,1,0:T(8,128)(2,1)} %bitcast.76), calls=%async_computation.3 | async-start | bytes 4194304 | tf_op jit(solution)/shard_map/all_to_all | solution.py:341
  137.7 34.6 %copy-start.13 = (s32[32]{0:T(128)}, s32[32]{0:T(128)S(1)}, u32[]{:S(2)}) copy-start(s32[32]{0:T(128)S(1)} %select_reduce_fusion.2.rank_ref) | copy-start | bytes 388
  166.8 11.9 %all-to-all-start.4 = ((f32[4,2,5120]{2,1,0:T(2,128)}), f32[4,2,5120]{2,1,0:T(2,128)S(1)}, u32[]{:S(2)}, u32[]{:S(2)}) async-start(f32[4,2,5120]{2,1,0:T(2,128)} %reshape.232), calls=%async_computation.4 | async-start | bytes 327680 | tf_op jit(solution)/shard_map/all_to_all | solution.py:591
  181.9 17.9 %all-to-all-start.5 = ((bf16[16,4,4096]{2,1,0:T(4,128)(2,1)}), bf16[16,4,4096]{2,1,0:T(4,128)(2,1)S(1)}, u32[]{:S(2)}, u32[]{:S(2)}) async-start(bf16[16,4,4096]{2,1,0:T(4,128)(2,1)} %reshape.227), calls=%async_computation.5 | async-start | bytes 1048576 | tf_op jit(solution)/shard_map/all_to_all | solution.py:341
  193.1 26.2 %collective-permute-start.18 = (bf16[2,128,1024]{2,1,0:T(8,128)(2,1)}, bf16[2,128,1024]{2,1,0:T(8,128)(2,1)}, u32[]{:S(2)}, u32[]{:S(2)}) collective-permute-start(bf16[2,128,1024]{2,1,0:T(8,128)(2,1)} %get-tuple-element.41), channel_id=1, source_target_pairs={{0,32},{32,64},{64,96},{96,0},{1,33},{33,65},{65,97},{97,1},{2,34}... | collective-permute-start | bytes 1572872 | tf_op jit(solution)/shard_map/ppermute | solution.py:603
  193.1 26.2 %collective-permute-start.19 = (bf16[2,128,1024]{2,1,0:T(8,128)(2,1)}, bf16[2,128,1024]{2,1,0:T(8,128)(2,1)}, u32[]{:S(2)}, u32[]{:S(2)}) collective-permute-start(bf16[2,128,1024]{2,1,0:T(8,128)(2,1)} %get-tuple-element.42), channel_id=1, source_target_pairs={{0,64},{32,96},{64,0},{96,32},{1,65},{33,97},{65,1},{97,33},{2,66}... | collective-permute-start | bytes 1572872 | tf_op jit(solution)/shard_map/ppermute | solution.py:603
  193.5 25.8 %collective-permute-start.20 = (bf16[2,128,1024]{2,1,0:T(8,128)(2,1)}, bf16[2,128,1024]{2,1,0:T(8,128)(2,1)}, u32[]{:S(2)}, u32[]{:S(2)}) collective-permute-start(bf16[2,128,1024]{2,1,0:T(8,128)(2,1)} %get-tuple-element.43), channel_id=1, source_target_pairs={{0,96},{32,0},{64,32},{96,64},{1,97},{33,1},{65,33},{97,65},{2,98}... | collective-permute-start | bytes 1572872 | tf_op jit(solution)/shard_map/ppermute | solution.py:603
  214.7 15.5 %all-to-all-start.6 = ((bf16[16,4,4096]{2,1,0:T(4,128)(2,1)}), bf16[16,4,4096]{2,1,0:T(4,128)(2,1)S(1)}, u32[]{:S(2)}, u32[]{:S(2)}) async-start(bf16[16,4,4096]{2,1,0:T(4,128)(2,1)} %reshape.229), calls=%async_computation.6 | async-start | bytes 1048576 | tf_op jit(solution)/shard_map/all_to_all | solution.py:341
  (13 other events, 127.6 us)

commit v5 on v4

--- a/solution.py
+++ b/solution.py
@@ -180,7 +180,7 @@
     length_cap, entry_width = cache_kv.shape[1:]
     kv_count = entry_width // (2 * HD)
     heads = peers * q_width // HD
-    rows_step = 8
+    rows_step = 16
     half = HD // 2
     frequency = ROPE_BASE ** (-2.0 * jnp.arange(half, dtype=F32) / HD)
     angles = lengths.astype(F32)[:, None] * frequency[None, :]

time: 235 us -> 234 us (level)
  no operation moved by 1% of the time
where the time goes in v5:
time: 234 us; the launch traced here: 233 us
  waiting for transfers between devices  61.6 us (26%)
  starting transfers between devices  57.9 us (25%)
  Pallas kernels  39.6 us (17%)
  other arithmetic  22.9 us (10%)
  local copies, waits for them, and re-layouts  21.8 us (9%)
  matrix products  16 us (7%)
  blocking collectives  11.8 us (5%)
    all_to_all x4, waiting for transfers between devices, exchange(): lax.all_to_all(array, 'cuts', 0, 0, tiled=True, axis_index_groups=groups)  36.3 us
    all_to_all x4, starting transfers between devices, exchange(): lax.all_to_all(array, 'cuts', 0, 0, tiled=True, axis_index_groups=groups)  20.9 us
    ppermute x8, starting transfers between devices, shift(): return lax.ppermute(array, 'cuts', moves)  12.3 us
    all_to_all x1, blocking collectives, exchange(): lax.all_to_all(array, 'cuts', 0, 0, tiled=True, axis_index_groups=groups)  11.8 us
    pallas_call x1, Pallas kernels, attend(): pl.pallas_call(functools.partial(attend_kernel, rows_step=rows_step, kv_c...  10.4 us
    ppermute x5, starting transfers between devices, from_pair(): return lax.ppermute(array, ('inst', 'cuts'), pair_perm(side))  9.6 us
    pallas_call x1, Pallas kernels, project_out(): pl.pallas_call(functools.partial(out_kernel, spots=spots), grid=(2 * step...  9.17 us
    dot_general x2, matrix products, expert_half(): return jnp.dot(activation, down, preferred_element_type=F32)  8.76 us
  transfers between devices with their start and end apart: 27, of which 10 were waited for; matrix products, arithmetic and copies ran while one was open for 21% of the time, Pallas kernels for 17%

profile of v5, /device:TPU:0, one launch (start us, length us, event | category | flops | bytes accessed | tf_op | source)
XLA Modules:
  0.0 232.8 jit_solution(11083037699201569623)
XLA Ops:
  4.6 2.8 %collective-permute-start = (bf16[32,4096]{1,0:T(8,128)(2,1)}, bf16[32,4096]{1,0:T(8,128)(2,1)}, u32[]{:S(2)}, u32[]{:S(2)}) collective-permute-start(bf16[32,4096]{1,0:T(8,128)(2,1)} %get-tuple-element.51), channel_id=1, source_target_pairs={{0,6},{1,7},{2,0},{3,1},{4,2},{5,3},{6,4},{7,5},{8,14},{9,15},{10,... | collective-permute-start | bytes 786440 | tf_op jit(solution)/shard_map/ppermute | solution.py:40
  12.8 4.0 %collective-permute-start.12 = (bf16[256,2048]{1,0:T(8,128)(2,1)}, bf16[256,2048]{1,0:T(8,128)(2,1)}, u32[]{:S(2)}, u32[]{:S(2)}) collective-permute-start(bf16[256,2048]{1,0:T(8,128)(2,1)} %constant_dynamic-slice_fusion), channel_id=1, source_target_pairs={{0,65},{2,67},{4,69},{6,71},{8,73},{10,75},{12,77},{14,79},{16,81}... | collective-permute-start | bytes 3145736 | tf_op jit(solution)/shard_map/ppermute | solution.py:71
  20.3 2.6 %collective-permute-start.1 = (bf16[16,4096]{1,0:T(8,128)(2,1)S(1)}, bf16[16,4096]{1,0:T(8,128)(2,1)S(1)}, u32[]{:S(2)}, u32[]{:S(2)}) collective-permute-start(bf16[16,4096]{1,0:T(8,128)(2,1)S(1)} %slice.84), channel_id=1, source_target_pairs={{0,6},{1,7},{2,0},{3,1},{4,2},{5,3},{6,4},{7,5},{8,14},{9,15},{10,... | collective-permute-start | bytes 393224 | tf_op jit(solution)/shard_map/ppermute | solution.py:40
  25.5 3.1 %collective-permute-start.4 = (bf16[4,32,4096]{2,1,0:T(8,128)(2,1)S(1)}, bf16[4,32,4096]{2,1,0:T(8,128)(2,1)}, u32[]{:S(2)}, u32[]{:S(2)}) collective-permute-start(bf16[4,32,4096]{2,1,0:T(8,128)(2,1)S(1)} %bitcast_dynamic-update-slice_fusion.refs_0_), channel_id=1, source_target_pairs={{0,24},{1,25},{2,26},{3,27},{4,28},{5,29},{6,30},{7,31},{8,0},{9,1... | collective-permute-start | bytes 3145736 | tf_op jit(solution)/shard_map/ppermute | solution.py:40
  29.1 3.2 %all-to-all-start = ((f32[4,2,32]{2,1,0:T(2,128)}), f32[4,2,32]{2,1,0:T(2,128)S(1)}, u32[]{:S(2)}, u32[]{:S(2)}) async-start(f32[4,2,32]{2,1,0:T(2,128)} %broadcast_in_dim.69), calls=%async_computation | async-start | bytes 8192 | tf_op jit(solution)/shard_map/all_to_all | solution.py:501
  32.4 7.4 %collective-permute-done.12 = bf16[256,2048]{1,0:T(8,128)(2,1)} collective-permute-done((bf16[256,2048]{1,0:T(8,128)(2,1)}, bf16[256,2048]{1,0:T(8,128)(2,1)}, u32[]{:S(2)}, u32[]{:S(2)}) %collective-permute-start.12) | collective-permute-done | bytes 1048608 | tf_op jit(solution)/shard_map/ppermute | solution.py:71
  41.6 3.0 %collective-permute-start.13 = (bf16[512,2048]{1,0:T(8,128)(2,1)S(1)}, bf16[512,2048]{1,0:T(8,128)(2,1)}, u32[]{:S(2)}, u32[]{:S(2)}) collective-permute-start(bf16[512,2048]{1,0:T(8,128)(2,1)S(1)} %pad_maximum_fusion.1.refs_0_), channel_id=1, source_target_pairs={{0,6},{1,7},{2,4},{3,5},{4,2},{5,3},{6,0},{7,1},{8,14},{9,15},{10,... | collective-permute-start | bytes 6291464 | tf_op jit(solution)/shard_map/ppermute | solution.py:50
  44.6 4.0 %broadcast_select_fusion = bf16[4096,384]{1,0:T(8,128)(2,1)} fusion(bf16[4096,384]{1,0:T(8,128)(2,1)} %param.29, bf16[4096,384]{1,0:T(8,128)(2,1)} %param.30, pred[]{:T(512)S(6)} %eq.101), kind=kLoop, calls=%fused_computation.10 | loop fusion | flops 1572864 | bytes 9437185 | tf_op jit(solution)/shard_map/jit(_where)/select_n | solution.py:519
  48.6 3.1 %collective-permute-start.16 = (bf16[4096,384]{1,0:T(8,128)(2,1)}, bf16[4096,384]{1,0:T(8,128)(2,1)}, u32[]{:S(2)}, u32[]{:S(2)}) collective-permute-start(bf16[4096,384]{1,0:T(8,128)(2,1)} %broadcast_select_fusion), channel_id=1, source_target_pairs={{0,65},{2,67},{4,69},{6,71},{8,73},{10,75},{12,77},{14,79},{16,81}... | collective-permute-start | bytes 9437192 | tf_op jit(solution)/shard_map/ppermute | solution.py:71
  53.5 3.0 %collective-permute-start.5 = (bf16[2,32,4096]{2,1,0:T(8,128)(2,1)}, bf16[2,32,4096]{2,1,0:T(8,128)(2,1)}, u32[]{:S(2)}, u32[]{:S(2)}) collective-permute-start(bf16[2,32,4096]{2,1,0:T(8,128)(2,1)} %slice.86), channel_id=1, source_target_pairs={{0,24},{1,25},{2,26},{3,27},{4,28},{5,29},{6,30},{7,31},{8,0},{9,1... | collective-permute-start | bytes 1572872 | tf_op jit(solution)/shard_map/ppermute | solution.py:40
  61.7 2.9 %maximum_select_fusion = bf16[4096,256]{1,0:T(8,128)(2,1)S(1)} fusion(bf16[2048,256]{1,0:T(8,128)(2,1)} %collective-permute-done.9, bf16[2048,256]{1,0:T(8,128)(2,1)} %collective-permute-done.8, pred[]{:T(512)S(6)} %eq.101), kind=kLoop, calls=%fused_computation.11 | loop fusion | flops 9437184 | bytes 4194305 | tf_op jit(solution)/shard_map/jit(_where)/select_n | solution.py:523
  64.6 4.0 %pad_maximum_fusion.refs_5_ = bf16[4096,576]{1,0:T(8,128)(2,1)} fusion(bf16[4096,32]{1,0:T(8,128)(2,1)S(1)} %copy.58, bf16[4096,32]{1,0:T(8,128)(2,1)S(1)} %copy-done.6, bf16[4096,256]{1,0:T(8,128)(2,1)S(1)} %maximum_select_fusion, bf16[4096,256]{1,0:T(8,128)(2,1)S(1)} %copy-done.3), kind=kLoop, calls=%fused_computation.3 | loop fusion | flops 18874368 | bytes 9437184 | tf_op jit(solution)/shard_map/concatenate | solution.py:529
  68.5 2.5 %collective-permute-done.7.refs_3_ = bf16[2,32,4096]{2,1,0:T(8,128)(2,1)} collective-permute-done((bf16[2,32,4096]{2,1,0:T(8,128)(2,1)}, bf16[2,32,4096]{2,1,0:T(8,128)(2,1)}, u32[]{:S(2)}, u32[]{:S(2)}) %collective-permute-start.7) | collective-permute-done | bytes 524320 | tf_op jit(solution)/shard_map/ppermute | solution.py:40
  71.0 8.3 %project_rows.1 = bf16[4,128,576]{2,1,0:T(8,128)(2,1)} custom-call(s32[4]{0:T(128)} %and_select_fusion.2.places_ref, bf16[4,32,4096]{2,1,0:T(8,128)(2,1)} %copy-done.5, bf16[4,32,4096]{2,1,0:T(8,128)(2,1)} %collective-permute-done.4.refs_1_, bf16[2,32,4096]{2,1,0:T(8,128)(2,1)} %collective-permute-done.5.refs_2_, ...), custom_call_target="tpu_custom_call" | custom-call | flops 2415919104 | bytes 8912896 | tf_op jit(solution)/shard_map/project_rows/pallas_call | solution.py:382
  79.4 6.5 %all-to-all-start.1 = ((bf16[16,32,576]{2,1,0:T(8,128)(2,1)}), bf16[16,32,576]{2,1,0:T(8,128)(2,1)S(1)}, u32[]{:S(2)}, u32[]{:S(2)}) async-start(bf16[16,32,576]{2,1,0:T(8,128)(2,1)} %bitcast.77), calls=%async_computation.1 | async-start | bytes 1310720 | tf_op jit(solution)/shard_map/all_to_all | solution.py:341
  87.2 7.3 %collective-permute-done.13.refs_1_ = bf16[512,2048]{1,0:T(8,128)(2,1)} collective-permute-done((bf16[512,2048]{1,0:T(8,128)(2,1)S(1)}, bf16[512,2048]{1,0:T(8,128)(2,1)}, u32[]{:S(2)}, u32[]{:S(2)}) %collective-permute-start.13) | collective-permute-done | bytes 2097184 | tf_op jit(solution)/shard_map/ppermute | solution.py:50
  94.6 4.1 %all-to-all-done.1.q_ref = bf16[16,32,576]{2,1,0:T(8,128)(2,1)S(1)} async-done(((bf16[16,32,576]{2,1,0:T(8,128)(2,1)}), bf16[16,32,576]{2,1,0:T(8,128)(2,1)S(1)}, u32[]{:S(2)}, u32[]{:S(2)}) %all-to-all-start.1) | async-done | bytes 589856 | tf_op jit(solution)/shard_map/all_to_all | solution.py:341
  99.8 10.4 %attend.1 = (bf16[16,32,512]{2,1,0:T(8,128)(2,1)}, bf16[32,1024]{1,0:T(8,128)(2,1)}) custom-call(s32[32]{0:T(128)} %get-tuple-element.73.lens_ref, bf16[16,32,576]{2,1,0:T(8,128)(2,1)} %copy-done.4, bf16[32,1024]{1,0:T(8,128)(2,1)} %reshape.223.kv_ref, f32[32,128]{1,0:T(8,128)} %get-tuple-element.74.gcos_ref, f32[32,128]{1,0:T(8,128)} %get-tuple-element.61.gsin_ref, ...), custom_call_target="tpu_custom_call" | custom-call | flops 134217728 | bytes 9568256 | tf_op jit(solution)/shard_map/attend/pallas_call | solution.py:196
  111.4 11.8 %all_to_all.35.heads_ref = bf16[8,2,32,512]{3,2,1,0:T(8,128)(2,1)} all-to-all(bf16[8,2,32,512]{3,2,1,0:T(8,128)(2,1)S(1)} %pad_maximum_fusion.3), channel_id=1, replica_groups={{0,2,8,10,16,18,24,26},{1,3,9,11,17,19,25,27},{4,6,12,14,20,22,28,30},{..., dimensions={0} | all-to-all | bytes 1048576 | tf_op jit(solution)/shard_map/all_to_all | solution.py:341
  123.8 9.2 %project_out.1 = bf16[256,4096]{1,0:T(8,128)(2,1)} custom-call(bf16[8,2,32,512]{3,2,1,0:T(8,128)(2,1)} %all_to_all.35.heads_ref, bf16[512,2048]{1,0:T(8,128)(2,1)} %copy-done.2, bf16[512,2048]{1,0:T(8,128)(2,1)} %collective-permute-done.13.refs_1_, bf16[512,2048]{1,0:T(8,128)(2,1)} %collective-permute-done.14.refs_2_, ...), custom_call_target="tpu_custom_call" | custom-call | flops 2147483648 | bytes 8388608 | tf_op jit(solution)/shard_map/project_out/pallas_call | solution.py:441
  133.0 3.7 %all-to-all-start.3 = ((bf16[8,32,4096]{2,1,0:T(8,128)(2,1)}), bf16[8,32,4096]{2,1,0:T(8,128)(2,1)S(1)}, u32[]{:S(2)}, u32[]{:S(2)}) async-start(bf16[8,32,4096]{2,1,0:T(8,128)(2,1)} %bitcast.76), calls=%async_computation.3 | async-start | bytes 4194304 | tf_op jit(solution)/shard_map/all_to_all | solution.py:341
  138.1 26.5 %all-to-all-done.3 = bf16[8,32,4096]{2,1,0:T(8,128)(2,1)S(1)} async-done(((bf16[8,32,4096]{2,1,0:T(8,128)(2,1)}), bf16[8,32,4096]{2,1,0:T(8,128)(2,1)S(1)}, u32[]{:S(2)}, u32[]{:S(2)}) %all-to-all-start.3) | async-done | bytes 2097184 | tf_op jit(solution)/shard_map/all_to_all | solution.py:341
  166.5 5.4 %all-to-all-start.4 = ((f32[4,2,5120]{2,1,0:T(2,128)}), f32[4,2,5120]{2,1,0:T(2,128)S(1)}, u32[]{:S(2)}, u32[]{:S(2)}) async-start(f32[4,2,5120]{2,1,0:T(2,128)} %reshape.232), calls=%async_computation.4 | async-start | bytes 327680 | tf_op jit(solution)/shard_map/all_to_all | solution.py:591
  171.9 6.5 %all-to-all-done.4 = f32[4,2,5120]{2,1,0:T(2,128)S(1)} async-done(((f32[4,2,5120]{2,1,0:T(2,128)}), f32[4,2,5120]{2,1,0:T(2,128)S(1)}, u32[]{:S(2)}, u32[]{:S(2)}) %all-to-all-start.4) | async-done | bytes 163872 | tf_op jit(solution)/shard_map/all_to_all | solution.py:591
  181.6 6.8 %all-to-all-start.5 = ((bf16[16,4,4096]{2,1,0:T(4,128)(2,1)}), bf16[16,4,4096]{2,1,0:T(4,128)(2,1)S(1)}, u32[]{:S(2)}, u32[]{:S(2)}) async-start(bf16[16,4,4096]{2,1,0:T(4,128)(2,1)} %reshape.227), calls=%async_computation.5 | async-start | bytes 1048576 | tf_op jit(solution)/shard_map/all_to_all | solution.py:341
  189.7 3.1 %pick_caches.1 = (bf16[2,128,1024]{2,1,0:T(8,128)(2,1)}, bf16[2,128,1024]{2,1,0:T(8,128)(2,1)}, bf16[2,128,1024]{2,1,0:T(8,128)(2,1)}) custom-call(s32[3,2]{1,0:T(4,128)} %gather_fusion.2, bf16[32,128,1024]{2,1,0:T(8,128)(2,1)} %cache_ref.3, bf16[32,128,1024]{2,1,0:T(8,128)(2,1)} %cache_ref.3, bf16[32,128,1024]{2,1,0:T(8,128)(2,1)} %cache_ref.3), custom_call_target="tpu_custom_call" | custom-call | bytes 3145728 | tf_op jit(solution)/shard_map/pick_caches/pallas_call | solution.py:316
  193.2 2.9 %collective-permute-start.20 = (bf16[2,128,1024]{2,1,0:T(8,128)(2,1)}, bf16[2,128,1024]{2,1,0:T(8,128)(2,1)}, u32[]{:S(2)}, u32[]{:S(2)}) collective-permute-start(bf16[2,128,1024]{2,1,0:T(8,128)(2,1)} %get-tuple-element.43), channel_id=1, source_target_pairs={{0,96},{32,0},{64,32},{96,64},{1,97},{33,1},{65,33},{97,65},{2,98}... | collective-permute-start | bytes 1572872 | tf_op jit(solution)/shard_map/ppermute | solution.py:603
  196.1 3.4 %all-to-all-done.5 = bf16[16,4,4096]{2,1,0:T(4,128)(2,1)S(1)} async-done(((bf16[16,4,4096]{2,1,0:T(4,128)(2,1)}), bf16[16,4,4096]{2,1,0:T(4,128)(2,1)S(1)}, u32[]{:S(2)}, u32[]{:S(2)}) %all-to-all-start.5) | async-done | bytes 524320 | tf_op jit(solution)/shard_map/all_to_all | solution.py:341
  204.6 4.4 %fusion.16 = f32[64,4096]{1,0:T(8,128)S(1)} fusion(bf16[384,4096]{1,0:T(8,128)(2,1)} %collective-permute-done.11, f32[64,384]{1,0:T(8,128)S(1)} %fusion.51, pred[]{:T(512)S(6)} %eq.101, bf16[64,4096]{1,0:T(8,128)(2,1)S(1)} %reshape.228, bf16[4096,384]{1,0:T(8,128)(2,1)} %collective-permute-done.17), kind=kOutput, calls=%fused_computation.54 | convolution fusion | flops 402849792 | bytes 7962625 | tf_op jit(solution)/shard_map/dot_general | solution.py:633
  209.0 4.4 %fusion = bf16[64,4096]{1,0:T(8,128)(2,1)S(1)} fusion(f32[64,4096]{1,0:T(8,128)S(1)} %fusion.16, bf16[384,4096]{1,0:T(8,128)(2,1)} %param.31, bf16[64,4096]{1,0:T(8,128)(2,1)S(1)} %reshape.228, bf16[4096,384]{1,0:T(8,128)(2,1)} %param.30, f32[64,384]{1,0:T(8,128)S(1)} %fusion.50), kind=kOutput, calls=%fused_computation.5 | convolution fusion | flops 403324928 | bytes 8486912 | tf_op jit(solution)/shard_map/dot_general | solution.py:633
  214.4 3.8 %all-to-all-start.6 = ((bf16[16,4,4096]{2,1,0:T(4,128)(2,1)}), bf16[16,4,4096]{2,1,0:T(4,128)(2,1)S(1)}, u32[]{:S(2)}, u32[]{:S(2)}) async-start(bf16[16,4,4096]{2,1,0:T(4,128)(2,1)} %reshape.229), calls=%async_computation.6 | async-start | bytes 1048576 | tf_op jit(solution)/shard_map/all_to_all | solution.py:341
  219.0 8.6 %place_cache.1 = bf16[32,128,1024]{2,1,0:T(8,128)(2,1)} custom-call(s32[32]{0:T(128)} %lens_ref.1, s32[32]{0:T(128)} %get-tuple-element.46.distance_ref, s32[32]{0:T(128)} %copy-done.13, bf16[32,1,1024]{2,1,0:T(2,128)(2,1)} %copy.64.entry_ref, bf16[32,128,1024]{2,1,0:T(8,128)(2,1)} %cache_ref.3, bf16[2,128,1024]{2,1,0:T(8,128)(2,1)} %collective-permute-done.18.refs_0_, ...), custom_call_target="tpu_custom_call" | custom-call | bytes 16777216 | tf_op jit(solution)/shard_map/place_cache/pallas_call | solution.py:282
  (162 shorter events, 48.8 us)
Async XLA Ops:
  1.5 16.1 %copy-start.17 = (s32[32]{0:T(128)S(1)}, s32[32]{0:T(128)}, u32[]{:S(2)}) copy-start(s32[32]{0:T(128)} %param.19) | copy-start | bytes 388
  4.6 14.8 %collective-permute-start = (bf16[32,4096]{1,0:T(8,128)(2,1)}, bf16[32,4096]{1,0:T(8,128)(2,1)}, u32[]{:S(2)}, u32[]{:S(2)}) collective-permute-start(bf16[32,4096]{1,0:T(8,128)(2,1)} %get-tuple-element.51), channel_id=1, source_target_pairs={{0,6},{1,7},{2,0},{3,1},{4,2},{5,3},{6,4},{7,5},{8,14},{9,15},{10,... | collective-permute-start | bytes 786440 | tf_op jit(solution)/shard_map/ppermute | solution.py:40
  7.5 11.1 %collective-permute-start.2 = (bf16[32,4096]{1,0:T(8,128)(2,1)}, bf16[32,4096]{1,0:T(8,128)(2,1)S(1)}, u32[]{:S(2)}, u32[]{:S(2)}) collective-permute-start(bf16[32,4096]{1,0:T(8,128)(2,1)} %get-tuple-element.51), channel_id=1, source_target_pairs={{0,2},{1,3},{2,4},{3,5},{4,6},{5,7},{6,0},{7,1},{8,10},{9,11},{10,... | collective-permute-start | bytes 786440 | tf_op jit(solution)/shard_map/ppermute | solution.py:40
  9.7 34.9 %collective-permute-start.8 = (bf16[2048,256]{1,0:T(8,128)(2,1)}, bf16[2048,256]{1,0:T(8,128)(2,1)}, u32[]{:S(2)}, u32[]{:S(2)}) collective-permute-start(bf16[2048,256]{1,0:T(8,128)(2,1)} %constant_dynamic-slice_fusion.1), channel_id=1, source_target_pairs={{0,1},{2,3},{4,5},{6,7},{8,9},{10,11},{12,13},{14,15},{16,17},{18,... | collective-permute-start | bytes 3145736 | tf_op jit(solution)/shard_map/ppermute | solution.py:71
  11.6 46.8 %collective-permute-start.10 = (bf16[4096,32]{0,1:T(8,128)(2,1)}, bf16[4096,32]{0,1:T(8,128)(2,1)}, u32[]{:S(2)}, u32[]{:S(2)}) collective-permute-start(bf16[4096,32]{0,1:T(8,128)(2,1)} %param.24), channel_id=1, source_target_pairs={{0,1},{2,3},{4,5},{6,7},{8,9},{10,11},{12,13},{14,15},{16,17},{18,... | collective-permute-start | bytes 786440 | tf_op jit(solution)/shard_map/ppermute | solution.py:71
  12.8 26.9 %collective-permute-start.12 = (bf16[256,2048]{1,0:T(8,128)(2,1)}, bf16[256,2048]{1,0:T(8,128)(2,1)}, u32[]{:S(2)}, u32[]{:S(2)}) collective-permute-start(bf16[256,2048]{1,0:T(8,128)(2,1)} %constant_dynamic-slice_fusion), channel_id=1, source_target_pairs={{0,65},{2,67},{4,69},{6,71},{8,73},{10,75},{12,77},{14,79},{16,81}... | collective-permute-start | bytes 3145736 | tf_op jit(solution)/shard_map/ppermute | solution.py:71
  18.6 6.2 %collective-permute-start.3 = (bf16[16,4096]{1,0:T(8,128)(2,1)S(1)}, bf16[16,4096]{1,0:T(8,128)(2,1)S(1)}, u32[]{:S(2)}, u32[]{:S(2)}) collective-permute-start(bf16[16,4096]{1,0:T(8,128)(2,1)S(1)} %slice.85), channel_id=1, source_target_pairs={{0,2},{1,3},{2,4},{3,5},{4,6},{5,7},{6,0},{7,1},{8,10},{9,11},{10,... | collective-permute-start | bytes 393224 | tf_op jit(solution)/shard_map/ppermute | solution.py:40
  20.3 5.1 %collective-permute-start.1 = (bf16[16,4096]{1,0:T(8,128)(2,1)S(1)}, bf16[16,4096]{1,0:T(8,128)(2,1)S(1)}, u32[]{:S(2)}, u32[]{:S(2)}) collective-permute-start(bf16[16,4096]{1,0:T(8,128)(2,1)S(1)} %slice.84), channel_id=1, source_target_pairs={{0,6},{1,7},{2,0},{3,1},{4,2},{5,3},{6,4},{7,5},{8,14},{9,15},{10,... | collective-permute-start | bytes 393224 | tf_op jit(solution)/shard_map/ppermute | solution.py:40
  25.4 23.1 %copy-start.5 = (bf16[4,32,4096]{2,1,0:T(8,128)(2,1)}, bf16[4,32,4096]{2,1,0:T(8,128)(2,1)S(1)}, u32[]{:S(2)}) copy-start(bf16[4,32,4096]{2,1,0:T(8,128)(2,1)S(1)} %bitcast_dynamic-update-slice_fusion.refs_0_) | copy-start | bytes 3145732
  25.5 23.1 %collective-permute-start.4 = (bf16[4,32,4096]{2,1,0:T(8,128)(2,1)S(1)}, bf16[4,32,4096]{2,1,0:T(8,128)(2,1)}, u32[]{:S(2)}, u32[]{:S(2)}) collective-permute-start(bf16[4,32,4096]{2,1,0:T(8,128)(2,1)S(1)} %bitcast_dynamic-update-slice_fusion.refs_0_), channel_id=1, source_target_pairs={{0,24},{1,25},{2,26},{3,27},{4,28},{5,29},{6,30},{7,31},{8,0},{9,1... | collective-permute-start | bytes 3145736 | tf_op jit(solution)/shard_map/ppermute | solution.py:40
  28.5 25.0 %collective-permute-start.6 = (bf16[4,32,4096]{2,1,0:T(8,128)(2,1)S(1)}, bf16[4,32,4096]{2,1,0:T(8,128)(2,1)}, u32[]{:S(2)}, u32[]{:S(2)}) collective-permute-start(bf16[4,32,4096]{2,1,0:T(8,128)(2,1)S(1)} %bitcast_dynamic-update-slice_fusion.refs_0_), channel_id=1, source_target_pairs={{0,8},{1,9},{2,10},{3,11},{4,12},{5,13},{6,14},{7,15},{8,16},{9,17... | collective-permute-start | bytes 3145736 | tf_op jit(solution)/shard_map/ppermute | solution.py:40
  29.1 50.2 %all-to-all-start = ((f32[4,2,32]{2,1,0:T(2,128)}), f32[4,2,32]{2,1,0:T(2,128)S(1)}, u32[]{:S(2)}, u32[]{:S(2)}) async-start(f32[4,2,32]{2,1,0:T(2,128)} %broadcast_in_dim.69), calls=%async_computation | async-start | bytes 8192 | tf_op jit(solution)/shard_map/all_to_all | solution.py:501
  41.6 44.8 %copy-start.2 = (bf16[512,2048]{1,0:T(8,128)(2,1)}, bf16[512,2048]{1,0:T(8,128)(2,1)S(1)}, u32[]{:S(2)}) copy-start(bf16[512,2048]{1,0:T(8,128)(2,1)S(1)} %pad_maximum_fusion.1.refs_0_) | copy-start | bytes 6291460
  41.6 53.0 %collective-permute-start.13 = (bf16[512,2048]{1,0:T(8,128)(2,1)S(1)}, bf16[512,2048]{1,0:T(8,128)(2,1)}, u32[]{:S(2)}, u32[]{:S(2)}) collective-permute-start(bf16[512,2048]{1,0:T(8,128)(2,1)S(1)} %pad_maximum_fusion.1.refs_0_), channel_id=1, source_target_pairs={{0,6},{1,7},{2,4},{3,5},{4,2},{5,3},{6,0},{7,1},{8,14},{9,15},{10,... | collective-permute-start | bytes 6291464 | tf_op jit(solution)/shard_map/ppermute | solution.py:50
  44.6 16.6 %collective-permute-start.9 = (bf16[2048,256]{1,0:T(8,128)(2,1)}, bf16[2048,256]{1,0:T(8,128)(2,1)}, u32[]{:S(2)}, u32[]{:S(2)}) collective-permute-start(bf16[2048,256]{1,0:T(8,128)(2,1)} %collective-permute-done.8), channel_id=1, source_target_pairs={{0,32},{32,0},{64,96},{96,64},{1,33},{33,1},{65,97},{97,65},{2,34}... | collective-permute-start | bytes 3145736 | tf_op jit(solution)/shard_map/ppermute | solution.py:349
  48.6 74.6 %collective-permute-start.16 = (bf16[4096,384]{1,0:T(8,128)(2,1)}, bf16[4096,384]{1,0:T(8,128)(2,1)}, u32[]{:S(2)}, u32[]{:S(2)}) collective-permute-start(bf16[4096,384]{1,0:T(8,128)(2,1)} %broadcast_select_fusion), channel_id=1, source_target_pairs={{0,65},{2,67},{4,69},{6,71},{8,73},{10,75},{12,77},{14,79},{16,81}... | collective-permute-start | bytes 9437192 | tf_op jit(solution)/shard_map/ppermute | solution.py:71
  53.5 15.0 %collective-permute-start.5 = (bf16[2,32,4096]{2,1,0:T(8,128)(2,1)}, bf16[2,32,4096]{2,1,0:T(8,128)(2,1)}, u32[]{:S(2)}, u32[]{:S(2)}) collective-permute-start(bf16[2,32,4096]{2,1,0:T(8,128)(2,1)} %slice.86), channel_id=1, source_target_pairs={{0,24},{1,25},{2,26},{3,27},{4,28},{5,29},{6,30},{7,31},{8,0},{9,1... | collective-permute-start | bytes 1572872 | tf_op jit(solution)/shard_map/ppermute | solution.py:40
  58.4 12.6 %collective-permute-start.7 = (bf16[2,32,4096]{2,1,0:T(8,128)(2,1)}, bf16[2,32,4096]{2,1,0:T(8,128)(2,1)}, u32[]{:S(2)}, u32[]{:S(2)}) collective-permute-start(bf16[2,32,4096]{2,1,0:T(8,128)(2,1)} %slice.87), channel_id=1, source_target_pairs={{0,8},{1,9},{2,10},{3,11},{4,12},{5,13},{6,14},{7,15},{8,16},{9,17... | collective-permute-start | bytes 1572872 | tf_op jit(solution)/shard_map/ppermute | solution.py:40
  61.2 62.0 %collective-permute-start.11 = (bf16[384,4096]{1,0:T(8,128)(2,1)}, bf16[384,4096]{1,0:T(8,128)(2,1)}, u32[]{:S(2)}, u32[]{:S(2)}) collective-permute-start(bf16[384,4096]{1,0:T(8,128)(2,1)} %param.31), channel_id=1, source_target_pairs={{0,1},{2,3},{4,5},{6,7},{8,9},{10,11},{12,13},{14,15},{16,17},{18,... | collective-permute-start | bytes 9437192 | tf_op jit(solution)/shard_map/ppermute | solution.py:71
  79.4 19.4 %all-to-all-start.1 = ((bf16[16,32,576]{2,1,0:T(8,128)(2,1)}), bf16[16,32,576]{2,1,0:T(8,128)(2,1)S(1)}, u32[]{:S(2)}, u32[]{:S(2)}) async-start(bf16[16,32,576]{2,1,0:T(8,128)(2,1)} %bitcast.77), calls=%async_computation.1 | async-start | bytes 1310720 | tf_op jit(solution)/shard_map/all_to_all | solution.py:341
  86.4 37.4 %collective-permute-start.14 = (bf16[512,2048]{1,0:T(8,128)(2,1)S(1)}, bf16[512,2048]{1,0:T(8,128)(2,1)}, u32[]{:S(2)}, u32[]{:S(2)}) collective-permute-start(bf16[512,2048]{1,0:T(8,128)(2,1)S(1)} %pad_maximum_fusion.1.refs_0_), channel_id=1, source_target_pairs={{0,32},{32,0},{64,96},{96,64},{1,33},{33,1},{65,97},{97,65},{2,34}... | collective-permute-start | bytes 6291464 | tf_op jit(solution)/shard_map/ppermute | solution.py:349
  94.6 29.2 %collective-permute-start.15 = (bf16[512,2048]{1,0:T(8,128)(2,1)}, bf16[512,2048]{1,0:T(8,128)(2,1)}, u32[]{:S(2)}, u32[]{:S(2)}) collective-permute-start(bf16[512,2048]{1,0:T(8,128)(2,1)} %collective-permute-done.13.refs_1_), channel_id=1, source_target_pairs={{0,32},{32,0},{64,96},{96,64},{1,33},{33,1},{65,97},{97,65},{2,34}... | collective-permute-start | bytes 6291464 | tf_op jit(solution)/shard_map/ppermute | solution.py:349
  123.2 41.5 %collective-permute-start.17 = (bf16[4096,384]{1,0:T(8,128)(2,1)}, bf16[4096,384]{1,0:T(8,128)(2,1)}, u32[]{:S(2)}, u32[]{:S(2)}) collective-permute-start(bf16[4096,384]{1,0:T(8,128)(2,1)} %collective-permute-done.16), channel_id=1, source_target_pairs={{0,32},{32,0},{64,96},{96,64},{1,33},{33,1},{65,97},{97,65},{2,34}... | collective-permute-start | bytes 9437192 | tf_op jit(solution)/shard_map/ppermute | solution.py:349
  133.0 32.0 %copy-start.7 = (bf16[32,4096]{1,0:T(8,128)(2,1)S(1)}, bf16[32,4096]{1,0:T(8,128)(2,1)}, u32[]{:S(2)}) copy-start(bf16[32,4096]{1,0:T(8,128)(2,1)} %param.16) | copy-start | bytes 786436
  133.0 31.6 %all-to-all-start.3 = ((bf16[8,32,4096]{2,1,0:T(8,128)(2,1)}), bf16[8,32,4096]{2,1,0:T(8,128)(2,1)S(1)}, u32[]{:S(2)}, u32[]{:S(2)}) async-start(bf16[8,32,4096]{2,1,0:T(8,128)(2,1)} %bitcast.76), calls=%async_computation.3 | async-start | bytes 4194304 | tf_op jit(solution)/shard_map/all_to_all | solution.py:341
  137.3 34.6 %copy-start.13 = (s32[32]{0:T(128)}, s32[32]{0:T(128)S(1)}, u32[]{:S(2)}) copy-start(s32[32]{0:T(128)S(1)} %select_reduce_fusion.2.rank_ref) | copy-start | bytes 388
  166.5 11.9 %all-to-all-start.4 = ((f32[4,2,5120]{2,1,0:T(2,128)}), f32[4,2,5120]{2,1,0:T(2,128)S(1)}, u32[]{:S(2)}, u32[]{:S(2)}) async-start(f32[4,2,5120]{2,1,0:T(2,128)} %reshape.232), calls=%async_computation.4 | async-start | bytes 327680 | tf_op jit(solution)/shard_map/all_to_all | solution.py:591
  181.6 17.9 %all-to-all-start.5 = ((bf16[16,4,4096]{2,1,0:T(4,128)(2,1)}), bf16[16,4,4096]{2,1,0:T(4,128)(2,1)S(1)}, u32[]{:S(2)}, u32[]{:S(2)}) async-start(bf16[16,4,4096]{2,1,0:T(4,128)(2,1)} %reshape.227), calls=%async_computation.5 | async-start | bytes 1048576 | tf_op jit(solution)/shard_map/all_to_all | solution.py:341
  192.8 26.2 %collective-permute-start.18 = (bf16[2,128,1024]{2,1,0:T(8,128)(2,1)}, bf16[2,128,1024]{2,1,0:T(8,128)(2,1)}, u32[]{:S(2)}, u32[]{:S(2)}) collective-permute-start(bf16[2,128,1024]{2,1,0:T(8,128)(2,1)} %get-tuple-element.41), channel_id=1, source_target_pairs={{0,32},{32,64},{64,96},{96,0},{1,33},{33,65},{65,97},{97,1},{2,34}... | collective-permute-start | bytes 1572872 | tf_op jit(solution)/shard_map/ppermute | solution.py:603
  192.8 26.2 %collective-permute-start.19 = (bf16[2,128,1024]{2,1,0:T(8,128)(2,1)}, bf16[2,128,1024]{2,1,0:T(8,128)(2,1)}, u32[]{:S(2)}, u32[]{:S(2)}) collective-permute-start(bf16[2,128,1024]{2,1,0:T(8,128)(2,1)} %get-tuple-element.42), channel_id=1, source_target_pairs={{0,64},{32,96},{64,0},{96,32},{1,65},{33,97},{65,1},{97,33},{2,66}... | collective-permute-start | bytes 1572872 | tf_op jit(solution)/shard_map/ppermute | solution.py:603
  193.2 25.8 %collective-permute-start.20 = (bf16[2,128,1024]{2,1,0:T(8,128)(2,1)}, bf16[2,128,1024]{2,1,0:T(8,128)(2,1)}, u32[]{:S(2)}, u32[]{:S(2)}) collective-permute-start(bf16[2,128,1024]{2,1,0:T(8,128)(2,1)} %get-tuple-element.43), channel_id=1, source_target_pairs={{0,96},{32,0},{64,32},{96,64},{1,97},{33,1},{65,33},{97,65},{2,98}... | collective-permute-start | bytes 1572872 | tf_op jit(solution)/shard_map/ppermute | solution.py:603
  214.4 15.5 %all-to-all-start.6 = ((bf16[16,4,4096]{2,1,0:T(4,128)(2,1)}), bf16[16,4,4096]{2,1,0:T(4,128)(2,1)S(1)}, u32[]{:S(2)}, u32[]{:S(2)}) async-start(bf16[16,4,4096]{2,1,0:T(4,128)(2,1)} %reshape.229), calls=%async_computation.6 | async-start | bytes 1048576 | tf_op jit(solution)/shard_map/all_to_all | solution.py:341
  (13 other events, 127.6 us)
